TPU v7x, 128 devices: a whole 4x4x4 slice. The times are simulated.
128 devices in a mesh: frame: 128 (over x, z, y, core).
Axes of the slice: x: 4, y: 4, z: 4, core: 2. Of those that a mesh axis runs over, the one named last changes fastest.
Arguments:
- video: bfloat16 [49152, 1280], P('frame'), may hold values from -6 to 6
- key_list: int32 [8], replicated, may hold values from 0 to 127, as said below
- pairs: int32 [128, 2], P('frame'), may hold values from 0 to 7, all different within a row
- norm_gain: float32 [1280], replicated, as said below
- qkv_weight: bfloat16 [1280, 3840], replicated, may hold values from -0.15625 to 0.15625
- out_weight: bfloat16 [1280, 1280], replicated, may hold values from -0.15625 to 0.15625
- time_gain: float32 [1280], replicated, as said below
- time_weight: bfloat16 [1280, 3840], replicated, may hold values from -0.15625 to 0.15625
Outputs:
- spatial: bfloat16 [49152, 1280], P('frame')
- temporal: bfloat16 [49152, 1280], P('frame')
Inputs may be any that keep to these rules, and one draw needn't show every extreme that they name: `key_list`: distinct frame numbers in rising order, the first 0 and the last 127. `pairs`: each frame names two different keyframes; every keyframe is named by some frame. `norm_gain`: positive. `time_gain`: positive.
All inputs are finite; a program needn't handle non-finite values.
Results may differ from a plain program's by a relative error of at most 0.029.
Values may be sent and summed in bfloat16 or wider, within the bound.
No kernel may reach another device: no remote copies, remote signals or barrier semaphores. Data moves between devices by JAX's collectives and lax.ppermute only.
A program may use at most 192 MiB of HBM per device.

v0:
```python
import jax
import jax.numpy as jnp
from jax import lax
from jax.experimental import pallas as pl
from jax.experimental.pallas import tpu as pltpu
from jax.sharding import PartitionSpec as P

WIDTH = 1280
HEADS = 20
HEAD = 64
TOK = 384
FRAMES = 128
KEYS = 8
PARTS = TOK // FRAMES
LANES = 128
COLS = WIDTH // LANES
SLAB = 32
GROUP = 256
GROUPS = WIDTH // GROUP
SCALE = 0.125 * 1.4426950408889634

bf16 = jnp.bfloat16
f32 = jnp.float32


def params(mib, **more):
    return pltpu.CompilerParams(vmem_limit_bytes=mib << 20, **more)


def cost(flops, moved, exps=0):
    return pl.CostEstimate(flops=int(flops), bytes_accessed=int(moved), transcendentals=int(exps))


def norm_rows(values, gain):
    centred = values - jnp.mean(values, axis=-1, keepdims=True)
    spread = jnp.mean(centred * centred, axis=-1, keepdims=True)
    return (centred * lax.rsqrt(spread + 1e-05) * gain).astype(bf16)


def swap_matrix():
    row = lax.broadcasted_iota(jnp.int32, (256, 256), 0)
    col = lax.broadcasted_iota(jnp.int32, (256, 256), 1)
    return jnp.where(col == (row % 16) * 16 + row // 16, 1.0, 0.0).astype(bf16)


def rows_to_slab(rows_ref, slab_ref, swap, spare=None):
    for half in range(2):
        for pair in range(4):
            sides = []
            for block in (2 * pair, 2 * pair + 1):
                tiles = []
                for unit in range(16 * half, 16 * half + 16):
                    k, g = divmod(unit, COLS)
                    if k < PARTS:
                        at = k * FRAMES + 16 * block
                        tiles.append(rows_ref[at : at + 16, g * LANES : (g + 1) * LANES])
                    elif spare is None:
                        tiles.append(jnp.zeros((16, LANES), bf16))
                    else:
                        tiles.append(spare[unit - PARTS * COLS])
                sides.append(jnp.concatenate(tiles, axis=0))
            both = jnp.concatenate(sides, axis=1)
            moved = jnp.dot(swap, both, preferred_element_type=f32).astype(bf16)
            for side in range(2):
                block = 2 * pair + side
                slab_ref[16 * block : 16 * block + 16, 16 * half : 16 * half + 16, :] = moved[
                    :, side * LANES : (side + 1) * LANES
                ].reshape(16, 16, LANES)


def slab_to_rows(load, rows_ref, swap, first=0):
    for block in range(8):
        both = jnp.concatenate(
            [load(block, half).reshape(256, LANES) for half in range(2)], axis=1
        )
        moved = jnp.dot(swap, both, preferred_element_type=f32).astype(bf16)
        for unit in range(PARTS * COLS):
            half, row = divmod(unit, 16)
            k, g = divmod(unit, COLS)
            at = first + k * FRAMES + 16 * block
            rows_ref[at : at + 16, g * LANES : (g + 1) * LANES] = moved[
                16 * row : 16 * row + 16, half * LANES : (half + 1) * LANES
            ]


def prep_kernel(pairs_ref, video_ref, gain_ref, normed_ref, slab_ref):
    for k in range(PARTS):
        rows = pl.ds(k * FRAMES, FRAMES)
        normed_ref[rows, :] = norm_rows(video_ref[rows, :].astype(f32), gain_ref[...])
    spare = [
        jnp.full((16, LANES), pairs_ref[0, which], jnp.int32).astype(f32).astype(bf16)
        for which in range(2)
    ]
    rows_to_slab(normed_ref, slab_ref, swap_matrix(), spare)


def prep(pairs, video, gain):
    whole = pl.BlockSpec(memory_space=pltpu.VMEM)
    return pl.pallas_call(
        prep_kernel,
        out_shape=(
            jax.ShapeDtypeStruct((TOK, WIDTH), bf16),
            jax.ShapeDtypeStruct((FRAMES, SLAB, LANES), bf16),
        ),
        in_specs=[pl.BlockSpec(memory_space=pltpu.SMEM), whole, whole],
        out_specs=(whole, whole),
        compiler_params=params(16),
        cost_estimate=cost(6 * TOK * WIDTH, 6 * TOK * WIDTH),
        name="prep",
    )(pairs, video, gain)


def project_kernel(rows_ref, weight_ref, out_ref):
    product = jnp.dot(rows_ref[...], weight_ref[...], preferred_element_type=f32)
    product = product * jnp.where(pl.program_id(0) < GROUPS, SCALE, 1.0)
    out_ref[...] = product.astype(bf16)


def project(rows, weight):
    return pl.pallas_call(
        project_kernel,
        grid=(3 * GROUPS,),
        out_shape=jax.ShapeDtypeStruct((TOK, 3 * WIDTH), bf16),
        in_specs=[
            pl.BlockSpec((TOK, WIDTH), lambda i: (0, 0)),
            pl.BlockSpec((WIDTH, GROUP), lambda i: (0, i)),
        ],
        out_specs=pl.BlockSpec((TOK, GROUP), lambda i: (0, i)),
        compiler_params=params(16),
        cost_estimate=cost(6 * TOK * WIDTH * WIDTH, 6 * WIDTH * WIDTH + 8 * TOK * WIDTH),
        name="project",
    )(rows, weight)


def low_lanes(rows):
    return lax.broadcasted_iota(jnp.int32, (rows, LANES), 1) < HEAD


def attend_pair(queries, keys, values, top=None):
    count = queries.shape[0]
    low_q = low_lanes(count)
    low_v = low_lanes(values.shape[0])
    outs, tops = [], []
    for head in range(2):
        keep = low_q if head == 0 else ~low_q
        mine = jnp.where(keep, queries.astype(f32), 0.0).astype(bf16)
        keep_v = low_v if head == 0 else ~low_v
        padded = jnp.where(keep_v, values, 1.0).astype(bf16)
        scores = lax.dot_general(
            mine, keys, (((1,), (1,)), ((), ())), preferred_element_type=f32
        )
        most = jnp.max(scores, axis=-1, keepdims=True)
        if top is not None:
            most = jnp.maximum(most, top[:, head * HEAD : head * HEAD + 1])
        weights = jnp.exp2(scores - most).astype(bf16)
        outs.append(jnp.dot(weights, padded, preferred_element_type=f32))
        tops.append(most)
    mixed = jnp.where(low_q, outs[0], outs[1])
    total = pltpu.roll(jnp.where(low_q, outs[1], outs[0]), HEAD, 1)
    return mixed, total, jnp.where(low_q, tops[0], tops[1])


def own_kernel(q_ref, k_ref, v_ref, mixed_ref, total_ref, top_ref):
    values = v_ref[...].astype(f32)
    for k in range(PARTS):
        rows = pl.ds(k * FRAMES, FRAMES)
        mixed, total, top = attend_pair(q_ref[rows, :], k_ref[...], values)
        mixed_ref[rows, :] = mixed
        total_ref[rows, :] = total
        top_ref[rows, :] = top


def own_attend(qkv):
    out = jax.ShapeDtypeStruct((TOK, WIDTH), f32)
    out_spec = pl.BlockSpec((TOK, LANES), lambda i: (0, i))
    return pl.pallas_call(
        own_kernel,
        grid=(COLS,),
        out_shape=(out, out, out),
        in_specs=[
            pl.BlockSpec((TOK, LANES), lambda i: (0, i)),
            pl.BlockSpec((TOK, LANES), lambda i: (0, COLS + i)),
            pl.BlockSpec((TOK, LANES), lambda i: (0, 2 * COLS + i)),
        ],
        out_specs=(out_spec, out_spec, out_spec),
        compiler_params=params(16),
        cost_estimate=cost(8 * TOK * TOK * WIDTH, 18 * TOK * WIDTH, HEADS * TOK * TOK),
        name="own_attend",
    )(qkv, qkv, qkv)


def choose_kernel(key_list_ref, slab_ref, out_ref):
    keys = jnp.concatenate([slab_ref[key_list_ref[s]] for s in range(KEYS)], axis=0)
    row = lax.broadcasted_iota(jnp.int32, (SLAB, KEYS * SLAB), 0)
    col = lax.broadcasted_iota(jnp.int32, (SLAB, KEYS * SLAB), 1)
    same = (col % SLAB) == row
    slot = (lax.broadcasted_iota(jnp.int32, (1, KEYS * SLAB), 1) // SLAB).astype(f32)

    def some(step, carry):
        first = pl.multiple_of(step * 8, 8)
        picks = []
        for f in range(8):
            spare = slab_ref[first + f, 16:32, :].astype(f32)
            for which in range(2):
                wanted = spare[14 + which : 15 + which, :]
                wanted = jnp.concatenate([wanted, wanted], axis=1)
                pick = jnp.where(same & (slot == wanted), 1.0, 0.0)
                picks.append(pick.astype(bf16))
        chosen = jnp.dot(jnp.concatenate(picks, axis=0), keys, preferred_element_type=f32)
        out_ref[pl.ds(first, 8)] = chosen.astype(bf16).reshape(8, 2, SLAB, LANES)
        return carry

    lax.fori_loop(0, FRAMES // 8, some, 0)


def choose(key_list, slab):
    whole = pl.BlockSpec(memory_space=pltpu.VMEM)
    return pl.pallas_call(
        choose_kernel,
        out_shape=jax.ShapeDtypeStruct((FRAMES, 2, SLAB, LANES), bf16),
        in_specs=[pl.BlockSpec(memory_space=pltpu.SMEM), whole],
        out_specs=whole,
        compiler_params=params(16),
        cost_estimate=cost(4 * FRAMES * SLAB * LANES * 256, 6 * FRAMES * SLAB * LANES),
        name="choose",
    )(key_list, slab)


def attend_kernel(
    slab_ref, q_ref, mixed_ref, total_ref, top_ref, wk_ref, wv_ref, wo_ref, video_ref,
    spatial_ref, out_slab_ref, rows_ref, heads_ref,
):
    step = pl.program_id(0)

    @pl.when(step == 0)
    def _():
        swap = swap_matrix()
        for which in range(2):
            slab_to_rows(
                lambda block, half: slab_ref[
                    16 * block : 16 * block + 16, which, 16 * half : 16 * half + 16, :
                ],
                rows_ref, swap, which * TOK,
            )

    keys = jnp.dot(rows_ref[...], wk_ref[...], preferred_element_type=f32).astype(bf16)
    values = jnp.dot(rows_ref[...], wv_ref[...], preferred_element_type=f32)
    for pair in range(2):
        lanes = slice(pair * LANES, (pair + 1) * LANES)
        for k in range(PARTS):
            rows = pl.ds(k * FRAMES, FRAMES)
            top = top_ref[rows, lanes]
            mixed, total, most = attend_pair(
                q_ref[rows, lanes], keys[:, lanes], values[:, lanes], top
            )
            less = jnp.exp2(top - most)
            mixed = mixed + mixed_ref[rows, lanes] * less
            total = total + total_ref[rows, lanes] * less
            heads_ref[step, rows, lanes] = (mixed / total).astype(bf16)

    @pl.when(step == GROUPS - 1)
    def _():
        for k in range(PARTS):
            rows = pl.ds(k * FRAMES, FRAMES)
            heads = jnp.concatenate([heads_ref[g, rows, :] for g in range(GROUPS)], axis=1)
            added = jnp.dot(heads, wo_ref[...], preferred_element_type=f32)
            spatial_ref[rows, :] = (video_ref[rows, :].astype(f32) + added).astype(bf16)
        rows_to_slab(spatial_ref, out_slab_ref, swap_matrix())


def attend(slab, qkv, mixed, total, top, qkv_weight, out_weight, video):
    once = pl.Buffered(1)
    by_group = pl.BlockSpec((TOK, GROUP), lambda i: (0, i))
    return pl.pallas_call(
        attend_kernel,
        grid=(GROUPS,),
        out_shape=(
            jax.ShapeDtypeStruct((TOK, WIDTH), bf16),
            jax.ShapeDtypeStruct((FRAMES, SLAB, LANES), bf16),
        ),
        in_specs=[
            pl.BlockSpec((FRAMES, 2, SLAB, LANES), lambda i: (0, 0, 0, 0), pipeline_mode=once),
            by_group,
            by_group,
            by_group,
            by_group,
            pl.BlockSpec((WIDTH, GROUP), lambda i: (0, GROUPS + i)),
            pl.BlockSpec((WIDTH, GROUP), lambda i: (0, 2 * GROUPS + i)),
            pl.BlockSpec((WIDTH, WIDTH), lambda i: (0, 0), pipeline_mode=once),
            pl.BlockSpec((TOK, WIDTH), lambda i: (0, 0), pipeline_mode=once),
        ],
        out_specs=(
            pl.BlockSpec((TOK, WIDTH), lambda i: (0, 0)),
            pl.BlockSpec((FRAMES, SLAB, LANES), lambda i: (0, 0, 0)),
        ),
        scratch_shapes=[
            pltpu.VMEM((2 * TOK, WIDTH), bf16),
            pltpu.VMEM((GROUPS, TOK, GROUP), bf16),
        ],
        compiler_params=params(40),
        cost_estimate=cost(
            8 * TOK * WIDTH * WIDTH + 16 * TOK * TOK * WIDTH,
            6 * WIDTH * WIDTH + 20 * TOK * WIDTH,
            2 * HEADS * TOK * TOK,
        ),
        name="attend",
    )(slab, qkv, mixed, total, top, qkv_weight, qkv_weight, out_weight, video)


def time_kernel(
    slab_ref, gain_ref, wq_ref, wk_ref, wv_ref, out_slab_ref, rows_ref, heads_ref, swap_ref
):
    step = pl.program_id(0)

    @pl.when(step == 0)
    def _():
        swap_ref[...] = swap_matrix()
        slab_to_rows(
            lambda block, half: slab_ref[
                16 * block : 16 * block + 16, 16 * half : 16 * half + 16, :
            ],
            rows_ref, swap_ref[...],
        )
        for k in range(PARTS):
            rows = pl.ds(k * FRAMES, FRAMES)
            rows_ref[rows, :] = norm_rows(rows_ref[rows, :].astype(f32), gain_ref[...])

    rows = rows_ref[...]
    queries = (jnp.dot(rows, wq_ref[...], preferred_element_type=f32) * SCALE).astype(bf16)
    keys = jnp.dot(rows, wk_ref[...], preferred_element_type=f32).astype(bf16)
    values = jnp.dot(rows, wv_ref[...], preferred_element_type=f32)
    for pair in range(2):
        lanes = slice(pair * LANES, (pair + 1) * LANES)
        for k in range(PARTS):
            at = slice(k * FRAMES, (k + 1) * FRAMES)
            mixed, total, _ = attend_pair(queries[at, lanes], keys[at, lanes], values[at, lanes])
            heads_ref[2 * step + pair, at, :] = (mixed / total).astype(bf16)

    @pl.when(step == GROUPS - 1)
    def _():
        for k in range(PARTS):
            at = slice(k * FRAMES, (k + 1) * FRAMES)
            for g in range(COLS):
                rows_ref[at, g * LANES : (g + 1) * LANES] = heads_ref[g, at, :]
        rows_to_slab(rows_ref, out_slab_ref, swap_ref[...])


def time_attend(slab, gain, weight):
    once = pl.Buffered(1)
    return pl.pallas_call(
        time_kernel,
        grid=(GROUPS,),
        out_shape=jax.ShapeDtypeStruct((FRAMES, SLAB, LANES), bf16),
        in_specs=[
            pl.BlockSpec((FRAMES, SLAB, LANES), lambda i: (0, 0, 0), pipeline_mode=once),
            pl.BlockSpec((1, WIDTH), lambda i: (0, 0)),
            pl.BlockSpec((WIDTH, GROUP), lambda i: (0, i)),
            pl.BlockSpec((WIDTH, GROUP), lambda i: (0, GROUPS + i)),
            pl.BlockSpec((WIDTH, GROUP), lambda i: (0, 2 * GROUPS + i)),
        ],
        out_specs=pl.BlockSpec((FRAMES, SLAB, LANES), lambda i: (0, 0, 0)),
        scratch_shapes=[
            pltpu.VMEM((TOK, WIDTH), bf16),
            pltpu.VMEM((COLS, TOK, LANES), bf16),
            pltpu.VMEM((256, 256), bf16),
        ],
        compiler_params=params(24),
        cost_estimate=cost(
            6 * TOK * WIDTH * WIDTH + 8 * TOK * FRAMES * WIDTH,
            6 * WIDTH * WIDTH + 4 * TOK * WIDTH,
            HEADS * TOK * FRAMES,
        ),
        name="time_attend",
    )(slab, gain, weight, weight, weight)


def unpack_kernel(slab_ref, out_ref):
    slab_to_rows(
        lambda block, half: slab_ref[16 * block : 16 * block + 16, 16 * half : 16 * half + 16, :],
        out_ref, swap_matrix(),
    )


def unpack(slab):
    whole = pl.BlockSpec(memory_space=pltpu.VMEM)
    return pl.pallas_call(
        unpack_kernel,
        out_shape=jax.ShapeDtypeStruct((TOK, WIDTH), bf16),
        in_specs=[whole],
        out_specs=whole,
        compiler_params=params(16),
        cost_estimate=cost(2 * TOK * WIDTH * 256, 4 * TOK * WIDTH),
        name="unpack",
    )(slab)


def exchange(slab):
    return lax.all_to_all(slab, "frame", split_axis=0, concat_axis=0, tiled=True)


def body(video, key_list, pairs, norm_gain, qkv_weight, out_weight, time_gain, time_weight):
    normed, slab = prep(pairs, video, norm_gain.reshape(1, WIDTH))
    spread = exchange(slab)
    qkv = project(normed, qkv_weight)
    wanted = exchange(choose(key_list, spread))
    mixed, total, top = own_attend(qkv)
    spatial, slab = attend(wanted, qkv, mixed, total, top, qkv_weight, out_weight, video)
    slab = time_attend(exchange(slab), time_gain.reshape(1, WIDTH), time_weight)
    return spatial, unpack(exchange(slab))


def solution(mesh):
    return jax.shard_map(
        body,
        mesh=mesh,
        in_specs=(P("frame", None), P(), P("frame", None), P(), P(), P(), P(), P()),
        out_specs=(P("frame", None), P("frame", None)),
        check_vma=False,
    )
```

profile of v0, /device:TPU:1, one launch (start us, length us, event | category | flops | bytes accessed | tf_op | source)
XLA Modules:
  0.0 203.6 jit_solution(18134172142421532403)
XLA Ops:
  1.3 1.2 copy-done.2
  3.2 1.6 prep.1
  5.8 30.4 %all_to_all.20.slab_ref = bf16[128,32,128]{2,1,0:T(8,128)(2,1)S(1)} all-to-all(bf16[128,32,128]{2,1,0:T(8,128)(2,1)S(1)} %get-tuple-element.9), channel_id=1, replica_groups=mesh['frame'=128] {'frame'}, dimensions={0} | all-to-all | bytes 2097152 | tf_op jit(solution)/shard_map/all_to_all | solution.py:398
  36.2 5.5 %choose.1 = bf16[128,2,32,128]{3,2,1,0:T(8,128)(2,1)} custom-call(s32[8]{0:T(128)S(1)} %copy-done.12, bf16[128,32,128]{2,1,0:T(8,128)(2,1)S(1)} %all_to_all.20.slab_ref), custom_call_target="tpu_custom_call" | custom-call | flops 536870912 | bytes 3145728 | tf_op jit(solution)/shard_map/choose/pallas_call | solution.py:218
  41.6 5.7 %all-to-all-start.1 = ((bf16[128,2,32,128]{3,2,1,0:T(8,128)(2,1)}), bf16[128,2,32,128]{3,2,1,0:T(8,128)(2,1)}, u32[]{:S(2)}, u32[]{:S(2)}) async-start(bf16[128,2,32,128]{3,2,1,0:T(8,128)(2,1)} %choose.1), calls=%async_computation.1 | async-start | bytes 4194304 | tf_op jit(solution)/shard_map/all_to_all | solution.py:398
  47.3 3.8 %copy-done.1 = bf16[1280,3840]{1,0:T(8,128)(2,1)S(1)} copy-done((bf16[1280,3840]{1,0:T(8,128)(2,1)S(1)}, bf16[1280,3840]{1,0:T(8,128)(2,1)}, u32[]{:S(2)}) %copy-start.1) | copy-done | bytes 9830424
  51.1 1.2 copy-done.14
  52.3 7.4 %project.1.q_ref.k_ref.v_ref = bf16[384,3840]{1,0:T(8,128)(2,1)S(1)} custom-call(bf16[384,1280]{1,0:T(8,128)(2,1)S(1)} %copy-done.14, bf16[1280,3840]{1,0:T(8,128)(2,1)S(1)} %copy-done.1), custom_call_target="tpu_custom_call" | custom-call | flops 3774873600 | bytes 13762560 | tf_op jit(solution)/shard_map/project/pallas_call | solution.py:120
  59.7 18.4 %own_attend.1 = (f32[384,1280]{1,0:T(8,128)S(1)}, f32[384,1280]{1,0:T(8,128)S(1)}, f32[384,1280]{1,0:T(8,128)S(1)}) custom-call(bf16[384,3840]{1,0:T(8,128)(2,1)S(1)} %project.1.q_ref.k_ref.v_ref, bf16[384,3840]{1,0:T(8,128)(2,1)S(1)} %project.1.q_ref.k_ref.v_ref, bf16[384,3840]{1,0:T(8,128)(2,1)S(1)} %project.1.q_ref.k_ref.v_ref), custom_call_target="tpu_custom_call" | custom-call | flops 1509949440 | bytes 8847360 | tf_op jit(solution)/shard_map/own_attend/pallas_call | solution.py:176
  78.1 1.3 copy-done.4
  79.4 1.3 copy-done.6
  80.7 1.3 copy-done.8
  82.0 1.2 copy-done.3
  83.2 1.5 copy-done.5
  84.8 1.5 copy-done.7
  86.3 1.5 copy-done.9
  87.9 36.3 %attend.1 = (bf16[384,1280]{1,0:T(8,128)(2,1)}, bf16[128,32,128]{2,1,0:T(8,128)(2,1)S(1)}) custom-call(bf16[128,2,32,128]{3,2,1,0:T(8,128)(2,1)} %all-to-all-done.1.slab_ref, bf16[384,3840]{1,0:T(8,128)(2,1)S(1)} %project.1.q_ref.k_ref.v_ref, f32[384,1280]{1,0:T(8,128)S(1)} %copy-done.5, f32[384,1280]{1,0:T(8,128)S(1)} %copy-done.7, ...), custom_call_target="tpu_custom_call" | custom-call | flops 8053063680 | bytes 19660800 | tf_op jit(solution)/shard_map/attend/pallas_call | solution.py:274
  124.1 1.0 copy-done.10
  125.1 9.9 %all-to-all-start.2 = ((bf16[128,32,128]{2,1,0:T(8,128)(2,1)}), bf16[128,32,128]{2,1,0:T(8,128)(2,1)S(1)}, u32[]{:S(2)}, u32[]{:S(2)}) async-start(bf16[128,32,128]{2,1,0:T(8,128)(2,1)} %copy-done.10), calls=%async_computation.2 | async-start | bytes 2097152 | tf_op jit(solution)/shard_map/all_to_all | solution.py:398
  135.1 19.0 %all-to-all-done.2.slab_ref = bf16[128,32,128]{2,1,0:T(8,128)(2,1)S(1)} async-done(((bf16[128,32,128]{2,1,0:T(8,128)(2,1)}), bf16[128,32,128]{2,1,0:T(8,128)(2,1)S(1)}, u32[]{:S(2)}, u32[]{:S(2)}) %all-to-all-start.2) | async-done | bytes 1048608 | tf_op jit(solution)/shard_map/all_to_all | solution.py:398
  154.1 3.8 %copy-done = bf16[1280,3840]{1,0:T(8,128)(2,1)S(1)} copy-done((bf16[1280,3840]{1,0:T(8,128)(2,1)S(1)}, bf16[1280,3840]{1,0:T(8,128)(2,1)}, u32[]{:S(2)}) %copy-start) | copy-done | bytes 9830424
  157.9 20.7 %time_attend.1 = bf16[128,32,128]{2,1,0:T(8,128)(2,1)S(1)} custom-call(bf16[128,32,128]{2,1,0:T(8,128)(2,1)S(1)} %all-to-all-done.2.slab_ref, f32[1,1280]{1,0:T(1,128)S(1)} %reshape.11.gain_ref, bf16[1280,3840]{1,0:T(8,128)(2,1)S(1)} %copy-done, bf16[1280,3840]{1,0:T(8,128)(2,1)S(1)} %copy-done, bf16[1280,3840]{1,0:T(8,128)(2,1)S(1)} %copy-done), custom_call_target="tpu_custom_call" | custom-call | flops 4278190080 | bytes 11796480 | tf_op jit(solution)/shard_map/time_attend/pallas_call | solution.py:350
  178.6 23.6 %all_to_all.21.slab_ref = bf16[128,32,128]{2,1,0:T(8,128)(2,1)S(1)} all-to-all(bf16[128,32,128]{2,1,0:T(8,128)(2,1)S(1)} %time_attend.1), channel_id=1, replica_groups=mesh['frame'=128] {'frame'}, dimensions={0} | all-to-all | bytes 2097152 | tf_op jit(solution)/shard_map/all_to_all | solution.py:398
  202.2 1.4 unpack.1
  (23 shorter events, 2.3 us)
Async XLA Ops:
  0.6 35.5 %copy-start.12 = (s32[8]{0:T(128)S(1)}, s32[8]{0:T(128)}, u32[]{:S(2)}) copy-start(s32[8]{0:T(128)} %key_list_ref.1) | copy-start | bytes 100
  1.3 1.2 copy-start.2
  2.5 0.7 copy-start.11
  4.8 0.9 copy-start.13
  41.6 40.4 %all-to-all-start.1 = ((bf16[128,2,32,128]{3,2,1,0:T(8,128)(2,1)}), bf16[128,2,32,128]{3,2,1,0:T(8,128)(2,1)}, u32[]{:S(2)}, u32[]{:S(2)}) async-start(bf16[128,2,32,128]{3,2,1,0:T(8,128)(2,1)} %choose.1), calls=%async_computation.1 | async-start | bytes 4194304 | tf_op jit(solution)/shard_map/all_to_all | solution.py:398
  47.3 3.8 %copy-start.1 = (bf16[1280,3840]{1,0:T(8,128)(2,1)S(1)}, bf16[1280,3840]{1,0:T(8,128)(2,1)}, u32[]{:S(2)}) copy-start(bf16[1280,3840]{1,0:T(8,128)(2,1)} %wv_ref.2) | copy-start | bytes 29491204
  51.1 1.2 copy-start.14
  78.1 1.3 copy-start.4
  79.4 1.3 copy-start.6
  80.7 1.3 copy-start.8
  82.0 1.2 copy-start.3
  83.2 1.5 copy-start.5
  84.8 1.5 copy-start.7
  86.3 1.5 copy-start.9
  124.1 1.0 copy-start.10
  125.1 9.9 %copy-start.15 = (f32[1280]{0:T(1024)S(1)}, f32[1280]{0:T(1024)}, u32[]{:S(2)}) copy-start(f32[1280]{0:T(1024)} %param.14) | copy-start | bytes 15364
  125.1 29.0 %all-to-all-start.2 = ((bf16[128,32,128]{2,1,0:T(8,128)(2,1)}), bf16[128,32,128]{2,1,0:T(8,128)(2,1)S(1)}, u32[]{:S(2)}, u32[]{:S(2)}) async-start(bf16[128,32,128]{2,1,0:T(8,128)(2,1)} %copy-done.10), calls=%async_computation.2 | async-start | bytes 2097152 | tf_op jit(solution)/shard_map/all_to_all | solution.py:398
  154.1 3.8 %copy-start = (bf16[1280,3840]{1,0:T(8,128)(2,1)S(1)}, bf16[1280,3840]{1,0:T(8,128)(2,1)}, u32[]{:S(2)}) copy-start(bf16[1280,3840]{1,0:T(8,128)(2,1)} %wv_ref.3) | copy-start | bytes 29491204
where the time goes:
time: 204 us
  Pallas kernels  91.2 us (45%)
  blocking collectives  53.9 us (26%)
  local copies, waits for them, and re-layouts  23.1 us (11%)
  waiting for transfers between devices  19 us (9%)
  starting transfers between devices  15.6 us (8%)
    all_to_all x2, blocking collectives, exchange(): lax.all_to_all(slab, 'frame', split_axis=0, concat_axis=0, tiled=True)  53.9 us
    pallas_call x1, Pallas kernels, attend(): pl.pallas_call(attend_kernel, grid=(GROUPS,), out_shape=(jax.ShapeDtypeSt...  36.3 us
    unnamed x32, local copies, waits for them, and re-layouts  22.4 us
    pallas_call x1, Pallas kernels, time_attend(): pl.pallas_call(time_kernel, grid=(GROUPS,), out_shape=jax.ShapeDtypeStruc...  20.7 us
    all_to_all x2, waiting for transfers between devices, exchange(): lax.all_to_all(slab, 'frame', split_axis=0, concat_axis=0, tiled=True)  19 us
    pallas_call x1, Pallas kernels, own_attend(): pl.pallas_call(own_kernel, grid=(COLS,), out_shape=(out, out, out), in_sp...  18.4 us
    all_to_all x2, starting transfers between devices, exchange(): lax.all_to_all(slab, 'frame', split_axis=0, concat_axis=0, tiled=True)  15.6 us
    pallas_call x1, Pallas kernels, project(): pl.pallas_call(project_kernel, grid=(3 * GROUPS,), out_shape=jax.ShapeDty...  7.36 us
  transfers between devices with their start and end apart: 2, of which 1 were waited for; matrix products, arithmetic and copies ran while one was open for 0% of the time, Pallas kernels for 13%

commit v1 on v0

--- a/solution.py
+++ b/solution.py
@@ -17,6 +17,8 @@
 SLAB = 32
 GROUP = 256
 GROUPS = WIDTH // GROUP
+CHOSEN = 32
+VMEM = 60
 SCALE = 0.125 * 1.4426950408889634
 
 bf16 = jnp.bfloat16
@@ -104,126 +106,140 @@
         ),
         in_specs=[pl.BlockSpec(memory_space=pltpu.SMEM), whole, whole],
         out_specs=(whole, whole),
-        compiler_params=params(16),
+        compiler_params=params(VMEM),
         cost_estimate=cost(6 * TOK * WIDTH, 6 * TOK * WIDTH),
         name="prep",
     )(pairs, video, gain)
 
 
-def project_kernel(rows_ref, weight_ref, out_ref):
-    product = jnp.dot(rows_ref[...], weight_ref[...], preferred_element_type=f32)
-    product = product * jnp.where(pl.program_id(0) < GROUPS, SCALE, 1.0)
-    out_ref[...] = product.astype(bf16)
+def project_kernel(rows_ref, wq_ref, wk_ref, wv_ref, q_ref, k_ref, v_ref):
+    rows = rows_ref[...]
+    queries = jnp.dot(rows, wq_ref[...], preferred_element_type=f32) * SCALE
+    q_ref[...] = queries.astype(bf16)
+    k_ref[...] = jnp.dot(rows, wk_ref[...], preferred_element_type=f32).astype(bf16)
+    v_ref[...] = jnp.dot(rows, wv_ref[...], preferred_element_type=f32).astype(bf16)
 
 
 def project(rows, weight):
+    out = jax.ShapeDtypeStruct((TOK, WIDTH), bf16)
+    out_spec = pl.BlockSpec((TOK, GROUP), lambda i: (0, i))
     return pl.pallas_call(
         project_kernel,
-        grid=(3 * GROUPS,),
-        out_shape=jax.ShapeDtypeStruct((TOK, 3 * WIDTH), bf16),
+        grid=(GROUPS,),
+        out_shape=(out, out, out),
         in_specs=[
             pl.BlockSpec((TOK, WIDTH), lambda i: (0, 0)),
             pl.BlockSpec((WIDTH, GROUP), lambda i: (0, i)),
-        ],
-        out_specs=pl.BlockSpec((TOK, GROUP), lambda i: (0, i)),
-        compiler_params=params(16),
+            pl.BlockSpec((WIDTH, GROUP), lambda i: (0, GROUPS + i)),
+            pl.BlockSpec((WIDTH, GROUP), lambda i: (0, 2 * GROUPS + i)),
+        ],
+        out_specs=(out_spec, out_spec, out_spec),
+        compiler_params=params(VMEM),
         cost_estimate=cost(6 * TOK * WIDTH * WIDTH, 6 * WIDTH * WIDTH + 8 * TOK * WIDTH),
         name="project",
-    )(rows, weight)
+    )(rows, weight, weight, weight)
 
 
 def low_lanes(rows):
     return lax.broadcasted_iota(jnp.int32, (rows, LANES), 1) < HEAD
 
 
-def attend_pair(queries, keys, values, top=None):
-    count = queries.shape[0]
-    low_q = low_lanes(count)
-    low_v = low_lanes(values.shape[0])
-    outs, tops = [], []
-    for head in range(2):
-        keep = low_q if head == 0 else ~low_q
-        mine = jnp.where(keep, queries.astype(f32), 0.0).astype(bf16)
-        keep_v = low_v if head == 0 else ~low_v
-        padded = jnp.where(keep_v, values, 1.0).astype(bf16)
-        scores = lax.dot_general(
-            mine, keys, (((1,), (1,)), ((), ())), preferred_element_type=f32
-        )
-        most = jnp.max(scores, axis=-1, keepdims=True)
+def attend_pairs(units):
+    scores, padded = [], []
+    for queries, keys, values, _ in units:
+        low_q, low_v = low_lanes(queries.shape[0]), low_lanes(values.shape[0])
+        wide = queries.astype(f32)
+        for head in range(2):
+            mine = jnp.where(low_q, wide, 0.0) if head == 0 else jnp.where(low_q, 0.0, wide)
+            rest = jnp.where(low_v, values, 1.0) if head == 0 else jnp.where(low_v, 1.0, values)
+            padded.append(rest.astype(bf16))
+            scores.append(
+                lax.dot_general(
+                    mine.astype(bf16), keys, (((1,), (1,)), ((), ())), preferred_element_type=f32
+                )
+            )
+    tops = [jnp.max(s, axis=-1, keepdims=True) for s in scores]
+    for i, (_, _, _, top) in enumerate(units):
         if top is not None:
-            most = jnp.maximum(most, top[:, head * HEAD : head * HEAD + 1])
-        weights = jnp.exp2(scores - most).astype(bf16)
-        outs.append(jnp.dot(weights, padded, preferred_element_type=f32))
-        tops.append(most)
-    mixed = jnp.where(low_q, outs[0], outs[1])
-    total = pltpu.roll(jnp.where(low_q, outs[1], outs[0]), HEAD, 1)
-    return mixed, total, jnp.where(low_q, tops[0], tops[1])
+            tops[2 * i] = jnp.maximum(tops[2 * i], top[:, 0:1])
+            tops[2 * i + 1] = jnp.maximum(tops[2 * i + 1], top[:, HEAD : HEAD + 1])
+    weights = [jnp.exp2(s - top).astype(bf16) for s, top in zip(scores, tops)]
+    outs = [jnp.dot(w, v, preferred_element_type=f32) for w, v in zip(weights, padded)]
+    given = []
+    for i, (queries, _, _, _) in enumerate(units):
+        low = low_lanes(queries.shape[0])
+        one, two = outs[2 * i], outs[2 * i + 1]
+        total = pltpu.roll(jnp.where(low, two, one), HEAD, 1)
+        given.append((jnp.where(low, one, two), total, jnp.where(low, tops[2 * i], tops[2 * i + 1])))
+    return given
 
 
 def own_kernel(q_ref, k_ref, v_ref, mixed_ref, total_ref, top_ref):
-    values = v_ref[...].astype(f32)
-    for k in range(PARTS):
-        rows = pl.ds(k * FRAMES, FRAMES)
-        mixed, total, top = attend_pair(q_ref[rows, :], k_ref[...], values)
-        mixed_ref[rows, :] = mixed
-        total_ref[rows, :] = total
-        top_ref[rows, :] = top
-
-
-def own_attend(qkv):
+    units = []
+    for pair in range(2):
+        lanes = slice(pair * LANES, (pair + 1) * LANES)
+        units.append((q_ref[:, lanes], k_ref[:, lanes], v_ref[:, lanes].astype(f32), None))
+    for pair, (mixed, total, top) in enumerate(attend_pairs(units)):
+        lanes = slice(pair * LANES, (pair + 1) * LANES)
+        mixed_ref[:, lanes] = mixed
+        total_ref[:, lanes] = total
+        top_ref[:, lanes] = top
+
+
+def own_attend(queries, keys, values):
     out = jax.ShapeDtypeStruct((TOK, WIDTH), f32)
-    out_spec = pl.BlockSpec((TOK, LANES), lambda i: (0, i))
+    out_spec = pl.BlockSpec((TOK, GROUP), lambda i: (0, i))
     return pl.pallas_call(
         own_kernel,
-        grid=(COLS,),
+        grid=(GROUPS,),
         out_shape=(out, out, out),
-        in_specs=[
-            pl.BlockSpec((TOK, LANES), lambda i: (0, i)),
-            pl.BlockSpec((TOK, LANES), lambda i: (0, COLS + i)),
-            pl.BlockSpec((TOK, LANES), lambda i: (0, 2 * COLS + i)),
-        ],
+        in_specs=[out_spec, out_spec, out_spec],
         out_specs=(out_spec, out_spec, out_spec),
-        compiler_params=params(16),
+        compiler_params=params(VMEM),
         cost_estimate=cost(8 * TOK * TOK * WIDTH, 18 * TOK * WIDTH, HEADS * TOK * TOK),
         name="own_attend",
-    )(qkv, qkv, qkv)
-
-
-def choose_kernel(key_list_ref, slab_ref, out_ref):
-    keys = jnp.concatenate([slab_ref[key_list_ref[s]] for s in range(KEYS)], axis=0)
-    row = lax.broadcasted_iota(jnp.int32, (SLAB, KEYS * SLAB), 0)
-    col = lax.broadcasted_iota(jnp.int32, (SLAB, KEYS * SLAB), 1)
-    same = (col % SLAB) == row
-    slot = (lax.broadcasted_iota(jnp.int32, (1, KEYS * SLAB), 1) // SLAB).astype(f32)
-
-    def some(step, carry):
-        first = pl.multiple_of(step * 8, 8)
+    )(queries, keys, values)
+
+
+def choose_kernel(key_list_ref, slab_ref, after_ref, out_ref):
+    del after_ref
+    halves = [
+        jnp.concatenate([slab_ref[key_list_ref[s], at : at + 16, :] for s in range(KEYS)], axis=0)
+        for at in (0, 16)
+    ]
+    keys = jnp.concatenate(halves, axis=1)
+    row = lax.broadcasted_iota(jnp.int32, (16, LANES), 0)
+    col = lax.broadcasted_iota(jnp.int32, (16, LANES), 1)
+    slot = jnp.where(col % 16 == row, col // 16, -1).astype(f32)
+    first = pl.program_id(0) * CHOSEN
+    for f in range(0, CHOSEN, 8):
         picks = []
-        for f in range(8):
-            spare = slab_ref[first + f, 16:32, :].astype(f32)
+        for more in range(8):
+            spare = slab_ref[first + f + more, 16:32, :].astype(f32)
             for which in range(2):
                 wanted = spare[14 + which : 15 + which, :]
-                wanted = jnp.concatenate([wanted, wanted], axis=1)
-                pick = jnp.where(same & (slot == wanted), 1.0, 0.0)
-                picks.append(pick.astype(bf16))
+                picks.append(jnp.where(slot == wanted, 1.0, 0.0).astype(bf16))
         chosen = jnp.dot(jnp.concatenate(picks, axis=0), keys, preferred_element_type=f32)
-        out_ref[pl.ds(first, 8)] = chosen.astype(bf16).reshape(8, 2, SLAB, LANES)
-        return carry
-
-    lax.fori_loop(0, FRAMES // 8, some, 0)
-
-
-def choose(key_list, slab):
-    whole = pl.BlockSpec(memory_space=pltpu.VMEM)
+        chosen = chosen.astype(bf16).reshape(8, 2, 16, 2 * LANES)
+        out_ref[f : f + 8, :, 0:16, :] = chosen[..., :LANES]
+        out_ref[f : f + 8, :, 16:32, :] = chosen[..., LANES:]
+
+
+def choose(key_list, slab, after):
     return pl.pallas_call(
         choose_kernel,
+        grid=(FRAMES // CHOSEN,),
         out_shape=jax.ShapeDtypeStruct((FRAMES, 2, SLAB, LANES), bf16),
-        in_specs=[pl.BlockSpec(memory_space=pltpu.SMEM), whole],
-        out_specs=whole,
-        compiler_params=params(16),
+        in_specs=[
+            pl.BlockSpec(memory_space=pltpu.SMEM),
+            pl.BlockSpec((FRAMES, SLAB, LANES), lambda i: (0, 0, 0)),
+            pl.BlockSpec(memory_space=pl.ANY),
+        ],
+        out_specs=pl.BlockSpec((CHOSEN, 2, SLAB, LANES), lambda i: (i, 0, 0, 0)),
+        compiler_params=params(VMEM),
         cost_estimate=cost(4 * FRAMES * SLAB * LANES * 256, 6 * FRAMES * SLAB * LANES),
         name="choose",
-    )(key_list, slab)
+    )(key_list, slab, after)
 
 
 def attend_kernel(
@@ -245,18 +261,16 @@
 
     keys = jnp.dot(rows_ref[...], wk_ref[...], preferred_element_type=f32).astype(bf16)
     values = jnp.dot(rows_ref[...], wv_ref[...], preferred_element_type=f32)
+    units = []
     for pair in range(2):
         lanes = slice(pair * LANES, (pair + 1) * LANES)
-        for k in range(PARTS):
-            rows = pl.ds(k * FRAMES, FRAMES)
-            top = top_ref[rows, lanes]
-            mixed, total, most = attend_pair(
-                q_ref[rows, lanes], keys[:, lanes], values[:, lanes], top
-            )
-            less = jnp.exp2(top - most)
-            mixed = mixed + mixed_ref[rows, lanes] * less
-            total = total + total_ref[rows, lanes] * less
-            heads_ref[step, rows, lanes] = (mixed / total).astype(bf16)
+        units.append((q_ref[:, lanes], keys[:, lanes], values[:, lanes], top_ref[:, lanes]))
+    for pair, (mixed, total, most) in enumerate(attend_pairs(units)):
+        lanes = slice(pair * LANES, (pair + 1) * LANES)
+        less = jnp.exp2(top_ref[:, lanes] - most)
+        mixed = mixed + mixed_ref[:, lanes] * less
+        total = total + total_ref[:, lanes] * less
+        heads_ref[step, :, lanes] = (mixed / total).astype(bf16)
 
     @pl.when(step == GROUPS - 1)
     def _():
@@ -268,7 +282,7 @@
         rows_to_slab(spatial_ref, out_slab_ref, swap_matrix())
 
 
-def attend(slab, qkv, mixed, total, top, qkv_weight, out_weight, video):
+def attend(slab, queries, mixed, total, top, qkv_weight, out_weight, video):
     once = pl.Buffered(1)
     by_group = pl.BlockSpec((TOK, GROUP), lambda i: (0, i))
     return pl.pallas_call(
@@ -297,14 +311,14 @@
             pltpu.VMEM((2 * TOK, WIDTH), bf16),
             pltpu.VMEM((GROUPS, TOK, GROUP), bf16),
         ],
-        compiler_params=params(40),
+        compiler_params=params(VMEM),
         cost_estimate=cost(
             8 * TOK * WIDTH * WIDTH + 16 * TOK * TOK * WIDTH,
             6 * WIDTH * WIDTH + 20 * TOK * WIDTH,
             2 * HEADS * TOK * TOK,
         ),
         name="attend",
-    )(slab, qkv, mixed, total, top, qkv_weight, qkv_weight, out_weight, video)
+    )(slab, queries, mixed, total, top, qkv_weight, qkv_weight, out_weight, video)
 
 
 def time_kernel(
@@ -329,12 +343,15 @@
     queries = (jnp.dot(rows, wq_ref[...], preferred_element_type=f32) * SCALE).astype(bf16)
     keys = jnp.dot(rows, wk_ref[...], preferred_element_type=f32).astype(bf16)
     values = jnp.dot(rows, wv_ref[...], preferred_element_type=f32)
+    units, places = [], []
     for pair in range(2):
         lanes = slice(pair * LANES, (pair + 1) * LANES)
         for k in range(PARTS):
             at = slice(k * FRAMES, (k + 1) * FRAMES)
-            mixed, total, _ = attend_pair(queries[at, lanes], keys[at, lanes], values[at, lanes])
-            heads_ref[2 * step + pair, at, :] = (mixed / total).astype(bf16)
+            units.append((queries[at, lanes], keys[at, lanes], values[at, lanes], None))
+            places.append((pair, at))
+    for (pair, at), (mixed, total, _) in zip(places, attend_pairs(units)):
+        heads_ref[2 * step + pair, at, :] = (mixed / total).astype(bf16)
 
     @pl.when(step == GROUPS - 1)
     def _():
@@ -364,7 +381,7 @@
             pltpu.VMEM((COLS, TOK, LANES), bf16),
             pltpu.VMEM((256, 256), bf16),
         ],
-        compiler_params=params(24),
+        compiler_params=params(VMEM),
         cost_estimate=cost(
             6 * TOK * WIDTH * WIDTH + 8 * TOK * FRAMES * WIDTH,
             6 * WIDTH * WIDTH + 4 * TOK * WIDTH,
@@ -388,7 +405,7 @@
         out_shape=jax.ShapeDtypeStruct((TOK, WIDTH), bf16),
         in_specs=[whole],
         out_specs=whole,
-        compiler_params=params(16),
+        compiler_params=params(VMEM),
         cost_estimate=cost(2 * TOK * WIDTH * 256, 4 * TOK * WIDTH),
         name="unpack",
     )(slab)
@@ -401,10 +418,10 @@
 def body(video, key_list, pairs, norm_gain, qkv_weight, out_weight, time_gain, time_weight):
     normed, slab = prep(pairs, video, norm_gain.reshape(1, WIDTH))
     spread = exchange(slab)
-    qkv = project(normed, qkv_weight)
-    wanted = exchange(choose(key_list, spread))
-    mixed, total, top = own_attend(qkv)
-    spatial, slab = attend(wanted, qkv, mixed, total, top, qkv_weight, out_weight, video)
+    queries, keys, values = project(normed, qkv_weight)
+    wanted = exchange(choose(key_list, spread, queries))
+    mixed, total, top = own_attend(queries, keys, values)
+    spatial, slab = attend(wanted, queries, mixed, total, top, qkv_weight, out_weight, video)
     slab = time_attend(exchange(slab), time_gain.reshape(1, WIDTH), time_weight)
     return spatial, unpack(exchange(slab))
 

time: 204 us -> 166 us (0.81)
  waiting for transfers between devices: 19 us -> 50.9 us
  blocking collectives: 53.9 us -> 24.7 us
  Pallas kernels: 91.2 us -> 63 us
  local copies, waits for them, and re-layouts: 23.1 us -> 5.19 us
  starting transfers between devices: 15.6 us -> 20.9 us
    all_to_all x2 -> x3, waiting for transfers between devices: 19 us -> 50.9 us  [exchange(): lax.all_to_all(slab, 'frame', split_axis=0, concat_axis=0, tiled=True)]
    all_to_all x2 -> x1, blocking collectives: 53.9 us -> 24.7 us  [exchange(): lax.all_to_all(slab, 'frame', split_axis=0, concat_axis=0, tiled=True)]
    unnamed x32 -> x8, local copies, waits for them, and re-layouts: 22.4 us -> 3.3 us
    pallas_call x1, Pallas kernels: 36.3 us -> 23.7 us  [attend(): pl.pallas_call(attend_kernel, grid=(GROUPS,), out_shape=(jax.ShapeDtypeSt...]
    pallas_call x3, Pallas kernels: 31.2 us -> 20.9 us  [the longest x1 9.16 us: project(): pl.pallas_call(project_kernel, grid=(GROUPS,), out_shape=(out, out, out),...]
    pallas_call x1, Pallas kernels: 20.7 us -> 12.4 us  [time_attend(): pl.pallas_call(time_kernel, grid=(GROUPS,), out_shape=jax.ShapeDtypeStruc...]
    all_to_all x2 -> x3, starting transfers between devices: 15.6 us -> 20.9 us  [exchange(): lax.all_to_all(slab, 'frame', split_axis=0, concat_axis=0, tiled=True)]
  transfers between devices with their start and end apart: 2 -> 3, of which waited for: 1 -> 3; matrix products, arithmetic and copies ran while one was open for 0% -> 0% of each run, Pallas kernels for 13% -> 10%
where the time goes in v1:
time: 166 us; the launch traced here: 165 us
  Pallas kernels  63 us (38%)
  waiting for transfers between devices  50.9 us (31%)
  blocking collectives  24.7 us (15%)
  starting transfers between devices  20.9 us (13%)
  local copies, waits for them, and re-layouts  5.19 us (3%)
    all_to_all x3, waiting for transfers between devices, exchange(): lax.all_to_all(slab, 'frame', split_axis=0, concat_axis=0, tiled=True)  50.9 us
    all_to_all x1, blocking collectives, exchange(): lax.all_to_all(slab, 'frame', split_axis=0, concat_axis=0, tiled=True)  24.7 us
    pallas_call x1, Pallas kernels, attend(): pl.pallas_call(attend_kernel, grid=(GROUPS,), out_shape=(jax.ShapeDtypeSt...  23.7 us
    all_to_all x3, starting transfers between devices, exchange(): lax.all_to_all(slab, 'frame', split_axis=0, concat_axis=0, tiled=True)  20.9 us
    pallas_call x1, Pallas kernels, time_attend(): pl.pallas_call(time_kernel, grid=(GROUPS,), out_shape=jax.ShapeDtypeStruc...  12.4 us
    pallas_call x1, Pallas kernels, project(): pl.pallas_call(project_kernel, grid=(GROUPS,), out_shape=(out, out, out),...  9.16 us
    pallas_call x1, Pallas kernels, own_attend(): pl.pallas_call(own_kernel, grid=(GROUPS,), out_shape=(out, out, out), in_...  8.01 us
    pallas_call x1, Pallas kernels, choose(): pl.pallas_call(choose_kernel, grid=(FRAMES // CHOSEN,), out_shape=jax.Sha...  3.71 us
  transfers between devices with their start and end apart: 3, of which 3 were waited for; matrix products, arithmetic and copies ran while one was open for 0% of the time, Pallas kernels for 10%

profile of v1, /device:TPU:1, one launch (start us, length us, event | category | flops | bytes accessed | tf_op | source)
XLA Modules:
  0.0 165.4 jit_solution(14042857038660563140)
XLA Ops:
  0.6 1.3 reshape.10.gain_ref
  1.9 3.4 %prep.1 = (bf16[384,1280]{1,0:T(8,128)(2,1)}, bf16[128,32,128]{2,1,0:T(8,128)(2,1)}) custom-call(s32[1,2]{1,0:T(1,128)} %pairs_ref.1, bf16[384,1280]{1,0:T(8,128)(2,1)} %video_ref.3, f32[1,1280]{1,0:T(1,128)} %reshape.10.gain_ref), custom_call_target="tpu_custom_call" | custom-call | flops 2949120 | bytes 2949120 | tf_op jit(solution)/shard_map/prep/pallas_call | solution.py:101
  5.3 11.5 %all-to-all-start = ((bf16[128,32,128]{2,1,0:T(8,128)(2,1)}), bf16[128,32,128]{2,1,0:T(8,128)(2,1)S(1)}, u32[]{:S(2)}, u32[]{:S(2)}) async-start(bf16[128,32,128]{2,1,0:T(8,128)(2,1)} %get-tuple-element.12), calls=%async_computation | async-start | bytes 2097152 | tf_op jit(solution)/shard_map/all_to_all | solution.py:415
  16.8 9.2 %project.1 = (bf16[384,1280]{1,0:T(8,128)(2,1)}, bf16[384,1280]{1,0:T(8,128)(2,1)}, bf16[384,1280]{1,0:T(8,128)(2,1)}) custom-call(bf16[384,1280]{1,0:T(8,128)(2,1)} %get-tuple-element.13.rows_ref, bf16[1280,3840]{1,0:T(8,128)(2,1)} %wv_ref.4, bf16[1280,3840]{1,0:T(8,128)(2,1)} %wv_ref.4, bf16[1280,3840]{1,0:T(8,128)(2,1)} %wv_ref.4), custom_call_target="tpu_custom_call" | custom-call | flops 3774873600 | bytes 13762560 | tf_op jit(solution)/shard_map/project/pallas_call | solution.py:126
  25.9 9.9 %all-to-all-done.slab_ref = bf16[128,32,128]{2,1,0:T(8,128)(2,1)S(1)} async-done(((bf16[128,32,128]{2,1,0:T(8,128)(2,1)}), bf16[128,32,128]{2,1,0:T(8,128)(2,1)S(1)}, u32[]{:S(2)}, u32[]{:S(2)}) %all-to-all-start) | async-done | bytes 1048608 | tf_op jit(solution)/shard_map/all_to_all | solution.py:415
  35.9 0.0 copy-start.2
  35.9 1.0 copy-done.2
  36.8 3.7 %choose.1 = bf16[128,2,32,128]{3,2,1,0:T(8,128)(2,1)} custom-call(s32[8]{0:T(128)} %key_list_ref.1, bf16[128,32,128]{2,1,0:T(8,128)(2,1)} %copy-done.2, bf16[384,1280]{1,0:T(8,128)(2,1)} %get-tuple-element.14.after_ref.q_ref), custom_call_target="tpu_custom_call" | custom-call | flops 536870912 | bytes 3145728 | tf_op jit(solution)/shard_map/choose/pallas_call | solution.py:229
  40.5 4.7 %all-to-all-start.1 = ((bf16[128,2,32,128]{3,2,1,0:T(8,128)(2,1)}), bf16[128,2,32,128]{3,2,1,0:T(8,128)(2,1)S(1)}, u32[]{:S(2)}, u32[]{:S(2)}) async-start(bf16[128,2,32,128]{3,2,1,0:T(8,128)(2,1)} %choose.1), calls=%async_computation.1 | async-start | bytes 4194304 | tf_op jit(solution)/shard_map/all_to_all | solution.py:415
  45.2 8.0 %own_attend.1 = (f32[384,1280]{1,0:T(8,128)}, f32[384,1280]{1,0:T(8,128)}, f32[384,1280]{1,0:T(8,128)}) custom-call(bf16[384,1280]{1,0:T(8,128)(2,1)} %get-tuple-element.14.after_ref.q_ref, bf16[384,1280]{1,0:T(8,128)(2,1)} %get-tuple-element.15.k_ref, bf16[384,1280]{1,0:T(8,128)(2,1)} %get-tuple-element.16.v_ref), custom_call_target="tpu_custom_call" | custom-call | flops 1509949440 | bytes 8847360 | tf_op jit(solution)/shard_map/own_attend/pallas_call | solution.py:192
  53.3 22.4 %all-to-all-done.1.slab_ref = bf16[128,2,32,128]{3,2,1,0:T(8,128)(2,1)S(1)} async-done(((bf16[128,2,32,128]{3,2,1,0:T(8,128)(2,1)}), bf16[128,2,32,128]{3,2,1,0:T(8,128)(2,1)S(1)}, u32[]{:S(2)}, u32[]{:S(2)}) %all-to-all-start.1) | async-done | bytes 2097184 | tf_op jit(solution)/shard_map/all_to_all | solution.py:415
  75.7 0.0 copy-start
  75.7 1.3 copy-done
  77.0 23.7 %attend.1 = (bf16[384,1280]{1,0:T(8,128)(2,1)}, bf16[128,32,128]{2,1,0:T(8,128)(2,1)}) custom-call(bf16[128,2,32,128]{3,2,1,0:T(8,128)(2,1)} %copy-done, bf16[384,1280]{1,0:T(8,128)(2,1)} %get-tuple-element.14.after_ref.q_ref, f32[384,1280]{1,0:T(8,128)} %get-tuple-element.17.mixed_ref, f32[384,1280]{1,0:T(8,128)} %get-tuple-element.18.total_ref, ...), custom_call_target="tpu_custom_call" | custom-call | flops 8053063680 | bytes 19660800 | tf_op jit(solution)/shard_map/attend/pallas_call | solution.py:288
  100.8 0.0 copy-start.3
  100.8 4.7 %all-to-all-start.2 = ((bf16[128,32,128]{2,1,0:T(8,128)(2,1)}), bf16[128,32,128]{2,1,0:T(8,128)(2,1)S(1)}, u32[]{:S(2)}, u32[]{:S(2)}) async-start(bf16[128,32,128]{2,1,0:T(8,128)(2,1)} %get-tuple-element.21), calls=%async_computation.2 | async-start | bytes 2097152 | tf_op jit(solution)/shard_map/all_to_all | solution.py:415
  105.5 0.0 copy-done.3
  105.5 0.6 reshape.11.gain_ref
  106.1 18.6 %all-to-all-done.2.slab_ref = bf16[128,32,128]{2,1,0:T(8,128)(2,1)S(1)} async-done(((bf16[128,32,128]{2,1,0:T(8,128)(2,1)}), bf16[128,32,128]{2,1,0:T(8,128)(2,1)S(1)}, u32[]{:S(2)}, u32[]{:S(2)}) %all-to-all-start.2) | async-done | bytes 1048608 | tf_op jit(solution)/shard_map/all_to_all | solution.py:415
  124.7 0.0 copy-start.1
  124.7 1.0 copy-done.1
  125.7 12.4 %time_attend.1 = bf16[128,32,128]{2,1,0:T(8,128)(2,1)} custom-call(bf16[128,32,128]{2,1,0:T(8,128)(2,1)} %copy-done.1, f32[1,1280]{1,0:T(1,128)} %reshape.11.gain_ref, bf16[1280,3840]{1,0:T(8,128)(2,1)} %wv_ref.5, bf16[1280,3840]{1,0:T(8,128)(2,1)} %wv_ref.5, bf16[1280,3840]{1,0:T(8,128)(2,1)} %wv_ref.5), custom_call_target="tpu_custom_call" | custom-call | flops 4278190080 | bytes 11796480 | tf_op jit(solution)/shard_map/time_attend/pallas_call | solution.py:367
  138.1 24.7 %all_to_all.20.slab_ref = bf16[128,32,128]{2,1,0:T(8,128)(2,1)} all-to-all(bf16[128,32,128]{2,1,0:T(8,128)(2,1)} %time_attend.1), channel_id=1, replica_groups=mesh['frame'=128] {'frame'}, dimensions={0} | all-to-all | bytes 2097152 | tf_op jit(solution)/shard_map/all_to_all | solution.py:415
  162.8 2.6 %unpack.1 = bf16[384,1280]{1,0:T(8,128)(2,1)} custom-call(bf16[128,32,128]{2,1,0:T(8,128)(2,1)} %all_to_all.20.slab_ref), custom_call_target="tpu_custom_call" | custom-call | flops 251658240 | bytes 1966080 | tf_op jit(solution)/shard_map/unpack/pallas_call | solution.py:403
Async XLA Ops:
  5.3 30.6 %all-to-all-start = ((bf16[128,32,128]{2,1,0:T(8,128)(2,1)}), bf16[128,32,128]{2,1,0:T(8,128)(2,1)S(1)}, u32[]{:S(2)}, u32[]{:S(2)}) async-start(bf16[128,32,128]{2,1,0:T(8,128)(2,1)} %get-tuple-element.12), calls=%async_computation | async-start | bytes 2097152 | tf_op jit(solution)/shard_map/all_to_all | solution.py:415
  35.9 1.0 copy-start.2
  40.5 35.1 %all-to-all-start.1 = ((bf16[128,2,32,128]{3,2,1,0:T(8,128)(2,1)}), bf16[128,2,32,128]{3,2,1,0:T(8,128)(2,1)S(1)}, u32[]{:S(2)}, u32[]{:S(2)}) async-start(bf16[128,2,32,128]{3,2,1,0:T(8,128)(2,1)} %choose.1), calls=%async_computation.1 | async-start | bytes 4194304 | tf_op jit(solution)/shard_map/all_to_all | solution.py:415
  75.7 1.3 copy-start
  100.8 4.7 %copy-start.3 = (f32[1280]{0:T(1024)S(1)}, f32[1280]{0:T(1024)}, u32[]{:S(2)}) copy-start(f32[1280]{0:T(1024)} %param.14) | copy-start | bytes 15364
  100.8 23.9 %all-to-all-start.2 = ((bf16[128,32,128]{2,1,0:T(8,128)(2,1)}), bf16[128,32,128]{2,1,0:T(8,128)(2,1)S(1)}, u32[]{:S(2)}, u32[]{:S(2)}) async-start(bf16[128,32,128]{2,1,0:T(8,128)(2,1)} %get-tuple-element.21), calls=%async_computation.2 | async-start | bytes 2097152 | tf_op jit(solution)/shard_map/all_to_all | solution.py:415
  124.7 1.0 copy-start.1

commit v2 on v1

v2 whole, which is shorter than its diff:
```python
import jax
import jax.numpy as jnp
from jax import lax
from jax.experimental import pallas as pl
from jax.experimental.pallas import tpu as pltpu
from jax.sharding import PartitionSpec as P

WIDTH = 1280
HEADS = 20
HEAD = 64
TOK = 384
FRAMES = 128
KEYS = 8
PARTS = TOK // FRAMES
LANES = 128
COLS = WIDTH // LANES
SLAB = 32
GROUP = 256
GROUPS = WIDTH // GROUP
VMEM = 52
SCALE = 0.125 * 1.4426950408889634

bf16 = jnp.bfloat16
f32 = jnp.float32


def params(mib, **more):
    return pltpu.CompilerParams(vmem_limit_bytes=mib << 20, **more)


def cost(flops, moved, exps=0):
    return pl.CostEstimate(flops=int(flops), bytes_accessed=int(moved), transcendentals=int(exps))


def in_vmem(x):
    return pltpu.with_memory_space_constraint(x, pltpu.VMEM)


def in_hbm(x):
    return pltpu.with_memory_space_constraint(x, pltpu.HBM)


WHOLE = pl.BlockSpec(memory_space=pltpu.VMEM)
THERE = pl.BlockSpec(memory_space=pl.ANY)
SMALL = pl.BlockSpec(memory_space=pltpu.SMEM)


def norm_rows(values, gain):
    centred = values - jnp.mean(values, axis=-1, keepdims=True)
    spread = jnp.mean(centred * centred, axis=-1, keepdims=True)
    return (centred * lax.rsqrt(spread + 1e-05) * gain).astype(bf16)


def swap_matrix():
    row = lax.broadcasted_iota(jnp.int32, (256, 256), 0)
    col = lax.broadcasted_iota(jnp.int32, (256, 256), 1)
    return jnp.where(col == (row % 16) * 16 + row // 16, 1.0, 0.0).astype(bf16)


def rows_to_slab(rows_ref, slab_ref, swap, spare=None):
    for half in range(2):
        for pair in range(4):
            sides = []
            for block in (2 * pair, 2 * pair + 1):
                tiles = []
                for unit in range(16 * half, 16 * half + 16):
                    k, g = divmod(unit, COLS)
                    if k < PARTS:
                        at = k * FRAMES + 16 * block
                        tiles.append(rows_ref[at : at + 16, g * LANES : (g + 1) * LANES])
                    elif spare is None:
                        tiles.append(jnp.zeros((16, LANES), bf16))
                    else:
                        tiles.append(spare[unit - PARTS * COLS])
                sides.append(jnp.concatenate(tiles, axis=0))
            both = jnp.concatenate(sides, axis=1)
            moved = jnp.dot(swap, both, preferred_element_type=f32).astype(bf16)
            for side in range(2):
                block = 2 * pair + side
                slab_ref[16 * block : 16 * block + 16, 16 * half : 16 * half + 16, :] = moved[
                    :, side * LANES : (side + 1) * LANES
                ].reshape(16, 16, LANES)


def slab_to_rows(load, rows_ref, swap, first=0):
    for block in range(8):
        both = jnp.concatenate(
            [load(block, half).reshape(256, LANES) for half in range(2)], axis=1
        )
        moved = jnp.dot(swap, both, preferred_element_type=f32).astype(bf16)
        for unit in range(PARTS * COLS):
            half, row = divmod(unit, 16)
            k, g = divmod(unit, COLS)
            at = first + k * FRAMES + 16 * block
            rows_ref[at : at + 16, g * LANES : (g + 1) * LANES] = moved[
                16 * row : 16 * row + 16, half * LANES : (half + 1) * LANES
            ]


def prep_kernel(pairs_ref, video_ref, gain_ref, normed_ref, slab_ref):
    for k in range(PARTS):
        rows = pl.ds(k * FRAMES, FRAMES)
        normed_ref[rows, :] = norm_rows(video_ref[rows, :].astype(f32), gain_ref[...].reshape(1, WIDTH))
    spare = [
        jnp.full((16, LANES), pairs_ref[0, which], jnp.int32).astype(f32).astype(bf16)
        for which in range(2)
    ]
    rows_to_slab(normed_ref, slab_ref, swap_matrix(), spare)


def prep(pairs, video, gain):
    return pl.pallas_call(
        prep_kernel,
        out_shape=(
            pltpu.HBM((TOK, WIDTH), bf16),
            pltpu.HBM((FRAMES, SLAB, LANES), bf16),
        ),
        in_specs=[SMALL, WHOLE, WHOLE],
        out_specs=(WHOLE, WHOLE),
        compiler_params=params(VMEM),
        cost_estimate=cost(6 * TOK * WIDTH, 6 * TOK * WIDTH),
        name="prep",
    )(in_hbm(pairs), in_hbm(video), in_hbm(gain))


def project_kernel(rows_ref, wq_ref, wk_ref, wv_ref, q_ref, k_ref, v_ref):
    rows = rows_ref[...]
    queries = jnp.dot(rows, wq_ref[...], preferred_element_type=f32) * SCALE
    q_ref[...] = queries.astype(bf16)
    k_ref[...] = jnp.dot(rows, wk_ref[...], preferred_element_type=f32).astype(bf16)
    v_ref[...] = jnp.dot(rows, wv_ref[...], preferred_element_type=f32).astype(bf16)


def project(rows, weight):
    out = pltpu.HBM((TOK, WIDTH), bf16)
    out_spec = pl.BlockSpec((TOK, GROUP), lambda i: (0, i))
    return pl.pallas_call(
        project_kernel,
        grid=(GROUPS,),
        out_shape=(out, out, out),
        in_specs=[
            WHOLE,
            pl.BlockSpec((WIDTH, GROUP), lambda i: (0, i)),
            pl.BlockSpec((WIDTH, GROUP), lambda i: (0, GROUPS + i)),
            pl.BlockSpec((WIDTH, GROUP), lambda i: (0, 2 * GROUPS + i)),
        ],
        out_specs=(out_spec, out_spec, out_spec),
        compiler_params=params(VMEM),
        cost_estimate=cost(6 * TOK * WIDTH * WIDTH, 6 * WIDTH * WIDTH + 8 * TOK * WIDTH),
        name="project",
    )(in_hbm(rows), in_hbm(weight), in_hbm(weight), in_hbm(weight))


def low_lanes(rows):
    return lax.broadcasted_iota(jnp.int32, (rows, LANES), 1) < HEAD


def attend_pairs(units):
    scores, padded = [], []
    for queries, keys, values, _ in units:
        low_q, low_v = low_lanes(queries.shape[0]), low_lanes(values.shape[0])
        wide = queries.astype(f32)
        for head in range(2):
            mine = jnp.where(low_q, wide, 0.0) if head == 0 else jnp.where(low_q, 0.0, wide)
            rest = jnp.where(low_v, values, 1.0) if head == 0 else jnp.where(low_v, 1.0, values)
            padded.append(rest.astype(bf16))
            scores.append(
                lax.dot_general(
                    mine.astype(bf16), keys, (((1,), (1,)), ((), ())), preferred_element_type=f32
                )
            )
    tops = [jnp.max(s, axis=-1, keepdims=True) for s in scores]
    for i, (_, _, _, top) in enumerate(units):
        if top is not None:
            for head in range(2):
                other = top[:, head * HEAD : head * HEAD + 1]
                tops[2 * i + head] = jnp.maximum(tops[2 * i + head], other)
    weights = [jnp.exp2(s - top).astype(bf16) for s, top in zip(scores, tops)]
    outs = [jnp.dot(w, v, preferred_element_type=f32) for w, v in zip(weights, padded)]
    given = []
    for i, (queries, _, _, _) in enumerate(units):
        low = low_lanes(queries.shape[0])
        one, two = outs[2 * i], outs[2 * i + 1]
        total = pltpu.roll(jnp.where(low, two, one), HEAD, 1)
        given.append((jnp.where(low, one, two), total, tops[2 * i : 2 * i + 2]))
    return given


def group_lanes(group, size, offset=0):
    return pl.ds(pl.multiple_of(offset + group * GROUP, LANES), size)


def own_kernel(q_ref, k_ref, v_ref, mixed_ref, total_ref, top_ref):
    @pl.loop(0, GROUPS)
    def _(group):
        places = [group_lanes(group, LANES, pair * LANES) for pair in range(2)]
        units = [(q_ref[:, at], k_ref[:, at], v_ref[:, at].astype(f32), None) for at in places]
        low = low_lanes(TOK)
        for at, (mixed, total, tops) in zip(places, attend_pairs(units)):
            mixed_ref[:, at] = mixed
            total_ref[:, at] = total
            top_ref[:, at] = jnp.where(low, tops[0], tops[1])


def own_attend(queries, keys, values):
    out = pltpu.HBM((TOK, WIDTH), f32)
    return pl.pallas_call(
        own_kernel,
        out_shape=(out, out, out),
        in_specs=[WHOLE, WHOLE, WHOLE],
        out_specs=(WHOLE, WHOLE, WHOLE),
        compiler_params=params(VMEM),
        cost_estimate=cost(8 * TOK * TOK * WIDTH, 30 * TOK * WIDTH, HEADS * TOK * TOK),
        name="own_attend",
    )(in_hbm(queries), in_hbm(keys), in_hbm(values))


def choose_kernel(key_list_ref, slab_ref, after_ref, out_ref):
    del after_ref
    halves = [
        jnp.concatenate([slab_ref[key_list_ref[s], at : at + 16, :] for s in range(KEYS)], axis=0)
        for at in (0, 16)
    ]
    keys = jnp.concatenate(halves, axis=1)
    row = lax.broadcasted_iota(jnp.int32, (16, LANES), 0)
    col = lax.broadcasted_iota(jnp.int32, (16, LANES), 1)
    slot = jnp.where(col % 16 == row, col // 16, -1).astype(f32)
    for f in range(0, FRAMES, 8):
        picks = []
        for more in range(8):
            spare = slab_ref[f + more, 16:32, :].astype(f32)
            for which in range(2):
                wanted = spare[14 + which : 15 + which, :]
                picks.append(jnp.where(slot == wanted, 1.0, 0.0).astype(bf16))
        chosen = jnp.dot(jnp.concatenate(picks, axis=0), keys, preferred_element_type=f32)
        chosen = chosen.astype(bf16).reshape(8, 2, 16, 2 * LANES)
        out_ref[f : f + 8, :, 0:16, :] = chosen[..., :LANES]
        out_ref[f : f + 8, :, 16:32, :] = chosen[..., LANES:]


def choose(key_list, slab, after):
    return pl.pallas_call(
        choose_kernel,
        out_shape=jax.ShapeDtypeStruct((FRAMES, 2, SLAB, LANES), bf16),
        in_specs=[SMALL, WHOLE, THERE],
        out_specs=WHOLE,
        compiler_params=params(VMEM),
        cost_estimate=cost(4 * FRAMES * SLAB * LANES * 256, 6 * FRAMES * SLAB * LANES),
        name="choose",
    )(in_hbm(key_list), in_vmem(slab), in_hbm(after))


LARGE = 1e30


def attend_kernel(
    slab_ref, q_hbm, mixed_hbm, total_hbm, top_hbm, weight_hbm, wo_hbm, video_hbm,
    spatial_ref, out_slab_ref,
    rows_ref, heads_ref, most_ref, q_ref, mixed_ref, total_ref, top_ref, wk_ref, wv_ref,
    wo_ref, video_ref, sems, last_sems,
):
    def copies(group):
        pairs = (
            (weight_hbm.at[:, group_lanes(group, GROUP, WIDTH)], wk_ref),
            (weight_hbm.at[:, group_lanes(group, GROUP, 2 * WIDTH)], wv_ref),
            (q_hbm.at[:, group_lanes(group, GROUP)], q_ref),
            (top_hbm.at[:, group_lanes(group, GROUP)], top_ref),
            (mixed_hbm.at[:, group_lanes(group, GROUP)], mixed_ref),
            (total_hbm.at[:, group_lanes(group, GROUP)], total_ref),
        )
        return [
            pltpu.make_async_copy(source, target.at[group], sems.at[i, group])
            for i, (source, target) in enumerate(pairs)
        ]

    last = (
        pltpu.make_async_copy(wo_hbm, wo_ref, last_sems.at[0]),
        pltpu.make_async_copy(video_hbm, video_ref, last_sems.at[1]),
    )
    for group in range(GROUPS):
        for copy in copies(group):
            copy.start()
    for copy in last:
        copy.start()

    swap = swap_matrix()
    for which in range(2):
        slab_to_rows(
            lambda block, half: slab_ref[
                16 * block : 16 * block + 16, which, 16 * half : 16 * half + 16, :
            ],
            rows_ref, swap, which * TOK,
        )
    most_ref[...] = jnp.zeros_like(most_ref)

    def project_group(group):
        rows = rows_ref[...]
        keys = jnp.dot(rows, wk_ref[group], preferred_element_type=f32).astype(bf16)
        return keys, jnp.dot(rows, wv_ref[group], preferred_element_type=f32)

    @pl.loop(0, GROUPS)
    def _(group):
        for copy in copies(group):
            copy.wait()
        keys, values = project_group(group)
        low_q, low_v = low_lanes(TOK), low_lanes(2 * TOK)
        outs = []
        for pair in range(2):
            lanes = slice(pair * LANES, (pair + 1) * LANES)
            queries = q_ref[group, :, lanes].astype(f32)
            some = values[:, lanes]
            top = top_ref[group, :, lanes]
            other = pltpu.roll(top, HEAD, 1)
            for head in range(2):
                if head == 0:
                    mine, padded = jnp.where(low_q, queries, 0.0), jnp.where(low_v, some, 1.0)
                    wide = jnp.where(low_q, top, other)
                else:
                    mine, padded = jnp.where(low_q, 0.0, queries), jnp.where(low_v, 1.0, some)
                    wide = jnp.where(low_q, other, top)
                scores = lax.dot_general(
                    mine.astype(bf16), keys[:, lanes], (((1,), (1,)), ((), ())),
                    preferred_element_type=f32,
                )
                tops = jnp.concatenate([wide] * (2 * TOK // LANES), axis=1)
                weights = jnp.exp2(scores - tops).astype(bf16)
                outs.append(jnp.dot(weights, padded.astype(bf16), preferred_element_type=f32))
        for pair in range(2):
            lanes = slice(pair * LANES, (pair + 1) * LANES)
            one, two = outs[2 * pair], outs[2 * pair + 1]
            mixed = jnp.where(low_q, one, two) + mixed_ref[group, :, lanes]
            total = jnp.where(low_q, two, one)
            total = pltpu.roll(total, HEAD, 1) + total_ref[group, :, lanes]
            heads_ref[2 * group + pair] = (mixed / total).astype(bf16)
            most = jnp.max(total.reshape(TOK // 8, 8, LANES), axis=0)
            most_ref[...] = jnp.maximum(most_ref[...], most)

    @pl.when(jnp.logical_not(jnp.max(most_ref[...]) < LARGE))
    def _():
        @pl.loop(0, GROUPS)
        def _(group):
            keys, values = project_group(group)
            for pair in range(2):
                lanes = slice(pair * LANES, (pair + 1) * LANES)
                top = top_ref[group, :, lanes]
                ((mixed, total, tops),) = attend_pairs(
                    [(q_ref[group, :, lanes], keys[:, lanes], values[:, lanes], top)]
                )
                less = jnp.exp2(top - jnp.where(low_lanes(TOK), tops[0], tops[1]))
                mixed = mixed + mixed_ref[group, :, lanes] * less
                total = total + total_ref[group, :, lanes] * less
                heads_ref[2 * group + pair] = (mixed / total).astype(bf16)

    for copy in last:
        copy.wait()
    for k in range(PARTS):
        rows = pl.ds(k * FRAMES, FRAMES)
        heads = jnp.concatenate([heads_ref[c, rows, :] for c in range(COLS)], axis=1)
        added = jnp.dot(heads, wo_ref[...], preferred_element_type=f32)
        spatial_ref[rows, :] = (video_ref[rows, :].astype(f32) + added).astype(bf16)
    rows_to_slab(spatial_ref, out_slab_ref, swap)


def attend(slab, queries, mixed, total, top, weight, out_weight, video):
    return pl.pallas_call(
        attend_kernel,
        out_shape=(
            jax.ShapeDtypeStruct((TOK, WIDTH), bf16),
            jax.ShapeDtypeStruct((FRAMES, SLAB, LANES), bf16),
        ),
        in_specs=[WHOLE] + [THERE] * 7,
        out_specs=(WHOLE, WHOLE),
        scratch_shapes=[
            pltpu.VMEM((2 * TOK, WIDTH), bf16),
            pltpu.VMEM((COLS, TOK, LANES), bf16),
            pltpu.VMEM((8, LANES), f32),
            pltpu.VMEM((GROUPS, TOK, GROUP), bf16),
            pltpu.VMEM((GROUPS, TOK, GROUP), f32),
            pltpu.VMEM((GROUPS, TOK, GROUP), f32),
            pltpu.VMEM((GROUPS, TOK, GROUP), f32),
            pltpu.VMEM((GROUPS, WIDTH, GROUP), bf16),
            pltpu.VMEM((GROUPS, WIDTH, GROUP), bf16),
            pltpu.VMEM((WIDTH, WIDTH), bf16),
            pltpu.VMEM((TOK, WIDTH), bf16),
            pltpu.SemaphoreType.DMA((6, GROUPS)),
            pltpu.SemaphoreType.DMA((2,)),
        ],
        compiler_params=params(VMEM),
        cost_estimate=cost(
            8 * TOK * WIDTH * WIDTH + 16 * TOK * TOK * WIDTH,
            6 * WIDTH * WIDTH + 20 * TOK * WIDTH,
            2 * HEADS * TOK * TOK,
        ),
        name="attend",
    )(
        in_vmem(slab), in_hbm(queries), in_hbm(mixed), in_hbm(total), in_hbm(top),
        in_hbm(weight), in_hbm(out_weight), in_hbm(video),
    )


def time_kernel(
    slab_ref, gain_ref, weight_hbm, out_slab_ref, rows_ref, heads_ref, weight_ref, sems
):
    def copies(group):
        return [
            pltpu.make_async_copy(
                weight_hbm.at[:, group_lanes(group, GROUP, which * WIDTH)],
                weight_ref.at[which, group],
                sems.at[which, group],
            )
            for which in range(3)
        ]

    for group in range(GROUPS):
        for copy in copies(group):
            copy.start()
    swap = swap_matrix()
    slab_to_rows(
        lambda block, half: slab_ref[16 * block : 16 * block + 16, 16 * half : 16 * half + 16, :],
        rows_ref, swap,
    )
    for k in range(PARTS):
        rows = pl.ds(k * FRAMES, FRAMES)
        rows_ref[rows, :] = norm_rows(rows_ref[rows, :].astype(f32), gain_ref[...].reshape(1, WIDTH))

    @pl.loop(0, GROUPS)
    def _(group):
        for copy in copies(group):
            copy.wait()
        rows = rows_ref[...]
        made = [
            jnp.dot(rows, weight_ref[which, group], preferred_element_type=f32)
            for which in range(3)
        ]
        queries, keys, values = (made[0] * SCALE).astype(bf16), made[1].astype(bf16), made[2]
        units, places = [], []
        for pair in range(2):
            lanes = slice(pair * LANES, (pair + 1) * LANES)
            for k in range(PARTS):
                at = slice(k * FRAMES, (k + 1) * FRAMES)
                units.append((queries[at, lanes], keys[at, lanes], values[at, lanes], None))
                places.append((pair, at))
        for (pair, at), (mixed, total, _) in zip(places, attend_pairs(units)):
            heads_ref[2 * group + pair, at, :] = (mixed / total).astype(bf16)

    for k in range(PARTS):
        at = slice(k * FRAMES, (k + 1) * FRAMES)
        for g in range(COLS):
            rows_ref[at, g * LANES : (g + 1) * LANES] = heads_ref[g, at, :]
    rows_to_slab(rows_ref, out_slab_ref, swap)


def time_attend(slab, gain, weight):
    return pl.pallas_call(
        time_kernel,
        out_shape=jax.ShapeDtypeStruct((FRAMES, SLAB, LANES), bf16),
        in_specs=[WHOLE, WHOLE, THERE],
        out_specs=WHOLE,
        scratch_shapes=[
            pltpu.VMEM((TOK, WIDTH), bf16),
            pltpu.VMEM((COLS, TOK, LANES), bf16),
            pltpu.VMEM((3, GROUPS, WIDTH, GROUP), bf16),
            pltpu.SemaphoreType.DMA((3, GROUPS)),
        ],
        compiler_params=params(VMEM),
        cost_estimate=cost(
            6 * TOK * WIDTH * WIDTH + 8 * TOK * FRAMES * WIDTH,
            6 * WIDTH * WIDTH + 4 * TOK * WIDTH,
            HEADS * TOK * FRAMES,
        ),
        name="time_attend",
    )(in_vmem(slab), in_hbm(gain), in_hbm(weight))


def unpack_kernel(slab_ref, out_ref):
    slab_to_rows(
        lambda block, half: slab_ref[16 * block : 16 * block + 16, 16 * half : 16 * half + 16, :],
        out_ref, swap_matrix(),
    )


def unpack(slab):
    return pl.pallas_call(
        unpack_kernel,
        out_shape=jax.ShapeDtypeStruct((TOK, WIDTH), bf16),
        in_specs=[WHOLE],
        out_specs=WHOLE,
        compiler_params=params(VMEM),
        cost_estimate=cost(2 * TOK * WIDTH * 256, 4 * TOK * WIDTH),
        name="unpack",
    )(in_vmem(slab))


def exchange(slab):
    return lax.all_to_all(slab, "frame", split_axis=0, concat_axis=0, tiled=True)


def body(video, key_list, pairs, norm_gain, qkv_weight, out_weight, time_gain, time_weight):
    normed, slab = prep(pairs, video, norm_gain)
    spread = exchange(slab)
    queries, keys, values = project(normed, qkv_weight)
    wanted = exchange(choose(key_list, spread, queries))
    mixed, total, top = own_attend(queries, keys, values)
    spatial, slab = attend(wanted, queries, mixed, total, top, qkv_weight, out_weight, video)
    slab = time_attend(exchange(slab), time_gain, time_weight)
    return spatial, unpack(exchange(slab))


def solution(mesh):
    return jax.shard_map(
        body,
        mesh=mesh,
        in_specs=(P("frame", None), P(), P("frame", None), P(), P(), P(), P(), P()),
        out_specs=(P("frame", None), P("frame", None)),
        check_vma=False,
    )
```

time: 166 us -> 154 us (0.928)
  blocking collectives: 24.7 us -> 48.1 us
  waiting for transfers between devices: 50.9 us -> 31.4 us
  Pallas kernels: 63 us -> 57 us
  local copies, waits for them, and re-layouts: 5.19 us -> 0 us
  starting transfers between devices: 20.9 us -> 16.2 us
    all_to_all x1 -> x2, blocking collectives: 24.7 us -> 48.1 us  [exchange(): lax.all_to_all(slab, 'frame', split_axis=0, concat_axis=0, tiled=True)]
    all_to_all x3 -> x2, waiting for transfers between devices: 50.9 us -> 31.4 us  [exchange(): lax.all_to_all(slab, 'frame', split_axis=0, concat_axis=0, tiled=True)]
    pallas_call x5, Pallas kernels: 51.2 us -> 46.4 us  [the longest x1 19.6 us: attend(): pl.pallas_call(attend_kernel, out_shape=(jax.ShapeDtypeStruct((TOK, WIDTH...]
    all_to_all x3 -> x2, starting transfers between devices: 20.9 us -> 16.2 us  [exchange(): lax.all_to_all(slab, 'frame', split_axis=0, concat_axis=0, tiled=True)]
    unnamed x8 -> x0, local copies, waits for them, and re-layouts: 3.3 us -> none
    reshape x2 -> x0, local copies, waits for them, and re-layouts: 1.89 us -> none  [the longest x1 1.29 us: body(): normed, slab = prep(pairs, video, norm_gain.reshape(1, WIDTH))]
  transfers between devices with their start and end apart: 3 -> 2, of which waited for: 3 -> 2; matrix products, arithmetic and copies ran while one was open for 0% -> 0% of each run, Pallas kernels for 10% -> 12%
where the time goes in v2:
time: 154 us; the launch traced here: 153 us
  Pallas kernels  57 us (37%)
  blocking collectives  48.1 us (31%)
  waiting for transfers between devices  31.4 us (20%)
  starting transfers between devices  16.2 us (11%)
    all_to_all x2, blocking collectives, exchange(): lax.all_to_all(slab, 'frame', split_axis=0, concat_axis=0, tiled=True)  48.1 us
    all_to_all x2, waiting for transfers between devices, exchange(): lax.all_to_all(slab, 'frame', split_axis=0, concat_axis=0, tiled=True)  31.4 us
    pallas_call x1, Pallas kernels, attend(): pl.pallas_call(attend_kernel, out_shape=(jax.ShapeDtypeStruct((TOK, WIDTH...  19.6 us
    all_to_all x2, starting transfers between devices, exchange(): lax.all_to_all(slab, 'frame', split_axis=0, concat_axis=0, tiled=True)  16.2 us
    pallas_call x1, Pallas kernels, time_attend(): pl.pallas_call(time_kernel, out_shape=jax.ShapeDtypeStruct((FRAMES, SLAB,...  11.8 us
    pallas_call x1, Pallas kernels, project(): pl.pallas_call(project_kernel, grid=(GROUPS,), out_shape=(out, out, out),...  9.16 us
    pallas_call x1, Pallas kernels, own_attend(): pl.pallas_call(own_kernel, out_shape=(out, out, out), in_specs=[WHOLE, WH...  8.98 us
    pallas_call x1, Pallas kernels, prep(): pl.pallas_call(prep_kernel, out_shape=(pltpu.HBM((TOK, WIDTH), bf16), plt...  3.36 us
  transfers between devices with their start and end apart: 2, of which 2 were waited for; matrix products, arithmetic and copies ran while one was open for 0% of the time, Pallas kernels for 12%

profile of v2, /device:TPU:1, one launch (start us, length us, event | category | flops | bytes accessed | tf_op | source)
XLA Modules:
  0.0 153.3 jit_solution(7295432223481788257)
XLA Ops:
  0.6 3.4 %prep.1 = (bf16[384,1280]{1,0:T(8,128)(2,1)}, bf16[128,32,128]{2,1,0:T(8,128)(2,1)}) custom-call(s32[1,2]{1,0:T(1,128)} %pairs_ref.1, bf16[384,1280]{1,0:T(8,128)(2,1)} %video_hbm.1, f32[1280]{0:T(1024)} %gain_ref.2), custom_call_target="tpu_custom_call" | custom-call | flops 2949120 | bytes 2949120 | tf_op jit(solution)/shard_map/prep/pallas_call | solution.py:112
  4.0 11.5 %all-to-all-start = ((bf16[128,32,128]{2,1,0:T(8,128)(2,1)}), bf16[128,32,128]{2,1,0:T(8,128)(2,1)S(1)}, u32[]{:S(2)}, u32[]{:S(2)}) async-start(bf16[128,32,128]{2,1,0:T(8,128)(2,1)} %get-tuple-element.12), calls=%async_computation | async-start | bytes 2097152 | tf_op jit(solution)/shard_map/all_to_all | solution.py:495
  15.5 9.2 %project.1 = (bf16[384,1280]{1,0:T(8,128)(2,1)}, bf16[384,1280]{1,0:T(8,128)(2,1)}, bf16[384,1280]{1,0:T(8,128)(2,1)}) custom-call(bf16[384,1280]{1,0:T(8,128)(2,1)} %get-tuple-element.13.rows_ref, bf16[1280,3840]{1,0:T(8,128)(2,1)} %weight_hbm.2, bf16[1280,3840]{1,0:T(8,128)(2,1)} %weight_hbm.2, bf16[1280,3840]{1,0:T(8,128)(2,1)} %weight_hbm.2), custom_call_target="tpu_custom_call" | custom-call | flops 3774873600 | bytes 13762560 | tf_op jit(solution)/shard_map/project/pallas_call | solution.py:137
  24.7 9.9 %all-to-all-done.slab_ref = bf16[128,32,128]{2,1,0:T(8,128)(2,1)S(1)} async-done(((bf16[128,32,128]{2,1,0:T(8,128)(2,1)}), bf16[128,32,128]{2,1,0:T(8,128)(2,1)S(1)}, u32[]{:S(2)}, u32[]{:S(2)}) %all-to-all-start) | async-done | bytes 1048608 | tf_op jit(solution)/shard_map/all_to_all | solution.py:495
  34.6 2.7 %choose.1 = bf16[128,2,32,128]{3,2,1,0:T(8,128)(2,1)} custom-call(s32[8]{0:T(128)} %key_list_ref.1, bf16[128,32,128]{2,1,0:T(8,128)(2,1)S(1)} %all-to-all-done.slab_ref, bf16[384,1280]{1,0:T(8,128)(2,1)} %get-tuple-element.14.after_ref.q_ref.q_hbm), custom_call_target="tpu_custom_call" | custom-call | flops 536870912 | bytes 3145728 | tf_op jit(solution)/shard_map/choose/pallas_call | solution.py:242
  37.3 4.7 %all-to-all-start.1 = ((bf16[128,2,32,128]{3,2,1,0:T(8,128)(2,1)}), bf16[128,2,32,128]{3,2,1,0:T(8,128)(2,1)S(1)}, u32[]{:S(2)}, u32[]{:S(2)}) async-start(bf16[128,2,32,128]{3,2,1,0:T(8,128)(2,1)} %choose.1), calls=%async_computation.1 | async-start | bytes 4194304 | tf_op jit(solution)/shard_map/all_to_all | solution.py:495
  42.0 9.0 %own_attend.1 = (f32[384,1280]{1,0:T(8,128)}, f32[384,1280]{1,0:T(8,128)}, f32[384,1280]{1,0:T(8,128)}) custom-call(bf16[384,1280]{1,0:T(8,128)(2,1)} %get-tuple-element.14.after_ref.q_ref.q_hbm, bf16[384,1280]{1,0:T(8,128)(2,1)} %get-tuple-element.15.k_ref, bf16[384,1280]{1,0:T(8,128)(2,1)} %get-tuple-element.16.v_ref), custom_call_target="tpu_custom_call" | custom-call | flops 1509949440 | bytes 14745600 | tf_op jit(solution)/shard_map/own_attend/pallas_call | solution.py:207
  51.0 21.5 %all-to-all-done.1.slab_ref = bf16[128,2,32,128]{3,2,1,0:T(8,128)(2,1)S(1)} async-done(((bf16[128,2,32,128]{3,2,1,0:T(8,128)(2,1)}), bf16[128,2,32,128]{3,2,1,0:T(8,128)(2,1)S(1)}, u32[]{:S(2)}, u32[]{:S(2)}) %all-to-all-start.1) | async-done | bytes 2097184 | tf_op jit(solution)/shard_map/all_to_all | solution.py:495
  72.4 19.6 %attend.1 = (bf16[384,1280]{1,0:T(8,128)(2,1)}, bf16[128,32,128]{2,1,0:T(8,128)(2,1)}) custom-call(bf16[128,2,32,128]{3,2,1,0:T(8,128)(2,1)S(1)} %all-to-all-done.1.slab_ref, bf16[384,1280]{1,0:T(8,128)(2,1)} %get-tuple-element.14.after_ref.q_ref.q_hbm, f32[384,1280]{1,0:T(8,128)} %get-tuple-element.17.mixed_hbm, f32[384,1280]{1,0:T(8,128)} %get-tuple-element.18.total_hbm, ...), custom_call_target="tpu_custom_call" | custom-call | flops 8053063680 | bytes 19660800 | tf_op jit(solution)/shard_map/attend/pallas_call | solution.py:365
  92.0 24.0 %all_to_all.20.slab_ref = bf16[128,32,128]{2,1,0:T(8,128)(2,1)S(1)} all-to-all(bf16[128,32,128]{2,1,0:T(8,128)(2,1)} %get-tuple-element.21), channel_id=1, replica_groups=mesh['frame'=128] {'frame'}, dimensions={0} | all-to-all | bytes 2097152 | tf_op jit(solution)/shard_map/all_to_all | solution.py:495
  116.0 11.8 %time_attend.1 = bf16[128,32,128]{2,1,0:T(8,128)(2,1)} custom-call(bf16[128,32,128]{2,1,0:T(8,128)(2,1)S(1)} %all_to_all.20.slab_ref, f32[1280]{0:T(1024)} %gain_ref.3, bf16[1280,3840]{1,0:T(8,128)(2,1)} %weight_hbm.3), custom_call_target="tpu_custom_call" | custom-call | flops 4278190080 | bytes 11796480 | tf_op jit(solution)/shard_map/time_attend/pallas_call | solution.py:454
  127.8 24.1 %all_to_all.21.slab_ref = bf16[128,32,128]{2,1,0:T(8,128)(2,1)S(1)} all-to-all(bf16[128,32,128]{2,1,0:T(8,128)(2,1)} %time_attend.1), channel_id=1, replica_groups=mesh['frame'=128] {'frame'}, dimensions={0} | all-to-all | bytes 2097152 | tf_op jit(solution)/shard_map/all_to_all | solution.py:495
  151.9 1.4 unpack.1
Async XLA Ops:
  4.0 30.6 %all-to-all-start = ((bf16[128,32,128]{2,1,0:T(8,128)(2,1)}), bf16[128,32,128]{2,1,0:T(8,128)(2,1)S(1)}, u32[]{:S(2)}, u32[]{:S(2)}) async-start(bf16[128,32,128]{2,1,0:T(8,128)(2,1)} %get-tuple-element.12), calls=%async_computation | async-start | bytes 2097152 | tf_op jit(solution)/shard_map/all_to_all | solution.py:495
  37.3 35.1 %all-to-all-start.1 = ((bf16[128,2,32,128]{3,2,1,0:T(8,128)(2,1)}), bf16[128,2,32,128]{3,2,1,0:T(8,128)(2,1)S(1)}, u32[]{:S(2)}, u32[]{:S(2)}) async-start(bf16[128,2,32,128]{3,2,1,0:T(8,128)(2,1)} %choose.1), calls=%async_computation.1 | async-start | bytes 4194304 | tf_op jit(solution)/shard_map/all_to_all | solution.py:495

commit v3 on v2

--- a/solution.py
+++ b/solution.py
@@ -57,8 +57,8 @@
     return jnp.where(col == (row % 16) * 16 + row // 16, 1.0, 0.0).astype(bf16)
 
 
-def rows_to_slab(rows_ref, slab_ref, swap, spare=None):
-    for half in range(2):
+def rows_to_slab(tile, slab_ref, swap, spare=None, halves=(0, 1)):
+    for half in halves:
         for pair in range(4):
             sides = []
             for block in (2 * pair, 2 * pair + 1):
@@ -66,8 +66,7 @@
                 for unit in range(16 * half, 16 * half + 16):
                     k, g = divmod(unit, COLS)
                     if k < PARTS:
-                        at = k * FRAMES + 16 * block
-                        tiles.append(rows_ref[at : at + 16, g * LANES : (g + 1) * LANES])
+                        tiles.append(tile(k * FRAMES + 16 * block, g))
                     elif spare is None:
                         tiles.append(jnp.zeros((16, LANES), bf16))
                     else:
@@ -82,8 +81,12 @@
                 ].reshape(16, 16, LANES)
 
 
-def slab_to_rows(load, rows_ref, swap, first=0):
-    for block in range(8):
+def tiles_of(rows_ref):
+    return lambda at, g: rows_ref[at : at + 16, g * LANES : (g + 1) * LANES]
+
+
+def slab_to_rows(load, rows_ref, swap, first=0, blocks=range(8)):
+    for block in blocks:
         both = jnp.concatenate(
             [load(block, half).reshape(256, LANES) for half in range(2)], axis=1
         )
@@ -97,41 +100,76 @@
             ]
 
 
-def prep_kernel(pairs_ref, video_ref, gain_ref, normed_ref, slab_ref):
-    for k in range(PARTS):
-        rows = pl.ds(k * FRAMES, FRAMES)
-        normed_ref[rows, :] = norm_rows(video_ref[rows, :].astype(f32), gain_ref[...].reshape(1, WIDTH))
+def prep_kernel(
+    pairs_ref, video_hbm, gain_ref, slab_hbm, video_ref, normed_ref, slab_ref, sems, out_sems
+):
+    arriving = []
+    for part in range(2 * PARTS):
+        rows = pl.ds(part * 64, 64)
+        arriving.append(
+            pltpu.make_async_copy(video_hbm.at[rows], video_ref.at[rows], sems.at[part])
+        )
+        arriving[-1].start()
     spare = [
         jnp.full((16, LANES), pairs_ref[0, which], jnp.int32).astype(f32).astype(bf16)
         for which in range(2)
     ]
-    rows_to_slab(normed_ref, slab_ref, swap_matrix(), spare)
+    swap = swap_matrix()
+    gain = gain_ref[...].reshape(1, WIDTH)
+    leaving = []
+
+    def give(half):
+        rows_to_slab(tiles_of(normed_ref), slab_ref, swap, spare, halves=(half,))
+        some = pl.ds(16 * half, 16)
+        leaving.append(
+            pltpu.make_async_copy(slab_ref.at[:, some], slab_hbm.at[:, some], out_sems.at[half])
+        )
+        leaving[-1].start()
+
+    for part, copy in enumerate(arriving):
+        copy.wait()
+        rows = pl.ds(part * 64, 64)
+        normed_ref[rows, :] = norm_rows(video_ref[rows, :].astype(f32), gain)
+        if part == 3:
+            give(0)
+    give(1)
+    for copy in leaving:
+        copy.wait()
 
 
 def prep(pairs, video, gain):
     return pl.pallas_call(
         prep_kernel,
-        out_shape=(
-            pltpu.HBM((TOK, WIDTH), bf16),
-            pltpu.HBM((FRAMES, SLAB, LANES), bf16),
-        ),
-        in_specs=[SMALL, WHOLE, WHOLE],
-        out_specs=(WHOLE, WHOLE),
-        compiler_params=params(VMEM),
-        cost_estimate=cost(6 * TOK * WIDTH, 6 * TOK * WIDTH),
+        out_shape=pltpu.HBM((FRAMES, SLAB, LANES), bf16),
+        in_specs=[SMALL, THERE, WHOLE],
+        out_specs=THERE,
+        scratch_shapes=[
+            pltpu.VMEM((TOK, WIDTH), bf16),
+            pltpu.VMEM((TOK, WIDTH), bf16),
+            pltpu.VMEM((FRAMES, SLAB, LANES), bf16),
+            pltpu.SemaphoreType.DMA((2 * PARTS,)),
+            pltpu.SemaphoreType.DMA((2,)),
+        ],
+        compiler_params=params(VMEM),
+        cost_estimate=cost(6 * TOK * WIDTH, 4 * TOK * WIDTH),
         name="prep",
     )(in_hbm(pairs), in_hbm(video), in_hbm(gain))
 
 
-def project_kernel(rows_ref, wq_ref, wk_ref, wv_ref, q_ref, k_ref, v_ref):
-    rows = rows_ref[...]
+def project_kernel(video_ref, gain_ref, wq_ref, wk_ref, wv_ref, q_ref, k_ref, v_ref, normed_ref):
+    @pl.when(pl.program_id(0) == 0)
+    def _():
+        gain = gain_ref[...].reshape(1, WIDTH)
+        normed_ref[...] = norm_rows(video_ref[...].astype(f32), gain)
+
+    rows = normed_ref[...]
     queries = jnp.dot(rows, wq_ref[...], preferred_element_type=f32) * SCALE
     q_ref[...] = queries.astype(bf16)
     k_ref[...] = jnp.dot(rows, wk_ref[...], preferred_element_type=f32).astype(bf16)
     v_ref[...] = jnp.dot(rows, wv_ref[...], preferred_element_type=f32).astype(bf16)
 
 
-def project(rows, weight):
+def project(video, gain, weight):
     out = pltpu.HBM((TOK, WIDTH), bf16)
     out_spec = pl.BlockSpec((TOK, GROUP), lambda i: (0, i))
     return pl.pallas_call(
@@ -139,16 +177,18 @@
         grid=(GROUPS,),
         out_shape=(out, out, out),
         in_specs=[
+            WHOLE,
             WHOLE,
             pl.BlockSpec((WIDTH, GROUP), lambda i: (0, i)),
             pl.BlockSpec((WIDTH, GROUP), lambda i: (0, GROUPS + i)),
             pl.BlockSpec((WIDTH, GROUP), lambda i: (0, 2 * GROUPS + i)),
         ],
         out_specs=(out_spec, out_spec, out_spec),
+        scratch_shapes=[pltpu.VMEM((TOK, WIDTH), bf16)],
         compiler_params=params(VMEM),
         cost_estimate=cost(6 * TOK * WIDTH * WIDTH, 6 * WIDTH * WIDTH + 8 * TOK * WIDTH),
         name="project",
-    )(in_hbm(rows), in_hbm(weight), in_hbm(weight), in_hbm(weight))
+    )(in_hbm(video), in_hbm(gain), in_hbm(weight), in_hbm(weight), in_hbm(weight))
 
 
 def low_lanes(rows):
@@ -215,8 +255,9 @@
     )(in_hbm(queries), in_hbm(keys), in_hbm(values))
 
 
-def choose_kernel(key_list_ref, slab_ref, after_ref, out_ref):
+def choose_kernel(key_list_ref, slab_ref, after_ref, out_hbm, out_ref, sems):
     del after_ref
+    copies = []
     halves = [
         jnp.concatenate([slab_ref[key_list_ref[s], at : at + 16, :] for s in range(KEYS)], axis=0)
         for at in (0, 16)
@@ -236,18 +277,30 @@
         chosen = chosen.astype(bf16).reshape(8, 2, 16, 2 * LANES)
         out_ref[f : f + 8, :, 0:16, :] = chosen[..., :LANES]
         out_ref[f : f + 8, :, 16:32, :] = chosen[..., LANES:]
+        if (f + 8) % 32 == 0:
+            some = pl.ds(f - 24, 32)
+            copies.append(
+                pltpu.make_async_copy(out_ref.at[some], out_hbm.at[some], sems.at[len(copies)])
+            )
+            copies[-1].start()
+    for copy in copies:
+        copy.wait()
 
 
 def choose(key_list, slab, after):
     return pl.pallas_call(
         choose_kernel,
-        out_shape=jax.ShapeDtypeStruct((FRAMES, 2, SLAB, LANES), bf16),
+        out_shape=pltpu.HBM((FRAMES, 2, SLAB, LANES), bf16),
         in_specs=[SMALL, WHOLE, THERE],
-        out_specs=WHOLE,
+        out_specs=THERE,
+        scratch_shapes=[
+            pltpu.VMEM((FRAMES, 2, SLAB, LANES), bf16),
+            pltpu.SemaphoreType.DMA((4,)),
+        ],
         compiler_params=params(VMEM),
         cost_estimate=cost(4 * FRAMES * SLAB * LANES * 256, 6 * FRAMES * SLAB * LANES),
         name="choose",
-    )(in_hbm(key_list), in_vmem(slab), in_hbm(after))
+    )(key_list, in_vmem(slab), in_hbm(after))
 
 
 LARGE = 1e30
@@ -255,9 +308,9 @@
 
 def attend_kernel(
     slab_ref, q_hbm, mixed_hbm, total_hbm, top_hbm, weight_hbm, wo_hbm, video_hbm,
-    spatial_ref, out_slab_ref,
-    rows_ref, heads_ref, most_ref, q_ref, mixed_ref, total_ref, top_ref, wk_ref, wv_ref,
-    wo_ref, video_ref, sems, last_sems,
+    spatial_hbm, out_slab_hbm,
+    spatial_ref, out_slab_ref, rows_ref, heads_ref, most_ref, q_ref, mixed_ref, total_ref, top_ref, wk_ref, wv_ref,
+    wo_ref, video_ref, sems, last_sems, out_sems,
 ):
     def copies(group):
         pairs = (
@@ -300,11 +353,14 @@
 
     @pl.loop(0, GROUPS)
     def _(group):
-        for copy in copies(group):
+        arriving = copies(group)
+        for copy in arriving[:2]:
             copy.wait()
         keys, values = project_group(group)
+        for copy in arriving[2:]:
+            copy.wait()
         low_q, low_v = low_lanes(TOK), low_lanes(2 * TOK)
-        outs = []
+        pending = []
         for pair in range(2):
             lanes = slice(pair * LANES, (pair + 1) * LANES)
             queries = q_ref[group, :, lanes].astype(f32)
@@ -323,8 +379,9 @@
                     preferred_element_type=f32,
                 )
                 tops = jnp.concatenate([wide] * (2 * TOK // LANES), axis=1)
-                weights = jnp.exp2(scores - tops).astype(bf16)
-                outs.append(jnp.dot(weights, padded.astype(bf16), preferred_element_type=f32))
+                pending.append((scores, tops, padded.astype(bf16)))
+        pending = [(jnp.exp2(s - tops).astype(bf16), padded) for s, tops, padded in pending]
+        outs = [jnp.dot(w, padded, preferred_element_type=f32) for w, padded in pending]
         for pair in range(2):
             lanes = slice(pair * LANES, (pair + 1) * LANES)
             one, two = outs[2 * pair], outs[2 * pair + 1]
@@ -351,6 +408,12 @@
                 total = total + total_ref[group, :, lanes] * less
                 heads_ref[2 * group + pair] = (mixed / total).astype(bf16)
 
+    given = []
+
+    def give(source, target):
+        given.append(pltpu.make_async_copy(source, target, out_sems.at[len(given)]))
+        given[-1].start()
+
     for copy in last:
         copy.wait()
     for k in range(PARTS):
@@ -358,7 +421,14 @@
         heads = jnp.concatenate([heads_ref[c, rows, :] for c in range(COLS)], axis=1)
         added = jnp.dot(heads, wo_ref[...], preferred_element_type=f32)
         spatial_ref[rows, :] = (video_ref[rows, :].astype(f32) + added).astype(bf16)
-    rows_to_slab(spatial_ref, out_slab_ref, swap)
+        give(spatial_ref.at[rows], spatial_hbm.at[rows])
+        if k == 1:
+            rows_to_slab(tiles_of(spatial_ref), out_slab_ref, swap, halves=(0,))
+            give(out_slab_ref.at[:, pl.ds(0, 16)], out_slab_hbm.at[:, pl.ds(0, 16)])
+    rows_to_slab(tiles_of(spatial_ref), out_slab_ref, swap, halves=(1,))
+    give(out_slab_ref.at[:, pl.ds(16, 16)], out_slab_hbm.at[:, pl.ds(16, 16)])
+    for copy in given:
+        copy.wait()
 
 
 def attend(slab, queries, mixed, total, top, weight, out_weight, video):
@@ -366,11 +436,13 @@
         attend_kernel,
         out_shape=(
             jax.ShapeDtypeStruct((TOK, WIDTH), bf16),
-            jax.ShapeDtypeStruct((FRAMES, SLAB, LANES), bf16),
+            pltpu.HBM((FRAMES, SLAB, LANES), bf16),
         ),
         in_specs=[WHOLE] + [THERE] * 7,
-        out_specs=(WHOLE, WHOLE),
+        out_specs=(THERE, THERE),
         scratch_shapes=[
+            pltpu.VMEM((TOK, WIDTH), bf16),
+            pltpu.VMEM((FRAMES, SLAB, LANES), bf16),
             pltpu.VMEM((2 * TOK, WIDTH), bf16),
             pltpu.VMEM((COLS, TOK, LANES), bf16),
             pltpu.VMEM((8, LANES), f32),
@@ -384,6 +456,7 @@
             pltpu.VMEM((TOK, WIDTH), bf16),
             pltpu.SemaphoreType.DMA((6, GROUPS)),
             pltpu.SemaphoreType.DMA((2,)),
+            pltpu.SemaphoreType.DMA((PARTS + 2,)),
         ],
         compiler_params=params(VMEM),
         cost_estimate=cost(
@@ -443,11 +516,7 @@
         for (pair, at), (mixed, total, _) in zip(places, attend_pairs(units)):
             heads_ref[2 * group + pair, at, :] = (mixed / total).astype(bf16)
 
-    for k in range(PARTS):
-        at = slice(k * FRAMES, (k + 1) * FRAMES)
-        for g in range(COLS):
-            rows_ref[at, g * LANES : (g + 1) * LANES] = heads_ref[g, at, :]
-    rows_to_slab(rows_ref, out_slab_ref, swap)
+    rows_to_slab(lambda at, g: heads_ref[g, at : at + 16, :], out_slab_ref, swap)
 
 
 def time_attend(slab, gain, weight):
@@ -469,14 +538,27 @@
             HEADS * TOK * FRAMES,
         ),
         name="time_attend",
-    )(in_vmem(slab), in_hbm(gain), in_hbm(weight))
-
-
-def unpack_kernel(slab_ref, out_ref):
-    slab_to_rows(
-        lambda block, half: slab_ref[16 * block : 16 * block + 16, 16 * half : 16 * half + 16, :],
-        out_ref, swap_matrix(),
-    )
+    )(in_vmem(slab), gain, in_hbm(weight))
+
+
+def unpack_kernel(slab_ref, out_hbm, out_ref, sems):
+    swap = swap_matrix()
+    copies = []
+    for part in range(4):
+        slab_to_rows(
+            lambda block, half: slab_ref[
+                16 * block : 16 * block + 16, 16 * half : 16 * half + 16, :
+            ],
+            out_ref, swap, blocks=(2 * part, 2 * part + 1),
+        )
+        for k in range(PARTS):
+            some = pl.ds(k * FRAMES + 32 * part, 32)
+            copies.append(
+                pltpu.make_async_copy(out_ref.at[some], out_hbm.at[some], sems.at[len(copies)])
+            )
+            copies[-1].start()
+    for copy in copies:
+        copy.wait()
 
 
 def unpack(slab):
@@ -484,7 +566,8 @@
         unpack_kernel,
         out_shape=jax.ShapeDtypeStruct((TOK, WIDTH), bf16),
         in_specs=[WHOLE],
-        out_specs=WHOLE,
+        out_specs=THERE,
+        scratch_shapes=[pltpu.VMEM((TOK, WIDTH), bf16), pltpu.SemaphoreType.DMA((4 * PARTS,))],
         compiler_params=params(VMEM),
         cost_estimate=cost(2 * TOK * WIDTH * 256, 4 * TOK * WIDTH),
         name="unpack",
@@ -496,9 +579,8 @@
 
 
 def body(video, key_list, pairs, norm_gain, qkv_weight, out_weight, time_gain, time_weight):
-    normed, slab = prep(pairs, video, norm_gain)
-    spread = exchange(slab)
-    queries, keys, values = project(normed, qkv_weight)
+    spread = exchange(prep(pairs, video, norm_gain))
+    queries, keys, values = project(video, norm_gain, qkv_weight)
     wanted = exchange(choose(key_list, spread, queries))
     mixed, total, top = own_attend(queries, keys, values)
     spatial, slab = attend(wanted, queries, mixed, total, top, qkv_weight, out_weight, video)

time: 154 us -> 153 us (level)
  no operation moved by 1% of the time
where the time goes in v3:
time: 153 us; the launch traced here: 152 us
  Pallas kernels  56.4 us (37%)
  blocking collectives  48 us (31%)
  waiting for transfers between devices  30.8 us (20%)
  starting transfers between devices  16.2 us (11%)
    all_to_all x2, blocking collectives, exchange(): lax.all_to_all(slab, 'frame', split_axis=0, concat_axis=0, tiled=True)  48 us
    all_to_all x2, waiting for transfers between devices, exchange(): lax.all_to_all(slab, 'frame', split_axis=0, concat_axis=0, tiled=True)  30.8 us
    pallas_call x1, Pallas kernels, attend(): pl.pallas_call(attend_kernel, out_shape=(jax.ShapeDtypeStruct((TOK, WIDTH...  18.8 us
    all_to_all x2, starting transfers between devices, exchange(): lax.all_to_all(slab, 'frame', split_axis=0, concat_axis=0, tiled=True)  16.2 us
    pallas_call x1, Pallas kernels, time_attend(): pl.pallas_call(time_kernel, out_shape=jax.ShapeDtypeStruct((FRAMES, SLAB,...  11 us
    pallas_call x1, Pallas kernels, project(): pl.pallas_call(project_kernel, grid=(GROUPS,), out_shape=(out, out, out),...  9.79 us
    pallas_call x1, Pallas kernels, own_attend(): pl.pallas_call(own_kernel, out_shape=(out, out, out), in_specs=[WHOLE, WH...  8.97 us
    pallas_call x1, Pallas kernels, prep(): pl.pallas_call(prep_kernel, out_shape=pltpu.HBM((FRAMES, SLAB, LANES), bf...  4.35 us
  transfers between devices with their start and end apart: 2, of which 2 were waited for; matrix products, arithmetic and copies ran while one was open for 0% of the time, Pallas kernels for 12%

profile of v3, /device:TPU:1, one launch (start us, length us, event | category | flops | bytes accessed | tf_op | source)
XLA Modules:
  0.0 152.2 jit_solution(10345738517729578541)
XLA Ops:
  0.6 4.4 %prep.1 = bf16[128,32,128]{2,1,0:T(8,128)(2,1)} custom-call(s32[1,2]{1,0:T(1,128)} %pairs_ref.1, bf16[384,1280]{1,0:T(8,128)(2,1)} %video_hbm.3, f32[1280]{0:T(1024)} %gain_ref.4), custom_call_target="tpu_custom_call" | custom-call | flops 2949120 | bytes 1966080 | tf_op jit(solution)/shard_map/prep/pallas_call | solution.py:141
  5.0 11.5 %all-to-all-start = ((bf16[128,32,128]{2,1,0:T(8,128)(2,1)}), bf16[128,32,128]{2,1,0:T(8,128)(2,1)S(1)}, u32[]{:S(2)}, u32[]{:S(2)}) async-start(bf16[128,32,128]{2,1,0:T(8,128)(2,1)} %prep.1), calls=%async_computation | async-start | bytes 2097152 | tf_op jit(solution)/shard_map/all_to_all | solution.py:578
  16.5 0.0 copy-start
  16.5 9.8 %project.1 = (bf16[384,1280]{1,0:T(8,128)(2,1)}, bf16[384,1280]{1,0:T(8,128)(2,1)}, bf16[384,1280]{1,0:T(8,128)(2,1)}) custom-call(bf16[384,1280]{1,0:T(8,128)(2,1)} %video_hbm.3, f32[1280]{0:T(1024)} %gain_ref.4, bf16[1280,3840]{1,0:T(8,128)(2,1)} %weight_hbm.2, bf16[1280,3840]{1,0:T(8,128)(2,1)} %weight_hbm.2, bf16[1280,3840]{1,0:T(8,128)(2,1)} %weight_hbm.2), custom_call_target="tpu_custom_call" | custom-call | flops 3774873600 | bytes 13762560 | tf_op jit(solution)/shard_map/project/pallas_call | solution.py:175
  26.3 9.3 %all-to-all-done.slab_ref = bf16[128,32,128]{2,1,0:T(8,128)(2,1)S(1)} async-done(((bf16[128,32,128]{2,1,0:T(8,128)(2,1)}), bf16[128,32,128]{2,1,0:T(8,128)(2,1)S(1)}, u32[]{:S(2)}, u32[]{:S(2)}) %all-to-all-start) | async-done | bytes 1048608 | tf_op jit(solution)/shard_map/all_to_all | solution.py:578
  35.6 0.0 copy-done
  35.6 2.2 %choose.1 = bf16[128,2,32,128]{3,2,1,0:T(8,128)(2,1)} custom-call(s32[8]{0:T(128)S(1)} %copy-done, bf16[128,32,128]{2,1,0:T(8,128)(2,1)S(1)} %all-to-all-done.slab_ref, bf16[384,1280]{1,0:T(8,128)(2,1)} %get-tuple-element.10.after_ref.q_ref.q_hbm), custom_call_target="tpu_custom_call" | custom-call | flops 536870912 | bytes 3145728 | tf_op jit(solution)/shard_map/choose/pallas_call | solution.py:291
  37.8 4.7 %all-to-all-start.1 = ((bf16[128,2,32,128]{3,2,1,0:T(8,128)(2,1)}), bf16[128,2,32,128]{3,2,1,0:T(8,128)(2,1)S(1)}, u32[]{:S(2)}, u32[]{:S(2)}) async-start(bf16[128,2,32,128]{3,2,1,0:T(8,128)(2,1)} %choose.1), calls=%async_computation.1 | async-start | bytes 4194304 | tf_op jit(solution)/shard_map/all_to_all | solution.py:578
  42.5 9.0 %own_attend.1 = (f32[384,1280]{1,0:T(8,128)}, f32[384,1280]{1,0:T(8,128)}, f32[384,1280]{1,0:T(8,128)}) custom-call(bf16[384,1280]{1,0:T(8,128)(2,1)} %get-tuple-element.10.after_ref.q_ref.q_hbm, bf16[384,1280]{1,0:T(8,128)(2,1)} %get-tuple-element.11.k_ref, bf16[384,1280]{1,0:T(8,128)(2,1)} %get-tuple-element.12.v_ref), custom_call_target="tpu_custom_call" | custom-call | flops 1509949440 | bytes 14745600 | tf_op jit(solution)/shard_map/own_attend/pallas_call | solution.py:247
  51.5 21.5 %all-to-all-done.1.slab_ref = bf16[128,2,32,128]{3,2,1,0:T(8,128)(2,1)S(1)} async-done(((bf16[128,2,32,128]{3,2,1,0:T(8,128)(2,1)}), bf16[128,2,32,128]{3,2,1,0:T(8,128)(2,1)S(1)}, u32[]{:S(2)}, u32[]{:S(2)}) %all-to-all-start.1) | async-done | bytes 2097184 | tf_op jit(solution)/shard_map/all_to_all | solution.py:578
  73.0 18.8 %attend.1 = (bf16[384,1280]{1,0:T(8,128)(2,1)}, bf16[128,32,128]{2,1,0:T(8,128)(2,1)}) custom-call(bf16[128,2,32,128]{3,2,1,0:T(8,128)(2,1)S(1)} %all-to-all-done.1.slab_ref, bf16[384,1280]{1,0:T(8,128)(2,1)} %get-tuple-element.10.after_ref.q_ref.q_hbm, f32[384,1280]{1,0:T(8,128)} %get-tuple-element.13.mixed_hbm, f32[384,1280]{1,0:T(8,128)} %get-tuple-element.14.total_hbm, ...), custom_call_target="tpu_custom_call" | custom-call | flops 8053063680 | bytes 19660800 | tf_op jit(solution)/shard_map/attend/pallas_call | solution.py:435
  91.7 0.0 copy-start.1
  91.7 24.0 %all_to_all.20.slab_ref = bf16[128,32,128]{2,1,0:T(8,128)(2,1)S(1)} all-to-all(bf16[128,32,128]{2,1,0:T(8,128)(2,1)} %get-tuple-element.17), channel_id=1, replica_groups=mesh['frame'=128] {'frame'}, dimensions={0} | all-to-all | bytes 2097152 | tf_op jit(solution)/shard_map/all_to_all | solution.py:578
  115.7 0.0 copy-done.1
  115.7 11.0 %time_attend.1 = bf16[128,32,128]{2,1,0:T(8,128)(2,1)} custom-call(bf16[128,32,128]{2,1,0:T(8,128)(2,1)S(1)} %all_to_all.20.slab_ref, f32[1280]{0:T(1024)S(1)} %copy-done.1, bf16[1280,3840]{1,0:T(8,128)(2,1)} %weight_hbm.3), custom_call_target="tpu_custom_call" | custom-call | flops 4278190080 | bytes 11796480 | tf_op jit(solution)/shard_map/time_attend/pallas_call | solution.py:523
  126.8 24.0 %all_to_all.21.slab_ref = bf16[128,32,128]{2,1,0:T(8,128)(2,1)S(1)} all-to-all(bf16[128,32,128]{2,1,0:T(8,128)(2,1)} %time_attend.1), channel_id=1, replica_groups=mesh['frame'=128] {'frame'}, dimensions={0} | all-to-all | bytes 2097152 | tf_op jit(solution)/shard_map/all_to_all | solution.py:578
  150.8 1.3 unpack.1
Async XLA Ops:
  5.0 30.6 %all-to-all-start = ((bf16[128,32,128]{2,1,0:T(8,128)(2,1)}), bf16[128,32,128]{2,1,0:T(8,128)(2,1)S(1)}, u32[]{:S(2)}, u32[]{:S(2)}) async-start(bf16[128,32,128]{2,1,0:T(8,128)(2,1)} %prep.1), calls=%async_computation | async-start | bytes 2097152 | tf_op jit(solution)/shard_map/all_to_all | solution.py:578
  16.5 19.1 %copy-start = (s32[8]{0:T(128)S(1)}, s32[8]{0:T(128)}, u32[]{:S(2)}) copy-start(s32[8]{0:T(128)} %key_list_ref.1) | copy-start | bytes 100
  37.8 35.2 %all-to-all-start.1 = ((bf16[128,2,32,128]{3,2,1,0:T(8,128)(2,1)}), bf16[128,2,32,128]{3,2,1,0:T(8,128)(2,1)S(1)}, u32[]{:S(2)}, u32[]{:S(2)}) async-start(bf16[128,2,32,128]{3,2,1,0:T(8,128)(2,1)} %choose.1), calls=%async_computation.1 | async-start | bytes 4194304 | tf_op jit(solution)/shard_map/all_to_all | solution.py:578
  91.7 24.0 %copy-start.1 = (f32[1280]{0:T(1024)S(1)}, f32[1280]{0:T(1024)}, u32[]{:S(2)}) copy-start(f32[1280]{0:T(1024)} %gain_ref.5) | copy-start | bytes 15364

commit v4 on v3

--- a/solution.py
+++ b/solution.py
@@ -101,24 +101,25 @@
 
 
 def prep_kernel(
-    pairs_ref, video_hbm, gain_ref, slab_hbm, video_ref, normed_ref, slab_ref, sems, out_sems
+    pairs_hbm, video_hbm, gain_hbm, slab_hbm,
+    pairs_ref, video_ref, gain_ref, normed_ref, slab_ref, sems, out_sems,
 ):
+    small = (
+        pltpu.make_async_copy(gain_hbm, gain_ref, sems.at[PARTS]),
+        pltpu.make_async_copy(pairs_hbm, pairs_ref, sems.at[PARTS + 1]),
+    )
     arriving = []
-    for part in range(2 * PARTS):
-        rows = pl.ds(part * 64, 64)
+    for part in range(PARTS):
+        rows = pl.ds(part * FRAMES, FRAMES)
         arriving.append(
             pltpu.make_async_copy(video_hbm.at[rows], video_ref.at[rows], sems.at[part])
         )
-        arriving[-1].start()
-    spare = [
-        jnp.full((16, LANES), pairs_ref[0, which], jnp.int32).astype(f32).astype(bf16)
-        for which in range(2)
-    ]
+    for copy in (small[0], arriving[0], small[1], *arriving[1:]):
+        copy.start()
     swap = swap_matrix()
-    gain = gain_ref[...].reshape(1, WIDTH)
     leaving = []
 
-    def give(half):
+    def give(half, spare=None):
         rows_to_slab(tiles_of(normed_ref), slab_ref, swap, spare, halves=(half,))
         some = pl.ds(16 * half, 16)
         leaving.append(
@@ -126,13 +127,20 @@
         )
         leaving[-1].start()
 
+    small[0].wait()
+    gain = gain_ref[...].reshape(1, WIDTH)
     for part, copy in enumerate(arriving):
         copy.wait()
-        rows = pl.ds(part * 64, 64)
+        rows = pl.ds(part * FRAMES, FRAMES)
         normed_ref[rows, :] = norm_rows(video_ref[rows, :].astype(f32), gain)
-        if part == 3:
+        if part == 1:
             give(0)
-    give(1)
+    small[1].wait()
+    spare = [
+        jnp.full((16, LANES), pairs_ref[0, which], jnp.int32).astype(f32).astype(bf16)
+        for which in range(2)
+    ]
+    give(1, spare)
     for copy in leaving:
         copy.wait()
 
@@ -141,13 +149,15 @@
     return pl.pallas_call(
         prep_kernel,
         out_shape=pltpu.HBM((FRAMES, SLAB, LANES), bf16),
-        in_specs=[SMALL, THERE, WHOLE],
+        in_specs=[THERE, THERE, THERE],
         out_specs=THERE,
         scratch_shapes=[
+            pltpu.SMEM((1, 2), jnp.int32),
             pltpu.VMEM((TOK, WIDTH), bf16),
+            pltpu.VMEM((WIDTH,), f32),
             pltpu.VMEM((TOK, WIDTH), bf16),
             pltpu.VMEM((FRAMES, SLAB, LANES), bf16),
-            pltpu.SemaphoreType.DMA((2 * PARTS,)),
+            pltpu.SemaphoreType.DMA((PARTS + 2,)),
             pltpu.SemaphoreType.DMA((2,)),
         ],
         compiler_params=params(VMEM),
@@ -230,27 +240,47 @@
     return pl.ds(pl.multiple_of(offset + group * GROUP, LANES), size)
 
 
-def own_kernel(q_ref, k_ref, v_ref, mixed_ref, total_ref, top_ref):
+def flipped_scores(queries, keys, head):
+    low = low_lanes(queries.shape[0])
+    wide = queries.astype(f32)
+    mine = jnp.where(low, wide, 0.0) if head == 0 else jnp.where(low, 0.0, wide)
+    return lax.dot_general(
+        keys, mine.astype(bf16), (((1,), (1,)), ((), ())), preferred_element_type=f32
+    )
+
+
+def with_ones(values):
+    return jnp.concatenate([values, jnp.ones((16, values.shape[1]), bf16)], axis=0)
+
+
+def own_kernel(q_ref, k_ref, v_ref, mixed_ref, stat_ref):
     @pl.loop(0, GROUPS)
     def _(group):
-        places = [group_lanes(group, LANES, pair * LANES) for pair in range(2)]
-        units = [(q_ref[:, at], k_ref[:, at], v_ref[:, at].astype(f32), None) for at in places]
-        low = low_lanes(TOK)
-        for at, (mixed, total, tops) in zip(places, attend_pairs(units)):
-            mixed_ref[:, at] = mixed
-            total_ref[:, at] = total
-            top_ref[:, at] = jnp.where(low, tops[0], tops[1])
+        at = group_lanes(group, GROUP)
+        queries, keys = q_ref[:, at], k_ref[:, at]
+        values = v_ref[:, at].T
+        scores = []
+        for head in range(4):
+            lanes = slice(head // 2 * LANES, (head // 2 + 1) * LANES)
+            scores.append(flipped_scores(queries[:, lanes], keys[:, lanes], head % 2))
+        tops = [jnp.max(s, axis=0, keepdims=True) for s in scores]
+        weights = [jnp.exp2(s - top).astype(bf16) for s, top in zip(scores, tops)]
+        for head in range(4):
+            rows = slice(head * HEAD, (head + 1) * HEAD)
+            out = jnp.dot(with_ones(values[rows]), weights[head], preferred_element_type=f32)
+            mixed_ref[group, rows, :] = out[:HEAD]
+            stat_ref[group, head : head + 1, :] = tops[head]
+            stat_ref[group, 4 + head : 5 + head, :] = out[HEAD : HEAD + 1]
 
 
 def own_attend(queries, keys, values):
-    out = pltpu.HBM((TOK, WIDTH), f32)
     return pl.pallas_call(
         own_kernel,
-        out_shape=(out, out, out),
+        out_shape=(pltpu.HBM((GROUPS, GROUP, TOK), f32), pltpu.HBM((GROUPS, 8, TOK), f32)),
         in_specs=[WHOLE, WHOLE, WHOLE],
-        out_specs=(WHOLE, WHOLE, WHOLE),
+        out_specs=(WHOLE, WHOLE),
         compiler_params=params(VMEM),
-        cost_estimate=cost(8 * TOK * TOK * WIDTH, 30 * TOK * WIDTH, HEADS * TOK * TOK),
+        cost_estimate=cost(8 * TOK * TOK * WIDTH, 10 * TOK * WIDTH, HEADS * TOK * TOK),
         name="own_attend",
     )(in_hbm(queries), in_hbm(keys), in_hbm(values))
 
@@ -307,19 +337,18 @@
 
 
 def attend_kernel(
-    slab_ref, q_hbm, mixed_hbm, total_hbm, top_hbm, weight_hbm, wo_hbm, video_hbm,
+    slab_ref, q_hbm, mixed_hbm, stat_hbm, weight_hbm, wo_hbm, video_hbm,
     spatial_hbm, out_slab_hbm,
-    spatial_ref, out_slab_ref, rows_ref, heads_ref, most_ref, q_ref, mixed_ref, total_ref, top_ref, wk_ref, wv_ref,
-    wo_ref, video_ref, sems, last_sems, out_sems,
+    spatial_ref, out_slab_ref, rows_ref, heads_ref, most_ref, q_ref, mixed_ref, stat_ref,
+    wk_ref, wv_ref, wo_ref, video_ref, sems, last_sems, out_sems,
 ):
     def copies(group):
         pairs = (
             (weight_hbm.at[:, group_lanes(group, GROUP, WIDTH)], wk_ref),
             (weight_hbm.at[:, group_lanes(group, GROUP, 2 * WIDTH)], wv_ref),
             (q_hbm.at[:, group_lanes(group, GROUP)], q_ref),
-            (top_hbm.at[:, group_lanes(group, GROUP)], top_ref),
-            (mixed_hbm.at[:, group_lanes(group, GROUP)], mixed_ref),
-            (total_hbm.at[:, group_lanes(group, GROUP)], total_ref),
+            (mixed_hbm.at[group], mixed_ref),
+            (stat_hbm.at[group], stat_ref),
         )
         return [
             pltpu.make_async_copy(source, target.at[group], sems.at[i, group])
@@ -349,7 +378,29 @@
     def project_group(group):
         rows = rows_ref[...]
         keys = jnp.dot(rows, wk_ref[group], preferred_element_type=f32).astype(bf16)
-        return keys, jnp.dot(rows, wv_ref[group], preferred_element_type=f32)
+        values = jnp.dot(rows, wv_ref[group], preferred_element_type=f32).astype(bf16)
+        return keys, values.T
+
+    def score_group(group, keys):
+        scores = []
+        for head in range(4):
+            lanes = slice(head // 2 * LANES, (head // 2 + 1) * LANES)
+            scores.append(flipped_scores(q_ref[group, :, lanes], keys[:, lanes], head % 2))
+        return scores
+
+    def mix_group(group, weights, values, less):
+        made, totals = [], []
+        for head in range(4):
+            rows = slice(head * HEAD, (head + 1) * HEAD)
+            out = jnp.dot(with_ones(values[rows]), weights[head], preferred_element_type=f32)
+            mixed, total = mixed_ref[group, rows, :], stat_ref[group, 4 + head : 5 + head, :]
+            if less is not None:
+                mixed, total = mixed * less[head], total * less[head]
+            mixed, total = mixed + out[:HEAD], total + out[HEAD : HEAD + 1]
+            made.append((mixed / total).astype(bf16))
+            totals.append(total)
+        heads_ref[group] = jnp.concatenate(made, axis=0).T
+        return totals
 
     @pl.loop(0, GROUPS)
     def _(group):
@@ -359,54 +410,26 @@
         keys, values = project_group(group)
         for copy in arriving[2:]:
             copy.wait()
-        low_q, low_v = low_lanes(TOK), low_lanes(2 * TOK)
-        pending = []
-        for pair in range(2):
-            lanes = slice(pair * LANES, (pair + 1) * LANES)
-            queries = q_ref[group, :, lanes].astype(f32)
-            some = values[:, lanes]
-            top = top_ref[group, :, lanes]
-            other = pltpu.roll(top, HEAD, 1)
-            for head in range(2):
-                if head == 0:
-                    mine, padded = jnp.where(low_q, queries, 0.0), jnp.where(low_v, some, 1.0)
-                    wide = jnp.where(low_q, top, other)
-                else:
-                    mine, padded = jnp.where(low_q, 0.0, queries), jnp.where(low_v, 1.0, some)
-                    wide = jnp.where(low_q, other, top)
-                scores = lax.dot_general(
-                    mine.astype(bf16), keys[:, lanes], (((1,), (1,)), ((), ())),
-                    preferred_element_type=f32,
-                )
-                tops = jnp.concatenate([wide] * (2 * TOK // LANES), axis=1)
-                pending.append((scores, tops, padded.astype(bf16)))
-        pending = [(jnp.exp2(s - tops).astype(bf16), padded) for s, tops, padded in pending]
-        outs = [jnp.dot(w, padded, preferred_element_type=f32) for w, padded in pending]
-        for pair in range(2):
-            lanes = slice(pair * LANES, (pair + 1) * LANES)
-            one, two = outs[2 * pair], outs[2 * pair + 1]
-            mixed = jnp.where(low_q, one, two) + mixed_ref[group, :, lanes]
-            total = jnp.where(low_q, two, one)
-            total = pltpu.roll(total, HEAD, 1) + total_ref[group, :, lanes]
-            heads_ref[2 * group + pair] = (mixed / total).astype(bf16)
-            most = jnp.max(total.reshape(TOK // 8, 8, LANES), axis=0)
-            most_ref[...] = jnp.maximum(most_ref[...], most)
+        scores = score_group(group, keys)
+        weights = [
+            jnp.exp2(scores[head] - stat_ref[group, head : head + 1, :]).astype(bf16)
+            for head in range(4)
+        ]
+        for total in mix_group(group, weights, values, None):
+            most_ref[...] = jnp.maximum(most_ref[...], total)
 
     @pl.when(jnp.logical_not(jnp.max(most_ref[...]) < LARGE))
     def _():
         @pl.loop(0, GROUPS)
         def _(group):
             keys, values = project_group(group)
-            for pair in range(2):
-                lanes = slice(pair * LANES, (pair + 1) * LANES)
-                top = top_ref[group, :, lanes]
-                ((mixed, total, tops),) = attend_pairs(
-                    [(q_ref[group, :, lanes], keys[:, lanes], values[:, lanes], top)]
-                )
-                less = jnp.exp2(top - jnp.where(low_lanes(TOK), tops[0], tops[1]))
-                mixed = mixed + mixed_ref[group, :, lanes] * less
-                total = total + total_ref[group, :, lanes] * less
-                heads_ref[2 * group + pair] = (mixed / total).astype(bf16)
+            scores = score_group(group, keys)
+            own = [stat_ref[group, head : head + 1, :] for head in range(4)]
+            tops = [
+                jnp.maximum(top, jnp.max(s, axis=0, keepdims=True)) for s, top in zip(scores, own)
+            ]
+            weights = [jnp.exp2(s - top).astype(bf16) for s, top in zip(scores, tops)]
+            mix_group(group, weights, values, [jnp.exp2(o - top) for o, top in zip(own, tops)])
 
     given = []
 
@@ -418,7 +441,7 @@
         copy.wait()
     for k in range(PARTS):
         rows = pl.ds(k * FRAMES, FRAMES)
-        heads = jnp.concatenate([heads_ref[c, rows, :] for c in range(COLS)], axis=1)
+        heads = jnp.concatenate([heads_ref[g, rows, :] for g in range(GROUPS)], axis=1)
         added = jnp.dot(heads, wo_ref[...], preferred_element_type=f32)
         spatial_ref[rows, :] = (video_ref[rows, :].astype(f32) + added).astype(bf16)
         give(spatial_ref.at[rows], spatial_hbm.at[rows])
@@ -431,30 +454,29 @@
         copy.wait()
 
 
-def attend(slab, queries, mixed, total, top, weight, out_weight, video):
+def attend(slab, queries, mixed, stat, weight, out_weight, video):
     return pl.pallas_call(
         attend_kernel,
         out_shape=(
             jax.ShapeDtypeStruct((TOK, WIDTH), bf16),
             pltpu.HBM((FRAMES, SLAB, LANES), bf16),
         ),
-        in_specs=[WHOLE] + [THERE] * 7,
+        in_specs=[WHOLE] + [THERE] * 6,
         out_specs=(THERE, THERE),
         scratch_shapes=[
             pltpu.VMEM((TOK, WIDTH), bf16),
             pltpu.VMEM((FRAMES, SLAB, LANES), bf16),
             pltpu.VMEM((2 * TOK, WIDTH), bf16),
-            pltpu.VMEM((COLS, TOK, LANES), bf16),
-            pltpu.VMEM((8, LANES), f32),
             pltpu.VMEM((GROUPS, TOK, GROUP), bf16),
-            pltpu.VMEM((GROUPS, TOK, GROUP), f32),
-            pltpu.VMEM((GROUPS, TOK, GROUP), f32),
-            pltpu.VMEM((GROUPS, TOK, GROUP), f32),
+            pltpu.VMEM((1, TOK), f32),
+            pltpu.VMEM((GROUPS, TOK, GROUP), bf16),
+            pltpu.VMEM((GROUPS, GROUP, TOK), f32),
+            pltpu.VMEM((GROUPS, 8, TOK), f32),
             pltpu.VMEM((GROUPS, WIDTH, GROUP), bf16),
             pltpu.VMEM((GROUPS, WIDTH, GROUP), bf16),
             pltpu.VMEM((WIDTH, WIDTH), bf16),
             pltpu.VMEM((TOK, WIDTH), bf16),
-            pltpu.SemaphoreType.DMA((6, GROUPS)),
+            pltpu.SemaphoreType.DMA((5, GROUPS)),
             pltpu.SemaphoreType.DMA((2,)),
             pltpu.SemaphoreType.DMA((PARTS + 2,)),
         ],
@@ -466,7 +488,7 @@
         ),
         name="attend",
     )(
-        in_vmem(slab), in_hbm(queries), in_hbm(mixed), in_hbm(total), in_hbm(top),
+        in_vmem(slab), in_hbm(queries), in_hbm(mixed), in_hbm(stat),
         in_hbm(weight), in_hbm(out_weight), in_hbm(video),
     )
 
@@ -582,8 +604,8 @@
     spread = exchange(prep(pairs, video, norm_gain))
     queries, keys, values = project(video, norm_gain, qkv_weight)
     wanted = exchange(choose(key_list, spread, queries))
-    mixed, total, top = own_attend(queries, keys, values)
-    spatial, slab = attend(wanted, queries, mixed, total, top, qkv_weight, out_weight, video)
+    mixed, stat = own_attend(queries, keys, values)
+    spatial, slab = attend(wanted, queries, mixed, stat, qkv_weight, out_weight, video)
     slab = time_attend(exchange(slab), time_gain, time_weight)
     return spatial, unpack(exchange(slab))
 

time: 153 us -> 150 us (0.980)
  Pallas kernels: 56.4 us -> 52.3 us
  waiting for transfers between devices: 30.8 us -> 32.4 us
    pallas_call x1, Pallas kernels: 8.97 us -> 7.34 us  [own_attend(): pl.pallas_call(own_kernel, out_shape=(pltpu.HBM((GROUPS, GROUP, TOK), f32...]
    all_to_all x2, waiting for transfers between devices: 30.8 us -> 32.4 us  [exchange(): lax.all_to_all(slab, 'frame', split_axis=0, concat_axis=0, tiled=True)]
  transfers between devices with their start and end apart: 2 -> 2, of which waited for: 2 -> 2; matrix products, arithmetic and copies ran while one was open for 0% -> 0% of each run, Pallas kernels for 12% -> 11%
where the time goes in v4:
time: 150 us
  Pallas kernels  52.3 us (35%)
  blocking collectives  48.2 us (32%)
  waiting for transfers between devices  32.4 us (22%)
  starting transfers between devices  16.2 us (11%)
    all_to_all x2, blocking collectives, exchange(): lax.all_to_all(slab, 'frame', split_axis=0, concat_axis=0, tiled=True)  48.2 us
    all_to_all x2, waiting for transfers between devices, exchange(): lax.all_to_all(slab, 'frame', split_axis=0, concat_axis=0, tiled=True)  32.4 us
    pallas_call x1, Pallas kernels, attend(): pl.pallas_call(attend_kernel, out_shape=(jax.ShapeDtypeStruct((TOK, WIDTH...  17.4 us
    all_to_all x2, starting transfers between devices, exchange(): lax.all_to_all(slab, 'frame', split_axis=0, concat_axis=0, tiled=True)  16.2 us
    pallas_call x1, Pallas kernels, time_attend(): pl.pallas_call(time_kernel, out_shape=jax.ShapeDtypeStruct((FRAMES, SLAB,...  11 us
    pallas_call x1, Pallas kernels, project(): pl.pallas_call(project_kernel, grid=(GROUPS,), out_shape=(out, out, out),...  9.8 us
    pallas_call x1, Pallas kernels, own_attend(): pl.pallas_call(own_kernel, out_shape=(pltpu.HBM((GROUPS, GROUP, TOK), f32...  7.34 us
    pallas_call x1, Pallas kernels, prep(): pl.pallas_call(prep_kernel, out_shape=pltpu.HBM((FRAMES, SLAB, LANES), bf...  3.32 us
  transfers between devices with their start and end apart: 2, of which 2 were waited for; matrix products, arithmetic and copies ran while one was open for 0% of the time, Pallas kernels for 11%

profile of v4, /device:TPU:1, one launch (start us, length us, event | category | flops | bytes accessed | tf_op | source)
XLA Modules:
  0.0 150.0 jit_solution(1878162247884766303)
XLA Ops:
  0.6 3.3 %prep.1 = bf16[128,32,128]{2,1,0:T(8,128)(2,1)} custom-call(s32[1,2]{1,0:T(1,128)} %pairs_hbm.1, bf16[384,1280]{1,0:T(8,128)(2,1)} %video_hbm.3, f32[1280]{0:T(1024)} %gain_ref.2), custom_call_target="tpu_custom_call" | custom-call | flops 2949120 | bytes 1966080 | tf_op jit(solution)/shard_map/prep/pallas_call | solution.py:149
  4.0 11.5 %all-to-all-start = ((bf16[128,32,128]{2,1,0:T(8,128)(2,1)}), bf16[128,32,128]{2,1,0:T(8,128)(2,1)S(1)}, u32[]{:S(2)}, u32[]{:S(2)}) async-start(bf16[128,32,128]{2,1,0:T(8,128)(2,1)} %prep.1), calls=%async_computation | async-start | bytes 2097152 | tf_op jit(solution)/shard_map/all_to_all | solution.py:600
  15.5 0.0 copy-start
  15.5 9.8 %project.1 = (bf16[384,1280]{1,0:T(8,128)(2,1)}, bf16[384,1280]{1,0:T(8,128)(2,1)}, bf16[384,1280]{1,0:T(8,128)(2,1)}) custom-call(bf16[384,1280]{1,0:T(8,128)(2,1)} %video_hbm.3, f32[1280]{0:T(1024)} %gain_ref.2, bf16[1280,3840]{1,0:T(8,128)(2,1)} %weight_hbm.2, bf16[1280,3840]{1,0:T(8,128)(2,1)} %weight_hbm.2, bf16[1280,3840]{1,0:T(8,128)(2,1)} %weight_hbm.2), custom_call_target="tpu_custom_call" | custom-call | flops 3774873600 | bytes 13762560 | tf_op jit(solution)/shard_map/project/pallas_call | solution.py:185
  25.3 9.3 %all-to-all-done.slab_ref = bf16[128,32,128]{2,1,0:T(8,128)(2,1)S(1)} async-done(((bf16[128,32,128]{2,1,0:T(8,128)(2,1)}), bf16[128,32,128]{2,1,0:T(8,128)(2,1)S(1)}, u32[]{:S(2)}, u32[]{:S(2)}) %all-to-all-start) | async-done | bytes 1048608 | tf_op jit(solution)/shard_map/all_to_all | solution.py:600
  34.5 0.0 copy-done
  34.5 2.2 %choose.1 = bf16[128,2,32,128]{3,2,1,0:T(8,128)(2,1)} custom-call(s32[8]{0:T(128)S(1)} %copy-done, bf16[128,32,128]{2,1,0:T(8,128)(2,1)S(1)} %all-to-all-done.slab_ref, bf16[384,1280]{1,0:T(8,128)(2,1)} %get-tuple-element.9.after_ref.q_ref.q_hbm), custom_call_target="tpu_custom_call" | custom-call | flops 536870912 | bytes 3145728 | tf_op jit(solution)/shard_map/choose/pallas_call | solution.py:321
  36.8 4.7 %all-to-all-start.1 = ((bf16[128,2,32,128]{3,2,1,0:T(8,128)(2,1)}), bf16[128,2,32,128]{3,2,1,0:T(8,128)(2,1)S(1)}, u32[]{:S(2)}, u32[]{:S(2)}) async-start(bf16[128,2,32,128]{3,2,1,0:T(8,128)(2,1)} %choose.1), calls=%async_computation.1 | async-start | bytes 4194304 | tf_op jit(solution)/shard_map/all_to_all | solution.py:600
  41.5 7.3 %own_attend.1 = (f32[5,256,384]{2,1,0:T(8,128)}, f32[5,8,384]{2,1,0:T(8,128)}) custom-call(bf16[384,1280]{1,0:T(8,128)(2,1)} %get-tuple-element.9.after_ref.q_ref.q_hbm, bf16[384,1280]{1,0:T(8,128)(2,1)} %get-tuple-element.10.k_ref, bf16[384,1280]{1,0:T(8,128)(2,1)} %get-tuple-element.11.v_ref), custom_call_target="tpu_custom_call" | custom-call | flops 1509949440 | bytes 4915200 | tf_op jit(solution)/shard_map/own_attend/pallas_call | solution.py:277
  48.8 23.1 %all-to-all-done.1.slab_ref = bf16[128,2,32,128]{3,2,1,0:T(8,128)(2,1)S(1)} async-done(((bf16[128,2,32,128]{3,2,1,0:T(8,128)(2,1)}), bf16[128,2,32,128]{3,2,1,0:T(8,128)(2,1)S(1)}, u32[]{:S(2)}, u32[]{:S(2)}) %all-to-all-start.1) | async-done | bytes 2097184 | tf_op jit(solution)/shard_map/all_to_all | solution.py:600
  71.9 0.0 copy-start.1
  71.9 17.4 %attend.1 = (bf16[384,1280]{1,0:T(8,128)(2,1)}, bf16[128,32,128]{2,1,0:T(8,128)(2,1)}) custom-call(bf16[128,2,32,128]{3,2,1,0:T(8,128)(2,1)S(1)} %all-to-all-done.1.slab_ref, bf16[384,1280]{1,0:T(8,128)(2,1)} %get-tuple-element.9.after_ref.q_ref.q_hbm, f32[5,256,384]{2,1,0:T(8,128)} %get-tuple-element.12.mixed_hbm, f32[5,8,384]{2,1,0:T(8,128)} %get-tuple-element.13.stat_hbm, ...), custom_call_target="tpu_custom_call" | custom-call | flops 8053063680 | bytes 19660800 | tf_op jit(solution)/shard_map/attend/pallas_call | solution.py:458
  89.3 24.2 %all_to_all.20.slab_ref = bf16[128,32,128]{2,1,0:T(8,128)(2,1)S(1)} all-to-all(bf16[128,32,128]{2,1,0:T(8,128)(2,1)} %get-tuple-element.15), channel_id=1, replica_groups=mesh['frame'=128] {'frame'}, dimensions={0} | all-to-all | bytes 2097152 | tf_op jit(solution)/shard_map/all_to_all | solution.py:600
  113.5 0.0 copy-done.1
  113.5 11.0 %time_attend.1 = bf16[128,32,128]{2,1,0:T(8,128)(2,1)} custom-call(bf16[128,32,128]{2,1,0:T(8,128)(2,1)S(1)} %all_to_all.20.slab_ref, f32[1280]{0:T(1024)S(1)} %copy-done.1, bf16[1280,3840]{1,0:T(8,128)(2,1)} %weight_hbm.3), custom_call_target="tpu_custom_call" | custom-call | flops 4278190080 | bytes 11796480 | tf_op jit(solution)/shard_map/time_attend/pallas_call | solution.py:545
  124.5 24.0 %all_to_all.21.slab_ref = bf16[128,32,128]{2,1,0:T(8,128)(2,1)S(1)} all-to-all(bf16[128,32,128]{2,1,0:T(8,128)(2,1)} %time_attend.1), channel_id=1, replica_groups=mesh['frame'=128] {'frame'}, dimensions={0} | all-to-all | bytes 2097152 | tf_op jit(solution)/shard_map/all_to_all | solution.py:600
  148.5 1.3 unpack.1
Async XLA Ops:
  4.0 30.6 %all-to-all-start = ((bf16[128,32,128]{2,1,0:T(8,128)(2,1)}), bf16[128,32,128]{2,1,0:T(8,128)(2,1)S(1)}, u32[]{:S(2)}, u32[]{:S(2)}) async-start(bf16[128,32,128]{2,1,0:T(8,128)(2,1)} %prep.1), calls=%async_computation | async-start | bytes 2097152 | tf_op jit(solution)/shard_map/all_to_all | solution.py:600
  15.5 19.1 %copy-start = (s32[8]{0:T(128)S(1)}, s32[8]{0:T(128)}, u32[]{:S(2)}) copy-start(s32[8]{0:T(128)} %key_list_ref.1) | copy-start | bytes 100
  36.8 35.2 %all-to-all-start.1 = ((bf16[128,2,32,128]{3,2,1,0:T(8,128)(2,1)}), bf16[128,2,32,128]{3,2,1,0:T(8,128)(2,1)S(1)}, u32[]{:S(2)}, u32[]{:S(2)}) async-start(bf16[128,2,32,128]{3,2,1,0:T(8,128)(2,1)} %choose.1), calls=%async_computation.1 | async-start | bytes 4194304 | tf_op jit(solution)/shard_map/all_to_all | solution.py:600
  71.9 41.5 %copy-start.1 = (f32[1280]{0:T(1024)S(1)}, f32[1280]{0:T(1024)}, u32[]{:S(2)}) copy-start(f32[1280]{0:T(1024)} %gain_ref.3) | copy-start | bytes 15364

commit v5 on v4

--- a/solution.py
+++ b/solution.py
@@ -100,47 +100,29 @@
             ]
 
 
-def prep_kernel(
-    pairs_hbm, video_hbm, gain_hbm, slab_hbm,
-    pairs_ref, video_ref, gain_ref, normed_ref, slab_ref, sems, out_sems,
-):
-    small = (
-        pltpu.make_async_copy(gain_hbm, gain_ref, sems.at[PARTS]),
-        pltpu.make_async_copy(pairs_hbm, pairs_ref, sems.at[PARTS + 1]),
-    )
-    arriving = []
-    for part in range(PARTS):
-        rows = pl.ds(part * FRAMES, FRAMES)
-        arriving.append(
-            pltpu.make_async_copy(video_hbm.at[rows], video_ref.at[rows], sems.at[part])
-        )
-    for copy in (small[0], arriving[0], small[1], *arriving[1:]):
-        copy.start()
+def prep_kernel(pairs_ref, video_ref, gain_ref, slab_hbm, normed_ref, slab_ref, sems):
     swap = swap_matrix()
-    leaving = []
-
-    def give(half, spare=None):
-        rows_to_slab(tiles_of(normed_ref), slab_ref, swap, spare, halves=(half,))
-        some = pl.ds(16 * half, 16)
-        leaving.append(
-            pltpu.make_async_copy(slab_ref.at[:, some], slab_hbm.at[:, some], out_sems.at[half])
-        )
-        leaving[-1].start()
-
-    small[0].wait()
     gain = gain_ref[...].reshape(1, WIDTH)
-    for part, copy in enumerate(arriving):
-        copy.wait()
-        rows = pl.ds(part * FRAMES, FRAMES)
-        normed_ref[rows, :] = norm_rows(video_ref[rows, :].astype(f32), gain)
-        if part == 1:
-            give(0)
-    small[1].wait()
     spare = [
         jnp.full((16, LANES), pairs_ref[0, which], jnp.int32).astype(f32).astype(bf16)
         for which in range(2)
     ]
-    give(1, spare)
+    leaving = []
+
+    def give(half):
+        rows_to_slab(tiles_of(normed_ref), slab_ref, swap, spare, halves=(half,))
+        some = pl.ds(16 * half, 16)
+        leaving.append(
+            pltpu.make_async_copy(slab_ref.at[:, some], slab_hbm.at[:, some], sems.at[half])
+        )
+        leaving[-1].start()
+
+    for k in range(PARTS):
+        rows = pl.ds(k * FRAMES, FRAMES)
+        normed_ref[rows, :] = norm_rows(video_ref[rows, :].astype(f32), gain)
+        if k == 1:
+            give(0)
+    give(1)
     for copy in leaving:
         copy.wait()
 
@@ -149,15 +131,11 @@
     return pl.pallas_call(
         prep_kernel,
         out_shape=pltpu.HBM((FRAMES, SLAB, LANES), bf16),
-        in_specs=[THERE, THERE, THERE],
+        in_specs=[SMALL, WHOLE, WHOLE],
         out_specs=THERE,
         scratch_shapes=[
-            pltpu.SMEM((1, 2), jnp.int32),
-            pltpu.VMEM((TOK, WIDTH), bf16),
-            pltpu.VMEM((WIDTH,), f32),
             pltpu.VMEM((TOK, WIDTH), bf16),
             pltpu.VMEM((FRAMES, SLAB, LANES), bf16),
-            pltpu.SemaphoreType.DMA((PARTS + 2,)),
             pltpu.SemaphoreType.DMA((2,)),
         ],
         compiler_params=params(VMEM),
@@ -338,8 +316,8 @@
 
 def attend_kernel(
     slab_ref, q_hbm, mixed_hbm, stat_hbm, weight_hbm, wo_hbm, video_hbm,
-    spatial_hbm, out_slab_hbm,
-    spatial_ref, out_slab_ref, rows_ref, heads_ref, most_ref, q_ref, mixed_ref, stat_ref,
+    spatial_hbm, out_slab_ref,
+    spatial_ref, rows_ref, heads_ref, most_ref, q_ref, mixed_ref, stat_ref,
     wk_ref, wv_ref, wo_ref, video_ref, sems, last_sems, out_sems,
 ):
     def copies(group):
@@ -432,11 +410,6 @@
             mix_group(group, weights, values, [jnp.exp2(o - top) for o, top in zip(own, tops)])
 
     given = []
-
-    def give(source, target):
-        given.append(pltpu.make_async_copy(source, target, out_sems.at[len(given)]))
-        given[-1].start()
-
     for copy in last:
         copy.wait()
     for k in range(PARTS):
@@ -444,12 +417,11 @@
         heads = jnp.concatenate([heads_ref[g, rows, :] for g in range(GROUPS)], axis=1)
         added = jnp.dot(heads, wo_ref[...], preferred_element_type=f32)
         spatial_ref[rows, :] = (video_ref[rows, :].astype(f32) + added).astype(bf16)
-        give(spatial_ref.at[rows], spatial_hbm.at[rows])
-        if k == 1:
-            rows_to_slab(tiles_of(spatial_ref), out_slab_ref, swap, halves=(0,))
-            give(out_slab_ref.at[:, pl.ds(0, 16)], out_slab_hbm.at[:, pl.ds(0, 16)])
-    rows_to_slab(tiles_of(spatial_ref), out_slab_ref, swap, halves=(1,))
-    give(out_slab_ref.at[:, pl.ds(16, 16)], out_slab_hbm.at[:, pl.ds(16, 16)])
+        given.append(
+            pltpu.make_async_copy(spatial_ref.at[rows], spatial_hbm.at[rows], out_sems.at[k])
+        )
+        given[-1].start()
+    rows_to_slab(tiles_of(spatial_ref), out_slab_ref, swap)
     for copy in given:
         copy.wait()
 
@@ -459,13 +431,12 @@
         attend_kernel,
         out_shape=(
             jax.ShapeDtypeStruct((TOK, WIDTH), bf16),
-            pltpu.HBM((FRAMES, SLAB, LANES), bf16),
+            pltpu.VMEM((FRAMES, SLAB, LANES), bf16),
         ),
         in_specs=[WHOLE] + [THERE] * 6,
-        out_specs=(THERE, THERE),
+        out_specs=(THERE, WHOLE),
         scratch_shapes=[
             pltpu.VMEM((TOK, WIDTH), bf16),
-            pltpu.VMEM((FRAMES, SLAB, LANES), bf16),
             pltpu.VMEM((2 * TOK, WIDTH), bf16),
             pltpu.VMEM((GROUPS, TOK, GROUP), bf16),
             pltpu.VMEM((1, TOK), f32),
@@ -478,7 +449,7 @@
             pltpu.VMEM((TOK, WIDTH), bf16),
             pltpu.SemaphoreType.DMA((5, GROUPS)),
             pltpu.SemaphoreType.DMA((2,)),
-            pltpu.SemaphoreType.DMA((PARTS + 2,)),
+            pltpu.SemaphoreType.DMA((PARTS,)),
         ],
         compiler_params=params(VMEM),
         cost_estimate=cost(
@@ -544,7 +515,7 @@
 def time_attend(slab, gain, weight):
     return pl.pallas_call(
         time_kernel,
-        out_shape=jax.ShapeDtypeStruct((FRAMES, SLAB, LANES), bf16),
+        out_shape=pltpu.VMEM((FRAMES, SLAB, LANES), bf16),
         in_specs=[WHOLE, WHOLE, THERE],
         out_specs=WHOLE,
         scratch_shapes=[
@@ -560,7 +531,7 @@
             HEADS * TOK * FRAMES,
         ),
         name="time_attend",
-    )(in_vmem(slab), gain, in_hbm(weight))
+    )(in_vmem(slab), in_hbm(gain), in_hbm(weight))
 
 
 def unpack_kernel(slab_ref, out_hbm, out_ref, sems):

time: 150 us -> 148 us (0.987)
  transfers between devices with their start and end apart: 2 -> 2, of which waited for: 2 -> 2; matrix products, arithmetic and copies ran while one was open for 0% -> 0% of each run, Pallas kernels for 11% -> 12%
where the time goes in v5:
time: 148 us
  Pallas kernels  51.3 us (35%)
  blocking collectives  46.9 us (32%)
  waiting for transfers between devices  32.4 us (22%)
  starting transfers between devices  16.2 us (11%)
    all_to_all x2, blocking collectives, exchange(): lax.all_to_all(slab, 'frame', split_axis=0, concat_axis=0, tiled=True)  46.9 us
    all_to_all x2, waiting for transfers between devices, exchange(): lax.all_to_all(slab, 'frame', split_axis=0, concat_axis=0, tiled=True)  32.4 us
    pallas_call x1, Pallas kernels, attend(): pl.pallas_call(attend_kernel, out_shape=(jax.ShapeDtypeStruct((TOK, WIDTH...  16.8 us
    all_to_all x2, starting transfers between devices, exchange(): lax.all_to_all(slab, 'frame', split_axis=0, concat_axis=0, tiled=True)  16.2 us
    pallas_call x1, Pallas kernels, time_attend(): pl.pallas_call(time_kernel, out_shape=pltpu.VMEM((FRAMES, SLAB, LANES), b...  10.8 us
    pallas_call x1, Pallas kernels, project(): pl.pallas_call(project_kernel, grid=(GROUPS,), out_shape=(out, out, out),...  9.77 us
    pallas_call x1, Pallas kernels, own_attend(): pl.pallas_call(own_kernel, out_shape=(pltpu.HBM((GROUPS, GROUP, TOK), f32...  7.34 us
    pallas_call x1, Pallas kernels, prep(): pl.pallas_call(prep_kernel, out_shape=pltpu.HBM((FRAMES, SLAB, LANES), bf...  3.14 us
  transfers between devices with their start and end apart: 2, of which 2 were waited for; matrix products, arithmetic and copies ran while one was open for 0% of the time, Pallas kernels for 12%

profile of v5, /device:TPU:1, one launch (start us, length us, event | category | flops | bytes accessed | tf_op | source)
XLA Modules:
  0.0 147.6 jit_solution(18157776942072922732)
XLA Ops:
  0.6 3.1 %prep.1 = bf16[128,32,128]{2,1,0:T(8,128)(2,1)} custom-call(s32[1,2]{1,0:T(1,128)} %pairs_ref.1, bf16[384,1280]{1,0:T(8,128)(2,1)} %video_hbm.1, f32[1280]{0:T(1024)} %gain_ref.4), custom_call_target="tpu_custom_call" | custom-call | flops 2949120 | bytes 1966080 | tf_op jit(solution)/shard_map/prep/pallas_call | solution.py:131
  3.8 11.5 %all-to-all-start = ((bf16[128,32,128]{2,1,0:T(8,128)(2,1)}), bf16[128,32,128]{2,1,0:T(8,128)(2,1)S(1)}, u32[]{:S(2)}, u32[]{:S(2)}) async-start(bf16[128,32,128]{2,1,0:T(8,128)(2,1)} %prep.1), calls=%async_computation | async-start | bytes 2097152 | tf_op jit(solution)/shard_map/all_to_all | solution.py:571
  15.3 0.0 copy-start
  15.3 9.8 %project.1 = (bf16[384,1280]{1,0:T(8,128)(2,1)}, bf16[384,1280]{1,0:T(8,128)(2,1)}, bf16[384,1280]{1,0:T(8,128)(2,1)}) custom-call(bf16[384,1280]{1,0:T(8,128)(2,1)} %video_hbm.1, f32[1280]{0:T(1024)} %gain_ref.4, bf16[1280,3840]{1,0:T(8,128)(2,1)} %weight_hbm.2, bf16[1280,3840]{1,0:T(8,128)(2,1)} %weight_hbm.2, bf16[1280,3840]{1,0:T(8,128)(2,1)} %weight_hbm.2), custom_call_target="tpu_custom_call" | custom-call | flops 3774873600 | bytes 13762560 | tf_op jit(solution)/shard_map/project/pallas_call | solution.py:163
  25.1 9.3 %all-to-all-done.slab_ref = bf16[128,32,128]{2,1,0:T(8,128)(2,1)S(1)} async-done(((bf16[128,32,128]{2,1,0:T(8,128)(2,1)}), bf16[128,32,128]{2,1,0:T(8,128)(2,1)S(1)}, u32[]{:S(2)}, u32[]{:S(2)}) %all-to-all-start) | async-done | bytes 1048608 | tf_op jit(solution)/shard_map/all_to_all | solution.py:571
  34.4 0.0 copy-done
  34.4 2.2 %choose.1 = bf16[128,2,32,128]{3,2,1,0:T(8,128)(2,1)} custom-call(s32[8]{0:T(128)S(1)} %copy-done, bf16[128,32,128]{2,1,0:T(8,128)(2,1)S(1)} %all-to-all-done.slab_ref, bf16[384,1280]{1,0:T(8,128)(2,1)} %get-tuple-element.9.after_ref.q_ref.q_hbm), custom_call_target="tpu_custom_call" | custom-call | flops 536870912 | bytes 3145728 | tf_op jit(solution)/shard_map/choose/pallas_call | solution.py:299
  36.6 4.7 %all-to-all-start.1 = ((bf16[128,2,32,128]{3,2,1,0:T(8,128)(2,1)}), bf16[128,2,32,128]{3,2,1,0:T(8,128)(2,1)S(1)}, u32[]{:S(2)}, u32[]{:S(2)}) async-start(bf16[128,2,32,128]{3,2,1,0:T(8,128)(2,1)} %choose.1), calls=%async_computation.1 | async-start | bytes 4194304 | tf_op jit(solution)/shard_map/all_to_all | solution.py:571
  41.3 7.3 %own_attend.1 = (f32[5,256,384]{2,1,0:T(8,128)}, f32[5,8,384]{2,1,0:T(8,128)}) custom-call(bf16[384,1280]{1,0:T(8,128)(2,1)} %get-tuple-element.9.after_ref.q_ref.q_hbm, bf16[384,1280]{1,0:T(8,128)(2,1)} %get-tuple-element.10.k_ref, bf16[384,1280]{1,0:T(8,128)(2,1)} %get-tuple-element.11.v_ref), custom_call_target="tpu_custom_call" | custom-call | flops 1509949440 | bytes 4915200 | tf_op jit(solution)/shard_map/own_attend/pallas_call | solution.py:255
  48.6 23.1 %all-to-all-done.1.slab_ref = bf16[128,2,32,128]{3,2,1,0:T(8,128)(2,1)S(1)} async-done(((bf16[128,2,32,128]{3,2,1,0:T(8,128)(2,1)}), bf16[128,2,32,128]{3,2,1,0:T(8,128)(2,1)S(1)}, u32[]{:S(2)}, u32[]{:S(2)}) %all-to-all-start.1) | async-done | bytes 2097184 | tf_op jit(solution)/shard_map/all_to_all | solution.py:571
  71.7 16.8 %attend.1 = (bf16[384,1280]{1,0:T(8,128)(2,1)}, bf16[128,32,128]{2,1,0:T(8,128)(2,1)S(1)}) custom-call(bf16[128,2,32,128]{3,2,1,0:T(8,128)(2,1)S(1)} %all-to-all-done.1.slab_ref, bf16[384,1280]{1,0:T(8,128)(2,1)} %get-tuple-element.9.after_ref.q_ref.q_hbm, f32[5,256,384]{2,1,0:T(8,128)} %get-tuple-element.12.mixed_hbm, ...), custom_call_target="tpu_custom_call" | custom-call | flops 8053063680 | bytes 19660800 | tf_op jit(solution)/shard_map/attend/pallas_call | solution.py:430
  88.5 23.3 %all_to_all.20.slab_ref = bf16[128,32,128]{2,1,0:T(8,128)(2,1)S(1)} all-to-all(bf16[128,32,128]{2,1,0:T(8,128)(2,1)S(1)} %get-tuple-element.15), channel_id=1, replica_groups=mesh['frame'=128] {'frame'}, dimensions={0} | all-to-all | bytes 2097152 | tf_op jit(solution)/shard_map/all_to_all | solution.py:571
  111.8 10.8 %time_attend.1 = bf16[128,32,128]{2,1,0:T(8,128)(2,1)S(1)} custom-call(bf16[128,32,128]{2,1,0:T(8,128)(2,1)S(1)} %all_to_all.20.slab_ref, f32[1280]{0:T(1024)} %gain_ref.5, bf16[1280,3840]{1,0:T(8,128)(2,1)} %weight_hbm.3), custom_call_target="tpu_custom_call" | custom-call | flops 4278190080 | bytes 11796480 | tf_op jit(solution)/shard_map/time_attend/pallas_call | solution.py:516
  122.6 23.6 %all_to_all.21.slab_ref = bf16[128,32,128]{2,1,0:T(8,128)(2,1)S(1)} all-to-all(bf16[128,32,128]{2,1,0:T(8,128)(2,1)S(1)} %time_attend.1), channel_id=1, replica_groups=mesh['frame'=128] {'frame'}, dimensions={0} | all-to-all | bytes 2097152 | tf_op jit(solution)/shard_map/all_to_all | solution.py:571
  146.2 1.3 unpack.1
Async XLA Ops:
  3.8 30.6 %all-to-all-start = ((bf16[128,32,128]{2,1,0:T(8,128)(2,1)}), bf16[128,32,128]{2,1,0:T(8,128)(2,1)S(1)}, u32[]{:S(2)}, u32[]{:S(2)}) async-start(bf16[128,32,128]{2,1,0:T(8,128)(2,1)} %prep.1), calls=%async_computation | async-start | bytes 2097152 | tf_op jit(solution)/shard_map/all_to_all | solution.py:571
  15.3 19.1 %copy-start = (s32[8]{0:T(128)S(1)}, s32[8]{0:T(128)}, u32[]{:S(2)}) copy-start(s32[8]{0:T(128)} %key_list_ref.1) | copy-start | bytes 100
  36.6 35.2 %all-to-all-start.1 = ((bf16[128,2,32,128]{3,2,1,0:T(8,128)(2,1)}), bf16[128,2,32,128]{3,2,1,0:T(8,128)(2,1)S(1)}, u32[]{:S(2)}, u32[]{:S(2)}) async-start(bf16[128,2,32,128]{3,2,1,0:T(8,128)(2,1)} %choose.1), calls=%async_computation.1 | async-start | bytes 4194304 | tf_op jit(solution)/shard_map/all_to_all | solution.py:571

commit v6 on v5

--- a/solution.py
+++ b/solution.py
@@ -142,41 +142,6 @@
         cost_estimate=cost(6 * TOK * WIDTH, 4 * TOK * WIDTH),
         name="prep",
     )(in_hbm(pairs), in_hbm(video), in_hbm(gain))
-
-
-def project_kernel(video_ref, gain_ref, wq_ref, wk_ref, wv_ref, q_ref, k_ref, v_ref, normed_ref):
-    @pl.when(pl.program_id(0) == 0)
-    def _():
-        gain = gain_ref[...].reshape(1, WIDTH)
-        normed_ref[...] = norm_rows(video_ref[...].astype(f32), gain)
-
-    rows = normed_ref[...]
-    queries = jnp.dot(rows, wq_ref[...], preferred_element_type=f32) * SCALE
-    q_ref[...] = queries.astype(bf16)
-    k_ref[...] = jnp.dot(rows, wk_ref[...], preferred_element_type=f32).astype(bf16)
-    v_ref[...] = jnp.dot(rows, wv_ref[...], preferred_element_type=f32).astype(bf16)
-
-
-def project(video, gain, weight):
-    out = pltpu.HBM((TOK, WIDTH), bf16)
-    out_spec = pl.BlockSpec((TOK, GROUP), lambda i: (0, i))
-    return pl.pallas_call(
-        project_kernel,
-        grid=(GROUPS,),
-        out_shape=(out, out, out),
-        in_specs=[
-            WHOLE,
-            WHOLE,
-            pl.BlockSpec((WIDTH, GROUP), lambda i: (0, i)),
-            pl.BlockSpec((WIDTH, GROUP), lambda i: (0, GROUPS + i)),
-            pl.BlockSpec((WIDTH, GROUP), lambda i: (0, 2 * GROUPS + i)),
-        ],
-        out_specs=(out_spec, out_spec, out_spec),
-        scratch_shapes=[pltpu.VMEM((TOK, WIDTH), bf16)],
-        compiler_params=params(VMEM),
-        cost_estimate=cost(6 * TOK * WIDTH * WIDTH, 6 * WIDTH * WIDTH + 8 * TOK * WIDTH),
-        name="project",
-    )(in_hbm(video), in_hbm(gain), in_hbm(weight), in_hbm(weight), in_hbm(weight))
 
 
 def low_lanes(rows):
@@ -231,12 +196,39 @@
     return jnp.concatenate([values, jnp.ones((16, values.shape[1]), bf16)], axis=0)
 
 
-def own_kernel(q_ref, k_ref, v_ref, mixed_ref, stat_ref):
+def group_copies(weight_hbm, weight_ref, sems, group):
+    return [
+        pltpu.make_async_copy(
+            weight_hbm.at[:, group_lanes(group, GROUP, which * WIDTH)],
+            weight_ref.at[which, group],
+            sems.at[which, group],
+        )
+        for which in range(3)
+    ]
+
+
+def own_kernel(
+    video_ref, gain_ref, weight_hbm, q_ref, mixed_ref, stat_ref, rows_ref, weight_ref, sems
+):
+    for group in range(GROUPS):
+        for copy in group_copies(weight_hbm, weight_ref, sems, group):
+            copy.start()
+    gain = gain_ref[...].reshape(1, WIDTH)
+    for k in range(PARTS):
+        rows = pl.ds(k * FRAMES, FRAMES)
+        rows_ref[rows, :] = norm_rows(video_ref[rows, :].astype(f32), gain)
+
     @pl.loop(0, GROUPS)
     def _(group):
-        at = group_lanes(group, GROUP)
-        queries, keys = q_ref[:, at], k_ref[:, at]
-        values = v_ref[:, at].T
+        for copy in group_copies(weight_hbm, weight_ref, sems, group):
+            copy.wait()
+        rows = rows_ref[...]
+        queries, keys, values = [
+            jnp.dot(rows, weight_ref[which, group], preferred_element_type=f32)
+            for which in range(3)
+        ]
+        queries, keys, values = (queries * SCALE).astype(bf16), keys.astype(bf16), values.astype(bf16).T
+        q_ref[:, group_lanes(group, GROUP)] = queries
         scores = []
         for head in range(4):
             lanes = slice(head // 2 * LANES, (head // 2 + 1) * LANES)
@@ -251,21 +243,33 @@
             stat_ref[group, 4 + head : 5 + head, :] = out[HEAD : HEAD + 1]
 
 
-def own_attend(queries, keys, values):
+def own_attend(video, gain, weight):
     return pl.pallas_call(
         own_kernel,
-        out_shape=(pltpu.HBM((GROUPS, GROUP, TOK), f32), pltpu.HBM((GROUPS, 8, TOK), f32)),
-        in_specs=[WHOLE, WHOLE, WHOLE],
-        out_specs=(WHOLE, WHOLE),
+        out_shape=(
+            pltpu.HBM((TOK, WIDTH), bf16),
+            pltpu.HBM((GROUPS, GROUP, TOK), f32),
+            pltpu.HBM((GROUPS, 8, TOK), f32),
+        ),
+        in_specs=[WHOLE, WHOLE, THERE],
+        out_specs=(WHOLE, WHOLE, WHOLE),
+        scratch_shapes=[
+            pltpu.VMEM((TOK, WIDTH), bf16),
+            pltpu.VMEM((3, GROUPS, WIDTH, GROUP), bf16),
+            pltpu.SemaphoreType.DMA((3, GROUPS)),
+        ],
         compiler_params=params(VMEM),
-        cost_estimate=cost(8 * TOK * TOK * WIDTH, 10 * TOK * WIDTH, HEADS * TOK * TOK),
+        cost_estimate=cost(
+            6 * TOK * WIDTH * WIDTH + 8 * TOK * TOK * WIDTH,
+            6 * WIDTH * WIDTH + 10 * TOK * WIDTH,
+            HEADS * TOK * TOK,
+        ),
         name="own_attend",
-    )(in_hbm(queries), in_hbm(keys), in_hbm(values))
-
-
-def choose_kernel(key_list_ref, slab_ref, after_ref, out_hbm, out_ref, sems):
+    )(in_hbm(video), in_hbm(gain), in_hbm(weight))
+
+
+def choose_kernel(key_list_ref, slab_ref, after_ref, out_ref):
     del after_ref
-    copies = []
     halves = [
         jnp.concatenate([slab_ref[key_list_ref[s], at : at + 16, :] for s in range(KEYS)], axis=0)
         for at in (0, 16)
@@ -285,26 +289,14 @@
         chosen = chosen.astype(bf16).reshape(8, 2, 16, 2 * LANES)
         out_ref[f : f + 8, :, 0:16, :] = chosen[..., :LANES]
         out_ref[f : f + 8, :, 16:32, :] = chosen[..., LANES:]
-        if (f + 8) % 32 == 0:
-            some = pl.ds(f - 24, 32)
-            copies.append(
-                pltpu.make_async_copy(out_ref.at[some], out_hbm.at[some], sems.at[len(copies)])
-            )
-            copies[-1].start()
-    for copy in copies:
-        copy.wait()
 
 
 def choose(key_list, slab, after):
     return pl.pallas_call(
         choose_kernel,
-        out_shape=pltpu.HBM((FRAMES, 2, SLAB, LANES), bf16),
+        out_shape=pltpu.VMEM((FRAMES, 2, SLAB, LANES), bf16),
         in_specs=[SMALL, WHOLE, THERE],
-        out_specs=THERE,
-        scratch_shapes=[
-            pltpu.VMEM((FRAMES, 2, SLAB, LANES), bf16),
-            pltpu.SemaphoreType.DMA((4,)),
-        ],
+        out_specs=WHOLE,
         compiler_params=params(VMEM),
         cost_estimate=cost(4 * FRAMES * SLAB * LANES * 256, 6 * FRAMES * SLAB * LANES),
         name="choose",
@@ -467,18 +459,8 @@
 def time_kernel(
     slab_ref, gain_ref, weight_hbm, out_slab_ref, rows_ref, heads_ref, weight_ref, sems
 ):
-    def copies(group):
-        return [
-            pltpu.make_async_copy(
-                weight_hbm.at[:, group_lanes(group, GROUP, which * WIDTH)],
-                weight_ref.at[which, group],
-                sems.at[which, group],
-            )
-            for which in range(3)
-        ]
-
     for group in range(GROUPS):
-        for copy in copies(group):
+        for copy in group_copies(weight_hbm, weight_ref, sems, group):
             copy.start()
     swap = swap_matrix()
     slab_to_rows(
@@ -491,7 +473,7 @@
 
     @pl.loop(0, GROUPS)
     def _(group):
-        for copy in copies(group):
+        for copy in group_copies(weight_hbm, weight_ref, sems, group):
             copy.wait()
         rows = rows_ref[...]
         made = [
@@ -573,9 +555,8 @@
 
 def body(video, key_list, pairs, norm_gain, qkv_weight, out_weight, time_gain, time_weight):
     spread = exchange(prep(pairs, video, norm_gain))
-    queries, keys, values = project(video, norm_gain, qkv_weight)
+    queries, mixed, stat = own_attend(video, norm_gain, qkv_weight)
     wanted = exchange(choose(key_list, spread, queries))
-    mixed, stat = own_attend(queries, keys, values)
     spatial, slab = attend(wanted, queries, mixed, stat, qkv_weight, out_weight, video)
     slab = time_attend(exchange(slab), time_gain, time_weight)
     return spatial, unpack(exchange(slab))

time: 148 us -> 147 us (level)
  blocking collectives: 46.9 us -> 81.7 us
  waiting for transfers between devices: 32.4 us -> 6.66 us
  Pallas kernels: 51.3 us -> 45.8 us
  starting transfers between devices: 16.2 us -> 11.5 us
    all_to_all x2 -> x3, blocking collectives: 46.9 us -> 81.7 us  [exchange(): lax.all_to_all(slab, 'frame', split_axis=0, concat_axis=0, tiled=True)]
    all_to_all x2 -> x1, waiting for transfers between devices: 32.4 us -> 6.66 us  [exchange(): lax.all_to_all(slab, 'frame', split_axis=0, concat_axis=0, tiled=True)]
    pallas_call x3 -> x2, Pallas kernels: 19.3 us -> 13.8 us  [the longest x1 12.4 us: own_attend(): pl.pallas_call(own_kernel, out_shape=(pltpu.HBM((TOK, WIDTH), bf16), pltp...]
    all_to_all x2 -> x1, starting transfers between devices: 16.2 us -> 11.5 us  [exchange(): lax.all_to_all(slab, 'frame', split_axis=0, concat_axis=0, tiled=True)]
  transfers between devices with their start and end apart: 2 -> 1, of which waited for: 2 -> 1; matrix products, arithmetic and copies ran while one was open for 0% -> 0% of each run, Pallas kernels for 12% -> 8%
where the time goes in v6:
time: 147 us; the launch traced here: 146 us
  blocking collectives  81.7 us (56%)
  Pallas kernels  45.8 us (31%)
  starting transfers between devices  11.5 us (8%)
  waiting for transfers between devices  6.66 us (5%)
    all_to_all x3, blocking collectives, exchange(): lax.all_to_all(slab, 'frame', split_axis=0, concat_axis=0, tiled=True)  81.7 us
    pallas_call x1, Pallas kernels, attend(): pl.pallas_call(attend_kernel, out_shape=(jax.ShapeDtypeStruct((TOK, WIDTH...  16.8 us
    pallas_call x1, Pallas kernels, own_attend(): pl.pallas_call(own_kernel, out_shape=(pltpu.HBM((TOK, WIDTH), bf16), pltp...  12.4 us
    all_to_all x1, starting transfers between devices, exchange(): lax.all_to_all(slab, 'frame', split_axis=0, concat_axis=0, tiled=True)  11.5 us
    pallas_call x1, Pallas kernels, time_attend(): pl.pallas_call(time_kernel, out_shape=pltpu.VMEM((FRAMES, SLAB, LANES), b...  10.8 us
    all_to_all x1, waiting for transfers between devices, exchange(): lax.all_to_all(slab, 'frame', split_axis=0, concat_axis=0, tiled=True)  6.66 us
    pallas_call x1, Pallas kernels, prep(): pl.pallas_call(prep_kernel, out_shape=pltpu.HBM((FRAMES, SLAB, LANES), bf...  3.12 us
  transfers between devices with their start and end apart: 1, of which 1 were waited for; matrix products, arithmetic and copies ran while one was open for 0% of the time, Pallas kernels for 8%

profile of v6, /device:TPU:1, one launch (start us, length us, event | category | flops | bytes accessed | tf_op | source)
XLA Modules:
  0.0 146.5 jit_solution(12140322154147660116)
XLA Ops:
  0.6 3.1 %prep.1 = bf16[128,32,128]{2,1,0:T(8,128)(2,1)} custom-call(s32[1,2]{1,0:T(1,128)} %pairs_ref.1, bf16[384,1280]{1,0:T(8,128)(2,1)} %video_hbm.1, f32[1280]{0:T(1024)} %gain_ref.4), custom_call_target="tpu_custom_call" | custom-call | flops 2949120 | bytes 1966080 | tf_op jit(solution)/shard_map/prep/pallas_call | solution.py:131
  3.8 11.5 %all-to-all-start = ((bf16[128,32,128]{2,1,0:T(8,128)(2,1)}), bf16[128,32,128]{2,1,0:T(8,128)(2,1)S(1)}, u32[]{:S(2)}, u32[]{:S(2)}) async-start(bf16[128,32,128]{2,1,0:T(8,128)(2,1)} %prep.1), calls=%async_computation | async-start | bytes 2097152 | tf_op jit(solution)/shard_map/all_to_all | solution.py:553
  15.3 12.4 %own_attend.1 = (bf16[384,1280]{1,0:T(8,128)(2,1)}, f32[5,256,384]{2,1,0:T(8,128)}, f32[5,8,384]{2,1,0:T(8,128)}) custom-call(bf16[384,1280]{1,0:T(8,128)(2,1)} %video_hbm.1, f32[1280]{0:T(1024)} %gain_ref.4, bf16[1280,3840]{1,0:T(8,128)(2,1)} %weight_hbm.4), custom_call_target="tpu_custom_call" | custom-call | flops 5284823040 | bytes 14745600 | tf_op jit(solution)/shard_map/own_attend/pallas_call | solution.py:247
  27.7 6.7 %all-to-all-done.slab_ref = bf16[128,32,128]{2,1,0:T(8,128)(2,1)S(1)} async-done(((bf16[128,32,128]{2,1,0:T(8,128)(2,1)}), bf16[128,32,128]{2,1,0:T(8,128)(2,1)S(1)}, u32[]{:S(2)}, u32[]{:S(2)}) %all-to-all-start) | async-done | bytes 1048608 | tf_op jit(solution)/shard_map/all_to_all | solution.py:553
  34.3 1.4 choose.1
  35.7 34.9 %all_to_all.20.slab_ref = bf16[128,2,32,128]{3,2,1,0:T(8,128)(2,1)S(1)} all-to-all(bf16[128,2,32,128]{3,2,1,0:T(8,128)(2,1)S(1)} %choose.1), channel_id=1, replica_groups=mesh['frame'=128] {'frame'}, dimensions={0} | all-to-all | bytes 4194304 | tf_op jit(solution)/shard_map/all_to_all | solution.py:553
  70.6 16.8 %attend.1 = (bf16[384,1280]{1,0:T(8,128)(2,1)}, bf16[128,32,128]{2,1,0:T(8,128)(2,1)S(1)}) custom-call(bf16[128,2,32,128]{3,2,1,0:T(8,128)(2,1)S(1)} %all_to_all.20.slab_ref, bf16[384,1280]{1,0:T(8,128)(2,1)} %get-tuple-element.7.after_ref.q_hbm, f32[5,256,384]{2,1,0:T(8,128)} %get-tuple-element.8.mixed_hbm, f32[5,8,384]{2,1,0:T(8,128)} %get-tuple-element.9.stat_hbm, ...), custom_call_target="tpu_custom_call" | custom-call | flops 8053063680 | bytes 19660800 | tf_op jit(solution)/shard_map/attend/pallas_call | solution.py:422
  87.4 23.3 %all_to_all.21.slab_ref = bf16[128,32,128]{2,1,0:T(8,128)(2,1)S(1)} all-to-all(bf16[128,32,128]{2,1,0:T(8,128)(2,1)S(1)} %get-tuple-element.11), channel_id=1, replica_groups=mesh['frame'=128] {'frame'}, dimensions={0} | all-to-all | bytes 2097152 | tf_op jit(solution)/shard_map/all_to_all | solution.py:553
  110.7 10.8 %time_attend.1 = bf16[128,32,128]{2,1,0:T(8,128)(2,1)S(1)} custom-call(bf16[128,32,128]{2,1,0:T(8,128)(2,1)S(1)} %all_to_all.21.slab_ref, f32[1280]{0:T(1024)} %gain_ref.5, bf16[1280,3840]{1,0:T(8,128)(2,1)} %weight_hbm.5), custom_call_target="tpu_custom_call" | custom-call | flops 4278190080 | bytes 11796480 | tf_op jit(solution)/shard_map/time_attend/pallas_call | solution.py:498
  121.5 23.6 %all_to_all.22.slab_ref = bf16[128,32,128]{2,1,0:T(8,128)(2,1)S(1)} all-to-all(bf16[128,32,128]{2,1,0:T(8,128)(2,1)S(1)} %time_attend.1), channel_id=1, replica_groups=mesh['frame'=128] {'frame'}, dimensions={0} | all-to-all | bytes 2097152 | tf_op jit(solution)/shard_map/all_to_all | solution.py:553
  145.1 1.3 unpack.1
Async XLA Ops:
  3.8 30.6 %all-to-all-start = ((bf16[128,32,128]{2,1,0:T(8,128)(2,1)}), bf16[128,32,128]{2,1,0:T(8,128)(2,1)S(1)}, u32[]{:S(2)}, u32[]{:S(2)}) async-start(bf16[128,32,128]{2,1,0:T(8,128)(2,1)} %prep.1), calls=%async_computation | async-start | bytes 2097152 | tf_op jit(solution)/shard_map/all_to_all | solution.py:553

commit v7 on v6

--- a/solution.py
+++ b/solution.py
@@ -100,44 +100,25 @@
             ]
 
 
-def prep_kernel(pairs_ref, video_ref, gain_ref, slab_hbm, normed_ref, slab_ref, sems):
-    swap = swap_matrix()
+def prep_kernel(pairs_ref, video_ref, gain_ref, slab_ref, normed_ref):
     gain = gain_ref[...].reshape(1, WIDTH)
+    for k in range(PARTS):
+        rows = pl.ds(k * FRAMES, FRAMES)
+        normed_ref[rows, :] = norm_rows(video_ref[rows, :].astype(f32), gain)
     spare = [
         jnp.full((16, LANES), pairs_ref[0, which], jnp.int32).astype(f32).astype(bf16)
         for which in range(2)
     ]
-    leaving = []
-
-    def give(half):
-        rows_to_slab(tiles_of(normed_ref), slab_ref, swap, spare, halves=(half,))
-        some = pl.ds(16 * half, 16)
-        leaving.append(
-            pltpu.make_async_copy(slab_ref.at[:, some], slab_hbm.at[:, some], sems.at[half])
-        )
-        leaving[-1].start()
-
-    for k in range(PARTS):
-        rows = pl.ds(k * FRAMES, FRAMES)
-        normed_ref[rows, :] = norm_rows(video_ref[rows, :].astype(f32), gain)
-        if k == 1:
-            give(0)
-    give(1)
-    for copy in leaving:
-        copy.wait()
+    rows_to_slab(tiles_of(normed_ref), slab_ref, swap_matrix(), spare)
 
 
 def prep(pairs, video, gain):
     return pl.pallas_call(
         prep_kernel,
-        out_shape=pltpu.HBM((FRAMES, SLAB, LANES), bf16),
+        out_shape=pltpu.VMEM((FRAMES, SLAB, LANES), bf16),
         in_specs=[SMALL, WHOLE, WHOLE],
-        out_specs=THERE,
-        scratch_shapes=[
-            pltpu.VMEM((TOK, WIDTH), bf16),
-            pltpu.VMEM((FRAMES, SLAB, LANES), bf16),
-            pltpu.SemaphoreType.DMA((2,)),
-        ],
+        out_specs=WHOLE,
+        scratch_shapes=[pltpu.VMEM((TOK, WIDTH), bf16)],
         compiler_params=params(VMEM),
         cost_estimate=cost(6 * TOK * WIDTH, 4 * TOK * WIDTH),
         name="prep",
@@ -208,8 +189,9 @@
 
 
 def own_kernel(
-    video_ref, gain_ref, weight_hbm, q_ref, mixed_ref, stat_ref, rows_ref, weight_ref, sems
+    video_ref, gain_ref, weight_hbm, after_ref, q_ref, mixed_ref, stat_ref, rows_ref, weight_ref, sems
 ):
+    del after_ref
     for group in range(GROUPS):
         for copy in group_copies(weight_hbm, weight_ref, sems, group):
             copy.start()
@@ -243,7 +225,7 @@
             stat_ref[group, 4 + head : 5 + head, :] = out[HEAD : HEAD + 1]
 
 
-def own_attend(video, gain, weight):
+def own_attend(video, gain, weight, after):
     return pl.pallas_call(
         own_kernel,
         out_shape=(
@@ -251,7 +233,7 @@
             pltpu.HBM((GROUPS, GROUP, TOK), f32),
             pltpu.HBM((GROUPS, 8, TOK), f32),
         ),
-        in_specs=[WHOLE, WHOLE, THERE],
+        in_specs=[WHOLE, WHOLE, THERE, THERE],
         out_specs=(WHOLE, WHOLE, WHOLE),
         scratch_shapes=[
             pltpu.VMEM((TOK, WIDTH), bf16),
@@ -265,11 +247,11 @@
             HEADS * TOK * TOK,
         ),
         name="own_attend",
-    )(in_hbm(video), in_hbm(gain), in_hbm(weight))
-
-
-def choose_kernel(key_list_ref, slab_ref, after_ref, out_ref):
-    del after_ref
+    )(in_hbm(video), in_hbm(gain), in_hbm(weight), in_hbm(after))
+
+
+def choose_kernel(key_list_ref, slab_ref, out_hbm, out_ref, sems):
+    copies = []
     halves = [
         jnp.concatenate([slab_ref[key_list_ref[s], at : at + 16, :] for s in range(KEYS)], axis=0)
         for at in (0, 16)
@@ -289,18 +271,30 @@
         chosen = chosen.astype(bf16).reshape(8, 2, 16, 2 * LANES)
         out_ref[f : f + 8, :, 0:16, :] = chosen[..., :LANES]
         out_ref[f : f + 8, :, 16:32, :] = chosen[..., LANES:]
-
-
-def choose(key_list, slab, after):
+        if (f + 8) % 32 == 0:
+            some = pl.ds(f - 24, 32)
+            copies.append(
+                pltpu.make_async_copy(out_ref.at[some], out_hbm.at[some], sems.at[len(copies)])
+            )
+            copies[-1].start()
+    for copy in copies:
+        copy.wait()
+
+
+def choose(key_list, slab):
     return pl.pallas_call(
         choose_kernel,
-        out_shape=pltpu.VMEM((FRAMES, 2, SLAB, LANES), bf16),
-        in_specs=[SMALL, WHOLE, THERE],
-        out_specs=WHOLE,
+        out_shape=pltpu.HBM((FRAMES, 2, SLAB, LANES), bf16),
+        in_specs=[SMALL, WHOLE],
+        out_specs=THERE,
+        scratch_shapes=[
+            pltpu.VMEM((FRAMES, 2, SLAB, LANES), bf16),
+            pltpu.SemaphoreType.DMA((4,)),
+        ],
         compiler_params=params(VMEM),
         cost_estimate=cost(4 * FRAMES * SLAB * LANES * 256, 6 * FRAMES * SLAB * LANES),
         name="choose",
-    )(key_list, in_vmem(slab), in_hbm(after))
+    )(key_list, in_vmem(slab))
 
 
 LARGE = 1e30
@@ -554,9 +548,9 @@
 
 
 def body(video, key_list, pairs, norm_gain, qkv_weight, out_weight, time_gain, time_weight):
-    spread = exchange(prep(pairs, video, norm_gain))
-    queries, mixed, stat = own_attend(video, norm_gain, qkv_weight)
-    wanted = exchange(choose(key_list, spread, queries))
+    chosen = choose(key_list, exchange(prep(pairs, video, norm_gain)))
+    wanted = exchange(chosen)
+    queries, mixed, stat = own_attend(video, norm_gain, qkv_weight, chosen)
     spatial, slab = attend(wanted, queries, mixed, stat, qkv_weight, out_weight, video)
     slab = time_attend(exchange(slab), time_gain, time_weight)
     return spatial, unpack(exchange(slab))

time: 147 us -> 147 us (level)
  waiting for transfers between devices: 6.66 us -> 18.1 us
  starting transfers between devices: 11.5 us -> 4.69 us
  blocking collectives: 81.7 us -> 77.2 us
    all_to_all x1, waiting for transfers between devices: 6.66 us -> 18.1 us  [exchange(): lax.all_to_all(slab, 'frame', split_axis=0, concat_axis=0, tiled=True)]
    all_to_all x1, starting transfers between devices: 11.5 us -> 4.69 us  [exchange(): lax.all_to_all(slab, 'frame', split_axis=0, concat_axis=0, tiled=True)]
    all_to_all x3, blocking collectives: 81.7 us -> 77.2 us  [exchange(): lax.all_to_all(slab, 'frame', split_axis=0, concat_axis=0, tiled=True)]
where the time goes in v7:
time: 147 us
  blocking collectives  77.2 us (53%)
  Pallas kernels  45.7 us (31%)
  waiting for transfers between devices  18.1 us (12%)
  starting transfers between devices  4.69 us (3%)
    all_to_all x3, blocking collectives, exchange(): lax.all_to_all(slab, 'frame', split_axis=0, concat_axis=0, tiled=True)  77.2 us
    all_to_all x1, waiting for transfers between devices, exchange(): lax.all_to_all(slab, 'frame', split_axis=0, concat_axis=0, tiled=True)  18.1 us
    pallas_call x1, Pallas kernels, attend(): pl.pallas_call(attend_kernel, out_shape=(jax.ShapeDtypeStruct((TOK, WIDTH...  16.8 us
    pallas_call x1, Pallas kernels, own_attend(): pl.pallas_call(own_kernel, out_shape=(pltpu.HBM((TOK, WIDTH), bf16), pltp...  12.4 us
    pallas_call x1, Pallas kernels, time_attend(): pl.pallas_call(time_kernel, out_shape=pltpu.VMEM((FRAMES, SLAB, LANES), b...  10.8 us
    all_to_all x1, starting transfers between devices, exchange(): lax.all_to_all(slab, 'frame', split_axis=0, concat_axis=0, tiled=True)  4.69 us
  transfers between devices with their start and end apart: 1, of which 1 were waited for; matrix products, arithmetic and copies ran while one was open for 0% of the time, Pallas kernels for 8%

profile of v7, /device:TPU:1, one launch (start us, length us, event | category | flops | bytes accessed | tf_op | source)
XLA Modules:
  0.0 146.6 jit_solution(12913011899180296199)
XLA Ops:
  0.6 0.0 copy-start
  0.6 2.3 %prep.1 = bf16[128,32,128]{2,1,0:T(8,128)(2,1)S(1)} custom-call(s32[1,2]{1,0:T(1,128)} %pairs_ref.1, bf16[384,1280]{1,0:T(8,128)(2,1)} %video_hbm.1, f32[1280]{0:T(1024)} %gain_ref.4), custom_call_target="tpu_custom_call" | custom-call | flops 2949120 | bytes 1966080 | tf_op jit(solution)/shard_map/prep/pallas_call | solution.py:116
  2.9 30.4 %all_to_all.20.slab_ref = bf16[128,32,128]{2,1,0:T(8,128)(2,1)S(1)} all-to-all(bf16[128,32,128]{2,1,0:T(8,128)(2,1)S(1)} %prep.1), channel_id=1, replica_groups=mesh['frame'=128] {'frame'}, dimensions={0} | all-to-all | bytes 2097152 | tf_op jit(solution)/shard_map/all_to_all | solution.py:547
  33.3 0.0 copy-done
  33.3 2.2 %choose.1.after_ref = bf16[128,2,32,128]{3,2,1,0:T(8,128)(2,1)} custom-call(s32[8]{0:T(128)S(1)} %copy-done, bf16[128,32,128]{2,1,0:T(8,128)(2,1)S(1)} %all_to_all.20.slab_ref), custom_call_target="tpu_custom_call" | custom-call | flops 536870912 | bytes 3145728 | tf_op jit(solution)/shard_map/choose/pallas_call | solution.py:285
  35.5 4.7 %all-to-all-start.1 = ((bf16[128,2,32,128]{3,2,1,0:T(8,128)(2,1)}), bf16[128,2,32,128]{3,2,1,0:T(8,128)(2,1)S(1)}, u32[]{:S(2)}, u32[]{:S(2)}) async-start(bf16[128,2,32,128]{3,2,1,0:T(8,128)(2,1)} %choose.1.after_ref), calls=%async_computation.1 | async-start | bytes 4194304 | tf_op jit(solution)/shard_map/all_to_all | solution.py:547
  40.2 12.4 %own_attend.1 = (bf16[384,1280]{1,0:T(8,128)(2,1)}, f32[5,256,384]{2,1,0:T(8,128)}, f32[5,8,384]{2,1,0:T(8,128)}) custom-call(bf16[384,1280]{1,0:T(8,128)(2,1)} %video_hbm.1, f32[1280]{0:T(1024)} %gain_ref.4, bf16[1280,3840]{1,0:T(8,128)(2,1)} %weight_hbm.4, bf16[128,2,32,128]{3,2,1,0:T(8,128)(2,1)} %choose.1.after_ref), custom_call_target="tpu_custom_call" | custom-call | flops 5284823040 | bytes 14745600 | tf_op jit(solution)/shard_map/own_attend/pallas_call | solution.py:229
  52.6 18.1 %all-to-all-done.1.slab_ref = bf16[128,2,32,128]{3,2,1,0:T(8,128)(2,1)S(1)} async-done(((bf16[128,2,32,128]{3,2,1,0:T(8,128)(2,1)}), bf16[128,2,32,128]{3,2,1,0:T(8,128)(2,1)S(1)}, u32[]{:S(2)}, u32[]{:S(2)}) %all-to-all-start.1) | async-done | bytes 2097184 | tf_op jit(solution)/shard_map/all_to_all | solution.py:547
  70.7 16.8 %attend.1 = (bf16[384,1280]{1,0:T(8,128)(2,1)}, bf16[128,32,128]{2,1,0:T(8,128)(2,1)S(1)}) custom-call(bf16[128,2,32,128]{3,2,1,0:T(8,128)(2,1)S(1)} %all-to-all-done.1.slab_ref, bf16[384,1280]{1,0:T(8,128)(2,1)} %get-tuple-element.7.q_hbm, f32[5,256,384]{2,1,0:T(8,128)} %get-tuple-element.8.mixed_hbm, f32[5,8,384]{2,1,0:T(8,128)} %get-tuple-element.9.stat_hbm, ...), custom_call_target="tpu_custom_call" | custom-call | flops 8053063680 | bytes 19660800 | tf_op jit(solution)/shard_map/attend/pallas_call | solution.py:416
  87.5 23.3 %all_to_all.21.slab_ref = bf16[128,32,128]{2,1,0:T(8,128)(2,1)S(1)} all-to-all(bf16[128,32,128]{2,1,0:T(8,128)(2,1)S(1)} %get-tuple-element.11), channel_id=1, replica_groups=mesh['frame'=128] {'frame'}, dimensions={0} | all-to-all | bytes 2097152 | tf_op jit(solution)/shard_map/all_to_all | solution.py:547
  110.8 10.8 %time_attend.1 = bf16[128,32,128]{2,1,0:T(8,128)(2,1)S(1)} custom-call(bf16[128,32,128]{2,1,0:T(8,128)(2,1)S(1)} %all_to_all.21.slab_ref, f32[1280]{0:T(1024)} %gain_ref.5, bf16[1280,3840]{1,0:T(8,128)(2,1)} %weight_hbm.5), custom_call_target="tpu_custom_call" | custom-call | flops 4278190080 | bytes 11796480 | tf_op jit(solution)/shard_map/time_attend/pallas_call | solution.py:492
  121.6 23.6 %all_to_all.22.slab_ref = bf16[128,32,128]{2,1,0:T(8,128)(2,1)S(1)} all-to-all(bf16[128,32,128]{2,1,0:T(8,128)(2,1)S(1)} %time_attend.1), channel_id=1, replica_groups=mesh['frame'=128] {'frame'}, dimensions={0} | all-to-all | bytes 2097152 | tf_op jit(solution)/shard_map/all_to_all | solution.py:547
  145.1 1.3 unpack.1
Async XLA Ops:
  0.6 32.7 %copy-start = (s32[8]{0:T(128)S(1)}, s32[8]{0:T(128)}, u32[]{:S(2)}) copy-start(s32[8]{0:T(128)} %key_list_ref.1) | copy-start | bytes 100
  35.5 35.2 %all-to-all-start.1 = ((bf16[128,2,32,128]{3,2,1,0:T(8,128)(2,1)}), bf16[128,2,32,128]{3,2,1,0:T(8,128)(2,1)S(1)}, u32[]{:S(2)}, u32[]{:S(2)}) async-start(bf16[128,2,32,128]{3,2,1,0:T(8,128)(2,1)} %choose.1.after_ref), calls=%async_computation.1 | async-start | bytes 4194304 | tf_op jit(solution)/shard_map/all_to_all | solution.py:547

commit v8 on v6

--- a/solution.py
+++ b/solution.py
@@ -200,7 +200,7 @@
     return [
         pltpu.make_async_copy(
             weight_hbm.at[:, group_lanes(group, GROUP, which * WIDTH)],
-            weight_ref.at[which, group],
+            weight_ref.at[group, :, pl.ds(which * GROUP, GROUP)],
             sems.at[which, group],
         )
         for which in range(3)
@@ -223,10 +223,8 @@
         for copy in group_copies(weight_hbm, weight_ref, sems, group):
             copy.wait()
         rows = rows_ref[...]
-        queries, keys, values = [
-            jnp.dot(rows, weight_ref[which, group], preferred_element_type=f32)
-            for which in range(3)
-        ]
+        made = jnp.dot(rows, weight_ref[group], preferred_element_type=f32)
+        queries, keys, values = [made[:, w * GROUP : (w + 1) * GROUP] for w in range(3)]
         queries, keys, values = (queries * SCALE).astype(bf16), keys.astype(bf16), values.astype(bf16).T
         q_ref[:, group_lanes(group, GROUP)] = queries
         scores = []
@@ -255,7 +253,7 @@
         out_specs=(WHOLE, WHOLE, WHOLE),
         scratch_shapes=[
             pltpu.VMEM((TOK, WIDTH), bf16),
-            pltpu.VMEM((3, GROUPS, WIDTH, GROUP), bf16),
+            pltpu.VMEM((GROUPS, WIDTH, 3 * GROUP), bf16),
             pltpu.SemaphoreType.DMA((3, GROUPS)),
         ],
         compiler_params=params(VMEM),
@@ -310,12 +308,12 @@
     slab_ref, q_hbm, mixed_hbm, stat_hbm, weight_hbm, wo_hbm, video_hbm,
     spatial_hbm, out_slab_ref,
     spatial_ref, rows_ref, heads_ref, most_ref, q_ref, mixed_ref, stat_ref,
-    wk_ref, wv_ref, wo_ref, video_ref, sems, last_sems, out_sems,
+    wkv_ref, wo_ref, video_ref, sems, last_sems, out_sems,
 ):
     def copies(group):
         pairs = (
-            (weight_hbm.at[:, group_lanes(group, GROUP, WIDTH)], wk_ref),
-            (weight_hbm.at[:, group_lanes(group, GROUP, 2 * WIDTH)], wv_ref),
+            (weight_hbm.at[:, group_lanes(group, GROUP, WIDTH)], wkv_ref.at[:, :, pl.ds(0, GROUP)]),
+            (weight_hbm.at[:, group_lanes(group, GROUP, 2 * WIDTH)], wkv_ref.at[:, :, pl.ds(GROUP, GROUP)]),
             (q_hbm.at[:, group_lanes(group, GROUP)], q_ref),
             (mixed_hbm.at[group], mixed_ref),
             (stat_hbm.at[group], stat_ref),
@@ -347,9 +345,8 @@
 
     def project_group(group):
         rows = rows_ref[...]
-        keys = jnp.dot(rows, wk_ref[group], preferred_element_type=f32).astype(bf16)
-        values = jnp.dot(rows, wv_ref[group], preferred_element_type=f32).astype(bf16)
-        return keys, values.T
+        both = jnp.dot(rows, wkv_ref[group], preferred_element_type=f32).astype(bf16)
+        return both[:, :GROUP], both[:, GROUP:].T
 
     def score_group(group, keys):
         scores = []
@@ -435,8 +432,7 @@
             pltpu.VMEM((GROUPS, TOK, GROUP), bf16),
             pltpu.VMEM((GROUPS, GROUP, TOK), f32),
             pltpu.VMEM((GROUPS, 8, TOK), f32),
-            pltpu.VMEM((GROUPS, WIDTH, GROUP), bf16),
-            pltpu.VMEM((GROUPS, WIDTH, GROUP), bf16),
+            pltpu.VMEM((GROUPS, WIDTH, 2 * GROUP), bf16),
             pltpu.VMEM((WIDTH, WIDTH), bf16),
             pltpu.VMEM((TOK, WIDTH), bf16),
             pltpu.SemaphoreType.DMA((5, GROUPS)),
@@ -476,10 +472,8 @@
         for copy in group_copies(weight_hbm, weight_ref, sems, group):
             copy.wait()
         rows = rows_ref[...]
-        made = [
-            jnp.dot(rows, weight_ref[which, group], preferred_element_type=f32)
-            for which in range(3)
-        ]
+        made = jnp.dot(rows, weight_ref[group], preferred_element_type=f32)
+        made = [made[:, w * GROUP : (w + 1) * GROUP] for w in range(3)]
         queries, keys, values = (made[0] * SCALE).astype(bf16), made[1].astype(bf16), made[2]
         units, places = [], []
         for pair in range(2):
@@ -503,7 +497,7 @@
         scratch_shapes=[
             pltpu.VMEM((TOK, WIDTH), bf16),
             pltpu.VMEM((COLS, TOK, LANES), bf16),
-            pltpu.VMEM((3, GROUPS, WIDTH, GROUP), bf16),
+            pltpu.VMEM((GROUPS, WIDTH, 3 * GROUP), bf16),
             pltpu.SemaphoreType.DMA((3, GROUPS)),
         ],
         compiler_params=params(VMEM),

time: 147 us -> 147 us (level)
  no operation moved by 1% of the time
where the time goes in v8:
time: 147 us; the launch traced here: 146 us
  blocking collectives  81.7 us (56%)
  Pallas kernels  45.7 us (31%)
  starting transfers between devices  11.5 us (8%)
  waiting for transfers between devices  6.65 us (5%)
    all_to_all x3, blocking collectives, exchange(): lax.all_to_all(slab, 'frame', split_axis=0, concat_axis=0, tiled=True)  81.7 us
    pallas_call x1, Pallas kernels, attend(): pl.pallas_call(attend_kernel, out_shape=(jax.ShapeDtypeStruct((TOK, WIDTH...  16.7 us
    pallas_call x1, Pallas kernels, own_attend(): pl.pallas_call(own_kernel, out_shape=(pltpu.HBM((TOK, WIDTH), bf16), pltp...  12.4 us
    all_to_all x1, starting transfers between devices, exchange(): lax.all_to_all(slab, 'frame', split_axis=0, concat_axis=0, tiled=True)  11.5 us
    pallas_call x1, Pallas kernels, time_attend(): pl.pallas_call(time_kernel, out_shape=pltpu.VMEM((FRAMES, SLAB, LANES), b...  10.8 us
    all_to_all x1, waiting for transfers between devices, exchange(): lax.all_to_all(slab, 'frame', split_axis=0, concat_axis=0, tiled=True)  6.65 us
    pallas_call x1, Pallas kernels, prep(): pl.pallas_call(prep_kernel, out_shape=pltpu.HBM((FRAMES, SLAB, LANES), bf...  3.12 us
  transfers between devices with their start and end apart: 1, of which 1 were waited for; matrix products, arithmetic and copies ran while one was open for 0% of the time, Pallas kernels for 8%

profile of v8, /device:TPU:1, one launch (start us, length us, event | category | flops | bytes accessed | tf_op | source)
XLA Modules:
  0.0 146.4 jit_solution(3709804883200038206)
XLA Ops:
  0.6 3.1 %prep.1 = bf16[128,32,128]{2,1,0:T(8,128)(2,1)} custom-call(s32[1,2]{1,0:T(1,128)} %pairs_ref.1, bf16[384,1280]{1,0:T(8,128)(2,1)} %video_hbm.1, f32[1280]{0:T(1024)} %gain_ref.4), custom_call_target="tpu_custom_call" | custom-call | flops 2949120 | bytes 1966080 | tf_op jit(solution)/shard_map/prep/pallas_call | solution.py:131
  3.8 11.5 %all-to-all-start = ((bf16[128,32,128]{2,1,0:T(8,128)(2,1)}), bf16[128,32,128]{2,1,0:T(8,128)(2,1)S(1)}, u32[]{:S(2)}, u32[]{:S(2)}) async-start(bf16[128,32,128]{2,1,0:T(8,128)(2,1)} %prep.1), calls=%async_computation | async-start | bytes 2097152 | tf_op jit(solution)/shard_map/all_to_all | solution.py:547
  15.3 12.4 %own_attend.1 = (bf16[384,1280]{1,0:T(8,128)(2,1)}, f32[5,256,384]{2,1,0:T(8,128)}, f32[5,8,384]{2,1,0:T(8,128)}) custom-call(bf16[384,1280]{1,0:T(8,128)(2,1)} %video_hbm.1, f32[1280]{0:T(1024)} %gain_ref.4, bf16[1280,3840]{1,0:T(8,128)(2,1)} %weight_hbm.4), custom_call_target="tpu_custom_call" | custom-call | flops 5284823040 | bytes 14745600 | tf_op jit(solution)/shard_map/own_attend/pallas_call | solution.py:245
  27.7 6.7 %all-to-all-done.slab_ref = bf16[128,32,128]{2,1,0:T(8,128)(2,1)S(1)} async-done(((bf16[128,32,128]{2,1,0:T(8,128)(2,1)}), bf16[128,32,128]{2,1,0:T(8,128)(2,1)S(1)}, u32[]{:S(2)}, u32[]{:S(2)}) %all-to-all-start) | async-done | bytes 1048608 | tf_op jit(solution)/shard_map/all_to_all | solution.py:547
  34.3 1.4 choose.1
  35.7 34.9 %all_to_all.20.slab_ref = bf16[128,2,32,128]{3,2,1,0:T(8,128)(2,1)S(1)} all-to-all(bf16[128,2,32,128]{3,2,1,0:T(8,128)(2,1)S(1)} %choose.1), channel_id=1, replica_groups=mesh['frame'=128] {'frame'}, dimensions={0} | all-to-all | bytes 4194304 | tf_op jit(solution)/shard_map/all_to_all | solution.py:547
  70.6 16.7 %attend.1 = (bf16[384,1280]{1,0:T(8,128)(2,1)}, bf16[128,32,128]{2,1,0:T(8,128)(2,1)S(1)}) custom-call(bf16[128,2,32,128]{3,2,1,0:T(8,128)(2,1)S(1)} %all_to_all.20.slab_ref, bf16[384,1280]{1,0:T(8,128)(2,1)} %get-tuple-element.7.after_ref.q_hbm, f32[5,256,384]{2,1,0:T(8,128)} %get-tuple-element.8.mixed_hbm, f32[5,8,384]{2,1,0:T(8,128)} %get-tuple-element.9.stat_hbm, ...), custom_call_target="tpu_custom_call" | custom-call | flops 8053063680 | bytes 19660800 | tf_op jit(solution)/shard_map/attend/pallas_call | solution.py:419
  87.3 23.3 %all_to_all.21.slab_ref = bf16[128,32,128]{2,1,0:T(8,128)(2,1)S(1)} all-to-all(bf16[128,32,128]{2,1,0:T(8,128)(2,1)S(1)} %get-tuple-element.11), channel_id=1, replica_groups=mesh['frame'=128] {'frame'}, dimensions={0} | all-to-all | bytes 2097152 | tf_op jit(solution)/shard_map/all_to_all | solution.py:547
  110.6 10.8 %time_attend.1 = bf16[128,32,128]{2,1,0:T(8,128)(2,1)S(1)} custom-call(bf16[128,32,128]{2,1,0:T(8,128)(2,1)S(1)} %all_to_all.21.slab_ref, f32[1280]{0:T(1024)} %gain_ref.5, bf16[1280,3840]{1,0:T(8,128)(2,1)} %weight_hbm.5), custom_call_target="tpu_custom_call" | custom-call | flops 4278190080 | bytes 11796480 | tf_op jit(solution)/shard_map/time_attend/pallas_call | solution.py:492
  121.4 23.6 %all_to_all.22.slab_ref = bf16[128,32,128]{2,1,0:T(8,128)(2,1)S(1)} all-to-all(bf16[128,32,128]{2,1,0:T(8,128)(2,1)S(1)} %time_attend.1), channel_id=1, replica_groups=mesh['frame'=128] {'frame'}, dimensions={0} | all-to-all | bytes 2097152 | tf_op jit(solution)/shard_map/all_to_all | solution.py:547
  145.0 1.3 unpack.1
Async XLA Ops:
  3.8 30.6 %all-to-all-start = ((bf16[128,32,128]{2,1,0:T(8,128)(2,1)}), bf16[128,32,128]{2,1,0:T(8,128)(2,1)S(1)}, u32[]{:S(2)}, u32[]{:S(2)}) async-start(bf16[128,32,128]{2,1,0:T(8,128)(2,1)} %prep.1), calls=%async_computation | async-start | bytes 2097152 | tf_op jit(solution)/shard_map/all_to_all | solution.py:547

commit v9 on v6

--- a/solution.py
+++ b/solution.py
@@ -212,7 +212,7 @@
 ):
     for group in range(GROUPS):
         for copy in group_copies(weight_hbm, weight_ref, sems, group):
-            copy.start()
+            copy.start(priority=0 if group == 0 else 1)
     gain = gain_ref[...].reshape(1, WIDTH)
     for k in range(PARTS):
         rows = pl.ds(k * FRAMES, FRAMES)
@@ -331,9 +331,9 @@
     )
     for group in range(GROUPS):
         for copy in copies(group):
-            copy.start()
+            copy.start(priority=0 if group == 0 else 1)
     for copy in last:
-        copy.start()
+        copy.start(priority=1)
 
     swap = swap_matrix()
     for which in range(2):
@@ -461,7 +461,7 @@
 ):
     for group in range(GROUPS):
         for copy in group_copies(weight_hbm, weight_ref, sems, group):
-            copy.start()
+            copy.start(priority=0 if group == 0 else 1)
     swap = swap_matrix()
     slab_to_rows(
         lambda block, half: slab_ref[16 * block : 16 * block + 16, 16 * half : 16 * half + 16, :],

time: 147 us -> 147 us (level)
  no operation moved by 1% of the time
where the time goes in v9:
time: 147 us; the launch traced here: 146 us
  blocking collectives  81.7 us (56%)
  Pallas kernels  45.8 us (31%)
  starting transfers between devices  11.5 us (8%)
  waiting for transfers between devices  6.66 us (5%)
    all_to_all x3, blocking collectives, exchange(): lax.all_to_all(slab, 'frame', split_axis=0, concat_axis=0, tiled=True)  81.7 us
    pallas_call x1, Pallas kernels, attend(): pl.pallas_call(attend_kernel, out_shape=(jax.ShapeDtypeStruct((TOK, WIDTH...  16.8 us
    pallas_call x1, Pallas kernels, own_attend(): pl.pallas_call(own_kernel, out_shape=(pltpu.HBM((TOK, WIDTH), bf16), pltp...  12.4 us
    all_to_all x1, starting transfers between devices, exchange(): lax.all_to_all(slab, 'frame', split_axis=0, concat_axis=0, tiled=True)  11.5 us
    pallas_call x1, Pallas kernels, time_attend(): pl.pallas_call(time_kernel, out_shape=pltpu.VMEM((FRAMES, SLAB, LANES), b...  10.8 us
    all_to_all x1, waiting for transfers between devices, exchange(): lax.all_to_all(slab, 'frame', split_axis=0, concat_axis=0, tiled=True)  6.66 us
    pallas_call x1, Pallas kernels, prep(): pl.pallas_call(prep_kernel, out_shape=pltpu.HBM((FRAMES, SLAB, LANES), bf...  3.12 us
  transfers between devices with their start and end apart: 1, of which 1 were waited for; matrix products, arithmetic and copies ran while one was open for 0% of the time, Pallas kernels for 8%

profile of v9, /device:TPU:1, one launch (start us, length us, event | category | flops | bytes accessed | tf_op | source)
XLA Modules:
  0.0 146.5 jit_solution(16429754085283336702)
XLA Ops:
  0.6 3.1 %prep.1 = bf16[128,32,128]{2,1,0:T(8,128)(2,1)} custom-call(s32[1,2]{1,0:T(1,128)} %pairs_ref.1, bf16[384,1280]{1,0:T(8,128)(2,1)} %video_hbm.1, f32[1280]{0:T(1024)} %gain_ref.4), custom_call_target="tpu_custom_call" | custom-call | flops 2949120 | bytes 1966080 | tf_op jit(solution)/shard_map/prep/pallas_call | solution.py:131
  3.8 11.5 %all-to-all-start = ((bf16[128,32,128]{2,1,0:T(8,128)(2,1)}), bf16[128,32,128]{2,1,0:T(8,128)(2,1)S(1)}, u32[]{:S(2)}, u32[]{:S(2)}) async-start(bf16[128,32,128]{2,1,0:T(8,128)(2,1)} %prep.1), calls=%async_computation | async-start | bytes 2097152 | tf_op jit(solution)/shard_map/all_to_all | solution.py:553
  15.3 12.4 %own_attend.1 = (bf16[384,1280]{1,0:T(8,128)(2,1)}, f32[5,256,384]{2,1,0:T(8,128)}, f32[5,8,384]{2,1,0:T(8,128)}) custom-call(bf16[384,1280]{1,0:T(8,128)(2,1)} %video_hbm.1, f32[1280]{0:T(1024)} %gain_ref.4, bf16[1280,3840]{1,0:T(8,128)(2,1)} %weight_hbm.4), custom_call_target="tpu_custom_call" | custom-call | flops 5284823040 | bytes 14745600 | tf_op jit(solution)/shard_map/own_attend/pallas_call | solution.py:247
  27.7 6.7 %all-to-all-done.slab_ref = bf16[128,32,128]{2,1,0:T(8,128)(2,1)S(1)} async-done(((bf16[128,32,128]{2,1,0:T(8,128)(2,1)}), bf16[128,32,128]{2,1,0:T(8,128)(2,1)S(1)}, u32[]{:S(2)}, u32[]{:S(2)}) %all-to-all-start) | async-done | bytes 1048608 | tf_op jit(solution)/shard_map/all_to_all | solution.py:553
  34.3 1.4 choose.1
  35.7 34.9 %all_to_all.20.slab_ref = bf16[128,2,32,128]{3,2,1,0:T(8,128)(2,1)S(1)} all-to-all(bf16[128,2,32,128]{3,2,1,0:T(8,128)(2,1)S(1)} %choose.1), channel_id=1, replica_groups=mesh['frame'=128] {'frame'}, dimensions={0} | all-to-all | bytes 4194304 | tf_op jit(solution)/shard_map/all_to_all | solution.py:553
  70.6 16.8 %attend.1 = (bf16[384,1280]{1,0:T(8,128)(2,1)}, bf16[128,32,128]{2,1,0:T(8,128)(2,1)S(1)}) custom-call(bf16[128,2,32,128]{3,2,1,0:T(8,128)(2,1)S(1)} %all_to_all.20.slab_ref, bf16[384,1280]{1,0:T(8,128)(2,1)} %get-tuple-element.7.after_ref.q_hbm, f32[5,256,384]{2,1,0:T(8,128)} %get-tuple-element.8.mixed_hbm, f32[5,8,384]{2,1,0:T(8,128)} %get-tuple-element.9.stat_hbm, ...), custom_call_target="tpu_custom_call" | custom-call | flops 8053063680 | bytes 19660800 | tf_op jit(solution)/shard_map/attend/pallas_call | solution.py:422
  87.4 23.3 %all_to_all.21.slab_ref = bf16[128,32,128]{2,1,0:T(8,128)(2,1)S(1)} all-to-all(bf16[128,32,128]{2,1,0:T(8,128)(2,1)S(1)} %get-tuple-element.11), channel_id=1, replica_groups=mesh['frame'=128] {'frame'}, dimensions={0} | all-to-all | bytes 2097152 | tf_op jit(solution)/shard_map/all_to_all | solution.py:553
  110.7 10.8 %time_attend.1 = bf16[128,32,128]{2,1,0:T(8,128)(2,1)S(1)} custom-call(bf16[128,32,128]{2,1,0:T(8,128)(2,1)S(1)} %all_to_all.21.slab_ref, f32[1280]{0:T(1024)} %gain_ref.5, bf16[1280,3840]{1,0:T(8,128)(2,1)} %weight_hbm.5), custom_call_target="tpu_custom_call" | custom-call | flops 4278190080 | bytes 11796480 | tf_op jit(solution)/shard_map/time_attend/pallas_call | solution.py:498
  121.5 23.6 %all_to_all.22.slab_ref = bf16[128,32,128]{2,1,0:T(8,128)(2,1)S(1)} all-to-all(bf16[128,32,128]{2,1,0:T(8,128)(2,1)S(1)} %time_attend.1), channel_id=1, replica_groups=mesh['frame'=128] {'frame'}, dimensions={0} | all-to-all | bytes 2097152 | tf_op jit(solution)/shard_map/all_to_all | solution.py:553
  145.1 1.3 unpack.1
Async XLA Ops:
  3.8 30.6 %all-to-all-start = ((bf16[128,32,128]{2,1,0:T(8,128)(2,1)}), bf16[128,32,128]{2,1,0:T(8,128)(2,1)S(1)}, u32[]{:S(2)}, u32[]{:S(2)}) async-start(bf16[128,32,128]{2,1,0:T(8,128)(2,1)} %prep.1), calls=%async_computation | async-start | bytes 2097152 | tf_op jit(solution)/shard_map/all_to_all | solution.py:553
